TPU v7x, 128 devices: a whole 4x4x4 slice. The times are simulated.
128 devices in a mesh: row: 8 (over y_lo, x), col: 16 (over z, y_hi, core).
Axes of the slice: x: 4, y: 4 (y_hi: 2, y_lo: 2; y = y_hi * 2 + y_lo), z: 4, core: 2. Of those that a mesh axis runs over, the one named last changes fastest.
Arguments:
- tokens: bfloat16 [128, 512, 256], P('row', 'col'), may hold values from -6 to 6
- target: bfloat16 [128, 512, 256], P('row', 'col'), may hold values from -6 to 6
- block_qkv: bfloat16 [256, 768], replicated, may hold values from -0.375 to 0.375
- block_out: bfloat16 [256, 256], replicated, may hold values from -0.375 to 0.375
- grid_qkv: bfloat16 [256, 768], replicated, may hold values from -0.375 to 0.375
- grid_out: bfloat16 [256, 256], replicated, may hold values from -0.375 to 0.375
- mlp_in: bfloat16 [256, 1024], replicated, may hold values from -0.375 to 0.375
- mlp_out: bfloat16 [1024, 256], replicated, may hold values from -0.1875 to 0.1875
- probe_block_qkv: int32 [9, 768], replicated, may hold values from 0 to 1073741823
- probe_block_out: int32 [9, 256], replicated, may hold values from 0 to 1073741823
- probe_grid_qkv: int32 [9, 768], replicated, may hold values from 0 to 1073741823
- probe_grid_out: int32 [9, 256], replicated, may hold values from 0 to 1073741823
- probe_mlp_in: int32 [9, 1024], replicated, may hold values from 0 to 1073741823
- probe_mlp_out: int32 [35, 256], replicated, may hold values from 0 to 1073741823
Outputs:
- hv_block_qkv: float32 [256, 768], replicated
- hv_block_out: float32 [256, 256], replicated
- hv_grid_qkv: float32 [256, 768], replicated
- hv_grid_out: float32 [256, 256], replicated
- hv_mlp_in: float32 [256, 1024], replicated
- hv_mlp_out: float32 [1024, 256], replicated
- trace_terms: float32 [6], replicated
All inputs are finite; a program needn't handle non-finite values.
Results may differ from a plain program's by a relative error of at most 0.035.
Values may be sent and summed in bfloat16 or wider, within the bound.
No kernel may reach another device: no remote copies, remote signals or barrier semaphores. Data moves between devices by JAX's collectives and lax.ppermute only.
A program may use at most 128 MiB of HBM per device.

v0:
```python
import functools
import math

import jax
import jax.numpy as jnp
from jax import lax
from jax.experimental import pallas as pl
from jax.experimental.pallas import tpu as pltpu
from jax.sharding import Mesh, PartitionSpec as P

F32 = jnp.float32
BF16 = jnp.bfloat16
HD = 32
WINDOW = 64
GROUP = 128
EPSILON = 1e-05
SCALE = HD ** (-0.5)
GELU_K = math.sqrt(2.0 / math.pi)
GELU_C = 0.044715
PEERS = ("y_lo", "x", "z", "y_hi")


def nn(a, b):
    return lax.dot_general(a, b, (((1,), (0,)), ((), ())), preferred_element_type=F32)


def nt(a, b):
    return lax.dot_general(a, b, (((1,), (1,)), ((), ())), preferred_element_type=F32)


def tn(a, b):
    return lax.dot_general(a, b, (((0,), (0,)), ((), ())), preferred_element_type=F32)


def lanes(*parts):
    return jnp.concatenate(parts, axis=1)


def rows(*parts):
    return jnp.concatenate(parts, axis=0)


def mean(values):
    return jnp.mean(values, axis=-1, keepdims=True)


def norm_pair(x, xd):
    center = x - mean(x)
    inverse = lax.rsqrt(mean(center * center) + EPSILON)
    h = center * inverse
    cd = xd - mean(xd)
    along = mean(h * cd)
    return h, inverse * (cd - h * along), inverse, -inverse * along


def norm_back_pair(h, hd, inverse, slope, dy, dyd):
    second = mean(dy * h)
    dx = inverse * (dy - mean(dy) - h * second)
    second_dot = mean(dyd * h + dy * hd)
    dxd = slope * dx + inverse * (dyd - mean(dyd) - hd * second - h * second_dot)
    return dx, dxd


def unpack_signs(words_ref, out_ref):
    total, width = out_ref.shape
    for start in range(0, total, 16):
        row = start + lax.broadcasted_iota(jnp.int32, (16, 1), 0)
        first = start // 30
        edge = 30 * (first + 1)
        word = jnp.broadcast_to(words_ref[first : first + 1, :], (16, width))
        shift = row - 30 * first
        if edge < start + 16:
            later = jnp.broadcast_to(words_ref[first + 1 : first + 2, :], (16, width))
            word = jnp.where(row < edge, word, later)
            shift = jnp.where(row < edge, shift, row - edge)
        bit = jnp.right_shift(word, jnp.broadcast_to(shift, (16, width))) & 1
        out_ref[start : start + 16, :] = (1 - 2 * bit).astype(F32).astype(BF16)


def fill_masks(ones_ref, mask_ref):
    head_row = lax.broadcasted_iota(jnp.int32, (256, 256), 0) // WINDOW
    head_col = lax.broadcasted_iota(jnp.int32, (256, 256), 1) // WINDOW
    ones_ref[...] = (head_row == head_col).astype(F32).astype(BF16)
    head_row = lax.broadcasted_iota(jnp.int32, (256, GROUP), 0) // WINDOW
    head_col = lax.broadcasted_iota(jnp.int32, (256, GROUP), 1) // HD
    mask_ref[...] = (head_row == head_col).astype(F32).astype(BF16)


def spread(values, mask):
    return rows(values, values, values, values) * mask


def collect(values):
    lane = lax.broadcasted_iota(jnp.int32, (WINDOW, GROUP), 1)
    parts = [values[WINDOW * i : WINDOW * (i + 1), :] for i in range(4)]
    low = jnp.where(lane < HD, parts[0], parts[1])
    high = jnp.where(lane < 3 * HD, parts[2], parts[3])
    return jnp.where(lane < 2 * HD, low, high)


def attend(qkv_ref, qkvd_ref, a_ref, ad_ref, o_ref, od_ref, ones_ref, mask_ref):
    windows = qkv_ref.shape[0] // WINDOW

    def step(w, carry):
        at = pl.ds(pl.multiple_of(w * WINDOW, WINDOW), WINDOW)
        ones = ones_ref[...]
        mask = mask_ref[...]
        for g in range(2):
            qs, ks, vs = (pl.ds(256 * i + GROUP * g, GROUP) for i in range(3))
            q, qd = qkv_ref[at, qs], qkvd_ref[at, qs]
            kb, kdb = spread(qkv_ref[at, ks], mask), spread(qkvd_ref[at, ks], mask)
            vb, vdb = spread(qkv_ref[at, vs], mask), spread(qkvd_ref[at, vs], mask)
            raised = jnp.exp(nt(q, kb) * SCALE)
            scores_dot = nt(lanes(qd, q), lanes(kb, kdb)) * SCALE
            weights = raised / nn(raised.astype(BF16), ones)
            moved = weights * scores_dot
            weights_dot = moved - weights * nn(moved.astype(BF16), ones)
            a, ad = weights.astype(BF16), weights_dot.astype(BF16)
            spot = pl.ds(256 * g, 256)
            a_ref[at, spot] = a
            ad_ref[at, spot] = ad
            here = pl.ds(GROUP * g, GROUP)
            o_ref[at, here] = nn(a, vb).astype(BF16)
            od_ref[at, here] = nn(lanes(ad, a), rows(vb, vdb)).astype(BF16)
        return carry

    lax.fori_loop(0, windows, step, 0)


def attend_back(
    qkv_ref, qkvd_ref, a_ref, ad_ref, do_ref, dod_ref, dqkv_ref, dqkvd_ref, ones_ref, mask_ref
):
    windows = qkv_ref.shape[0] // WINDOW

    def step(w, carry):
        at = pl.ds(pl.multiple_of(w * WINDOW, WINDOW), WINDOW)
        ones = ones_ref[...]
        mask = mask_ref[...]
        for g in range(2):
            qs, ks, vs = (pl.ds(256 * i + GROUP * g, GROUP) for i in range(3))
            q, qd = qkv_ref[at, qs], qkvd_ref[at, qs]
            kb, kdb = spread(qkv_ref[at, ks], mask), spread(qkvd_ref[at, ks], mask)
            vb, vdb = spread(qkv_ref[at, vs], mask), spread(qkvd_ref[at, vs], mask)
            here = pl.ds(GROUP * g, GROUP)
            do, dod = do_ref[at, here], dod_ref[at, here]
            spot = pl.ds(256 * g, 256)
            ab, adb = a_ref[at, spot], ad_ref[at, spot]
            a, ad = ab.astype(F32), adb.astype(F32)
            da = nt(do, vb)
            dad = nt(lanes(dod, do), lanes(vb, vdb))
            rest = da - nn((a * da).astype(BF16), ones)
            rest_dot = dad - nn((ad * da + a * dad).astype(BF16), ones)
            ds = (a * rest * SCALE).astype(BF16)
            dsd = ((ad * rest + a * rest_dot) * SCALE).astype(BF16)
            dqkvd_ref[at, qs] = nn(lanes(dsd, ds), rows(kb, kdb)).astype(BF16)
            dqkvd_ref[at, ks] = collect(tn(rows(dsd, ds), rows(q, qd))).astype(BF16)
            dqkvd_ref[at, vs] = collect(tn(rows(adb, ab), rows(do, dod))).astype(BF16)
            if dqkv_ref is not None:
                dqkv_ref[at, qs] = nn(ds, kb).astype(BF16)
                dqkv_ref[at, ks] = collect(tn(ds, q)).astype(BF16)
                dqkv_ref[at, vs] = collect(tn(ab, do)).astype(BF16)
        return carry

    lax.fori_loop(0, windows, step, 0)


def block_forward_kernel(
    tok_ref, tgt_ref, wq_ref, wo_ref, pq_ref, po_ref,
    pack_ref, h_ref, qkv_ref, qkvd_ref, a_ref, ad_ref, o_ref, od_ref, so_ref,
    sq_ref, x_ref, ones_ref, mask_ref,
):
    fill_masks(ones_ref, mask_ref)
    unpack_signs(pq_ref, sq_ref)
    unpack_signs(po_ref, so_ref)
    for half in range(2):
        at = pl.ds(256 * half, 256)
        slab = tok_ref[8 * half : 8 * half + 8].astype(F32)
        x = rows(*[slab[:, 8 * i : 8 * i + 8, :].reshape(WINDOW, 256) for i in range(4)])
        x_ref[at, :] = x
        center = x - mean(x)
        h = (center * lax.rsqrt(mean(center * center) + EPSILON)).astype(BF16)
        h_ref[at, :] = h
        qkv_ref[at, :] = nn(h, wq_ref[...]).astype(BF16)
        qkvd_ref[at, :] = nn(h, sq_ref[...]).astype(BF16)
    attend(qkv_ref, qkvd_ref, a_ref, ad_ref, o_ref, od_ref, ones_ref, mask_ref)
    for half in range(2):
        at = pl.ds(256 * half, 256)
        out = pl.ds(32 * half, 32)
        o, od = o_ref[at, :], od_ref[at, :]
        x = x_ref[at, :] + nn(o, wo_ref[...])
        xd = nn(lanes(od, o), rows(wo_ref[...], so_ref[...]))
        both = jnp.concatenate([x.reshape(32, 8, 256), xd.reshape(32, 8, 256)], axis=1)
        pack_ref[out, :, 0:256] = both.astype(BF16)
        slab = tgt_ref[8 * half : 8 * half + 8].astype(F32)
        t = jnp.concatenate([slab[:, 8 * i : 8 * i + 8, :] for i in range(4)], axis=0)
        both = jnp.concatenate([t[:, :, 0:128], t[:, :, 128:256]], axis=1)
        pack_ref[out, :, 256:384] = both.astype(BF16)


def middle_kernel(
    factor,
    core_ref, pack_ref, wq_ref, wo_ref, wi_ref, wf_ref, pq_ref, po_ref, pi_ref, pf_ref,
    back_ref, keep_ref, send_ref,
    sq_ref, so_ref, si_ref, sf_ref, ones_ref, mask_ref, mix_ref, mixd_ref, mixt_ref,
    x_ref, xd_ref, t_ref, h1_ref, h2_ref, qkv_ref, qkvd_ref, a_ref, ad_ref, o_ref,
    ud_ref, dz_ref, dx_ref, dxd_ref, dg_ref, do_ref, dod_ref, dqkv_ref, hv_ref,
):
    tokens = x_ref.shape[0]
    fill_masks(ones_ref, mask_ref)
    unpack_signs(pq_ref, sq_ref)
    unpack_signs(po_ref, so_ref)
    unpack_signs(pi_ref, si_ref)
    unpack_signs(pf_ref, sf_ref)
    arrived = pack_ref[:, :, 0:256].astype(F32)
    for c in range(2):
        mix_ref[c] = arrived[:, 0:8, 128 * c : 128 * c + 128].reshape(tokens, 128)
        mixd_ref[c] = arrived[:, 8:16, 128 * c : 128 * c + 128].reshape(tokens, 128)
    arrived = pack_ref[:, :, 256:384].astype(F32) * factor
    for c in range(2):
        mixt_ref[c] = arrived[:, 8 * c : 8 * c + 8, :].reshape(tokens, 128)
    for w in range(8):
        at = pl.ds(WINDOW * w, WINDOW)
        for c in range(2):
            cols = pl.ds(128 * c, 128)
            x_ref[at, cols] = mix_ref[c, pl.ds(w, WINDOW, stride=8), :]
            xd_ref[at, cols] = mixd_ref[c, pl.ds(w, WINDOW, stride=8), :]
            t_ref[at, cols] = mixt_ref[c, pl.ds(w, WINDOW, stride=8), :].astype(BF16)

    def first(i, carry):
        at = pl.ds(pl.multiple_of(i * 256, 256), 256)
        low = pl.ds(pl.multiple_of(i * 256 + tokens, 256), 256)
        h, hd, _, _ = norm_pair(x_ref[at, :], xd_ref[at, :])
        h, hd = h.astype(BF16), hd.astype(BF16)
        h1_ref[at, :] = hd
        h1_ref[low, :] = h
        qkv_ref[at, :] = nn(h, wq_ref[...]).astype(BF16)
        qkvd_ref[at, :] = nn(lanes(hd, h), rows(wq_ref[...], sq_ref[...])).astype(BF16)
        return carry

    lax.fori_loop(0, tokens // 256, first, 0)
    o_part, od_part = o_ref.at[pl.ds(tokens, tokens), :], o_ref.at[pl.ds(0, tokens), :]
    attend(qkv_ref, qkvd_ref, a_ref, ad_ref, o_part, od_part, ones_ref, mask_ref)

    def second(i, carry):
        at = pl.ds(pl.multiple_of(i * 256, 256), 256)
        low = pl.ds(pl.multiple_of(i * 256 + tokens, 256), 256)
        od, o = o_ref[at, :], o_ref[low, :]
        g = nn(o, wo_ref[...]).astype(BF16).astype(F32)
        gd = nn(lanes(od, o), rows(wo_ref[...], so_ref[...])).astype(BF16).astype(F32)
        h, hd, inverse, slope = norm_pair(x_ref[at, :] + g, xd_ref[at, :] + gd)
        hb, hdb = h.astype(BF16), hd.astype(BF16)
        h2_ref[at, :] = hdb
        h2_ref[low, :] = hb
        t = t_ref[at, :]
        dh = jnp.zeros((256, 256), F32)
        dhd = jnp.zeros((256, 256), F32)
        for c in range(4):
            cols = pl.ds(256 * c, 256)
            wi, si = wi_ref[:, cols], si_ref[:, cols]
            z = nn(hb, wi)
            zd = nn(lanes(hdb, hb), rows(wi, si))
            du = nt(t, wf_ref[cols, :])
            dud = nt(t, sf_ref[cols, :])
            square = z * z
            bend = jnp.tanh(z * (GELU_K + GELU_K * GELU_C * square))
            inner = GELU_K + (3.0 * GELU_K * GELU_C) * square
            flat = (1.0 - bend * bend) * inner
            half = 0.5 * z
            slope1 = 0.5 + 0.5 * bend + half * flat
            slope2 = flat * (1.0 - z * bend * inner) + (1.0 - bend * bend) * (
                3.0 * GELU_K * GELU_C
            ) * square
            ud_ref[at, cols] = (slope1 * zd).astype(BF16)
            dz = (du * slope1).astype(BF16)
            dzd = (dud * slope1 + du * slope2 * zd).astype(BF16)
            dz_ref[at, cols] = dz
            dz_ref[low, cols] = dzd
            dh = dh + nt(dz, wi)
            dhd = dhd + nt(lanes(dzd, dz), lanes(wi, si))
        dx, dxd = norm_back_pair(h, hd, inverse, slope, dh, dhd)
        dx = dx + t.astype(F32)
        dx_ref[at, :] = dx
        dxd_ref[at, :] = dxd
        dg, dgd = dx.astype(BF16), dxd.astype(BF16)
        dg_ref[at, :] = dg
        dg_ref[low, :] = dgd
        do_ref[at, :] = nt(dg, wo_ref[...]).astype(BF16)
        dod_ref[at, :] = nt(lanes(dgd, dg), lanes(wo_ref[...], so_ref[...])).astype(BF16)
        return carry

    lax.fori_loop(0, tokens // 256, second, 0)
    dqkv, dqkvd = dqkv_ref.at[pl.ds(0, tokens), :], dqkv_ref.at[pl.ds(tokens, tokens), :]
    attend_back(
        qkv_ref, qkvd_ref, a_ref, ad_ref, do_ref, dod_ref, dqkv, dqkvd, ones_ref, mask_ref
    )

    for i in range(tokens // 256):
        at = pl.ds(i * 256, 256)
        low = pl.ds(i * 256 + tokens, 256)
        dqkv, dqkvd = dqkv_ref[at, :], dqkv_ref[low, :]
        dh = nt(dqkv, wq_ref[...])
        dhd = nt(lanes(dqkvd, dqkv), lanes(wq_ref[...], sq_ref[...]))
        h, hd, inverse, slope = norm_pair(x_ref[at, :], xd_ref[at, :])
        dx, dxd = norm_back_pair(h, hd, inverse, slope, dh, dhd)
        dx_ref[at, :] += dx
        dxd_ref[at, :] += dxd
    for w in range(8):
        at = pl.ds(WINDOW * w, WINDOW)
        for c in range(2):
            cols = pl.ds(128 * c, 128)
            mix_ref[c, pl.ds(w, WINDOW, stride=8), :] = dx_ref[at, cols]
            mixd_ref[c, pl.ds(w, WINDOW, stride=8), :] = dxd_ref[at, cols]
    for c in range(2):
        dx = mix_ref[c].reshape(tokens // 8, 8, 128)
        dxd = mixd_ref[c].reshape(tokens // 8, 8, 128)
        both = jnp.concatenate([dx, dxd], axis=1)
        back_ref[:, :, 128 * c : 128 * c + 128] = both.astype(BF16)

    def put(block, value):
        hv_ref[block] = value.astype(BF16)

    h1 = h1_ref[...]
    for c in range(3):
        put(c, tn(h1, dqkv_ref[:, 256 * c : 256 * c + 256]))
    put(3, tn(o_ref[...], dg_ref[...]))
    h2 = h2_ref[...]
    for c in range(4):
        put(4 + c, tn(h2, dz_ref[:, 256 * c : 256 * c + 256]))
    t = t_ref[...]
    for c in range(4):
        put(8 + c, tn(ud_ref[:, 256 * c : 256 * c + 256], t))
    split_halves(core_ref, hv_ref, keep_ref, send_ref)


def split_halves(core_ref, hv_ref, keep_ref, send_ref):
    core = core_ref[0]
    mine = pl.ds(pl.multiple_of(core * 128, 128), 128)
    other = pl.ds(pl.multiple_of((1 - core) * 128, 128), 128)
    for block in range(hv_ref.shape[0]):
        keep_ref[128 * block : 128 * block + 128, :] = hv_ref[block, mine, :]
        send_ref[128 * block : 128 * block + 128, :] = hv_ref[block, other, :]


def block_back_kernel(
    core_ref, back_ref, h_ref, qkv_ref, qkvd_ref, a_ref, ad_ref, o_ref, od_ref, wo_ref, so_ref,
    keep_ref, send_ref,
    ones_ref, mask_ref, do_ref, dod_ref, dqkvd_ref, hv_ref,
):
    tokens = h_ref.shape[0]
    fill_masks(ones_ref, mask_ref)
    arrived = back_ref[...].astype(F32)
    dx = arrived[:, 0:8, :].reshape(tokens, 256).astype(BF16)
    dxd = arrived[:, 8:16, :].reshape(tokens, 256).astype(BF16)
    do_ref[...] = nt(dx, wo_ref[...]).astype(BF16)
    dod_ref[...] = nt(lanes(dxd, dx), lanes(wo_ref[...], so_ref[...])).astype(BF16)
    hv_ref[3] = tn(rows(od_ref[...], o_ref[...]), rows(dx, dxd)).astype(BF16)
    attend_back(
        qkv_ref, qkvd_ref, a_ref, ad_ref, do_ref, dod_ref, None, dqkvd_ref, ones_ref, mask_ref
    )
    h = h_ref[...]
    for c in range(3):
        hv_ref[c] = tn(h, dqkvd_ref[:, 256 * c : 256 * c + 256]).astype(BF16)
    split_halves(core_ref, hv_ref, keep_ref, send_ref)


def pair_sum_kernel(mid_keep_ref, mid_got_ref, keep_ref, got_ref, out_ref):
    count = mid_keep_ref.shape[0]
    out_ref[0:count, :] = (mid_keep_ref[...].astype(F32) + mid_got_ref[...].astype(F32)).astype(BF16)
    out_ref[count:, :] = (keep_ref[...].astype(F32) + got_ref[...].astype(F32)).astype(BF16)


def peer_sum_kernel(parts_ref, out_ref):
    total = parts_ref[0].astype(F32)
    for i in range(1, parts_ref.shape[0]):
        total = total + parts_ref[i].astype(F32)
    total = total.astype(BF16)
    for i in range(parts_ref.shape[0]):
        out_ref[i] = total


def finish_kernel(
    core_ref, mine_ref, other_ref, pbq_ref, pbo_ref, pgq_ref, pgo_ref, pmi_ref, pmo_ref,
    bq_ref, bo_ref, gq_ref, go_ref, mi_ref, mo_ref, trace_ref,
    sign_ref,
):
    core = core_ref[0]
    lane = lax.broadcasted_iota(jnp.int32, (1, 128), 1)
    traces = jnp.zeros((1, 128), F32)
    plan = (
        (bq_ref, pbq_ref, 12, 0),
        (bo_ref, pbo_ref, 15, 1),
        (gq_ref, pgq_ref, 0, 2),
        (go_ref, pgo_ref, 3, 3),
        (mi_ref, pmi_ref, 4, 4),
        (mo_ref, pmo_ref, 8, 5),
    )
    for out_ref, words_ref, base, place in plan:
        height, width = out_ref.shape
        across = width // 256
        for block in range(height * width // 65536):
            cols = pl.ds(256 * (block % across), 256)
            down = 256 * (block // across)
            for source_ref, who in ((mine_ref, core), (other_ref, 1 - core)):
                start = pl.multiple_of(down + who * 128, 128)
                value = source_ref[128 * (base + block) : 128 * (base + block) + 128, :]
                out_ref[pl.ds(start, 128), cols] = value.astype(F32)
        signs = sign_ref.at[0:height, 0:width]
        unpack_signs(words_ref, signs)
        total = jnp.sum(out_ref[...] * signs[...].astype(F32), axis=0, keepdims=True)
        total = jnp.sum(total, axis=1, keepdims=True) / math.sqrt(height * width)
        traces = jnp.where(lane == place, total, traces)
    trace_ref[...] = traces


def shaped(dtype, *shape):
    return jax.ShapeDtypeStruct(shape, dtype)


def call(kernel, outs, scratch, smem_first, operands, name, limit):
    spaces = [pltpu.SMEM if (smem_first and i == 0) else pltpu.VMEM for i in range(len(operands))]
    return pl.pallas_call(
        kernel,
        out_shape=outs,
        in_specs=[pl.BlockSpec(memory_space=space) for space in spaces],
        out_specs=[pl.BlockSpec(memory_space=pltpu.VMEM) for _ in outs],
        scratch_shapes=scratch,
        compiler_params=pltpu.CompilerParams(vmem_limit_bytes=limit * 2**20),
        name=name,
    )(*operands)


def body(
    tokens, target, block_qkv, block_out, grid_qkv, grid_out, mlp_in, mlp_out,
    probe_block_qkv, probe_block_out, probe_grid_qkv, probe_grid_out, probe_mlp_in, probe_mlp_out,
):
    count = tokens.shape[0] * tokens.shape[1]
    peers = lax.axis_size(PEERS)
    factor = 1.0 / math.sqrt(count * peers * lax.axis_size("core"))
    core = lax.axis_index("core").astype(jnp.int32).reshape(1)
    swap = [(0, 1), (1, 0)]
    masks = [pltpu.VMEM((256, 256), BF16), pltpu.VMEM((256, GROUP), BF16)]

    def exchange(values):
        return lax.all_to_all(values, PEERS, 0, 0, tiled=True)

    pack, h0, qkv, qkvd, a, ad, o, od, so = call(
        block_forward_kernel,
        [
            shaped(BF16, peers, 16, 384),
            shaped(BF16, count, 256),
            shaped(BF16, count, 768),
            shaped(BF16, count, 768),
            shaped(BF16, count, 512),
            shaped(BF16, count, 512),
            shaped(BF16, count, 256),
            shaped(BF16, count, 256),
            shaped(BF16, 256, 256),
        ],
        [pltpu.VMEM((256, 768), BF16), pltpu.VMEM((count, 256), F32)] + masks,
        False,
        (tokens, target, block_qkv, block_out, probe_block_qkv, probe_block_out),
        "block_forward",
        32,
    )
    pack = exchange(pack)
    back, mid_keep, mid_send = call(
        functools.partial(middle_kernel, factor),
        [shaped(BF16, peers, 16, 256), shaped(BF16, 1536, 256), shaped(BF16, 1536, 256)],
        [
            pltpu.VMEM((256, 768), BF16),
            pltpu.VMEM((256, 256), BF16),
            pltpu.VMEM((256, 1024), BF16),
            pltpu.VMEM((1024, 256), BF16),
        ]
        + masks
        + [pltpu.VMEM((2, count, 128), F32)] * 3
        + [pltpu.VMEM((count, 256), F32)] * 2
        + [
            pltpu.VMEM((count, 256), BF16),
            pltpu.VMEM((2 * count, 256), BF16),
            pltpu.VMEM((2 * count, 256), BF16),
            pltpu.VMEM((count, 768), BF16),
            pltpu.VMEM((count, 768), BF16),
            pltpu.VMEM((count, 512), BF16),
            pltpu.VMEM((count, 512), BF16),
            pltpu.VMEM((2 * count, 256), BF16),
            pltpu.VMEM((count, 1024), BF16),
            pltpu.VMEM((2 * count, 1024), BF16),
            pltpu.VMEM((count, 256), F32),
            pltpu.VMEM((count, 256), F32),
            pltpu.VMEM((2 * count, 256), BF16),
            pltpu.VMEM((count, 256), BF16),
            pltpu.VMEM((count, 256), BF16),
            pltpu.VMEM((2 * count, 768), BF16),
            pltpu.VMEM((12, 256, 256), BF16),
        ],
        True,
        (
            core, pack, grid_qkv, grid_out, mlp_in, mlp_out,
            probe_grid_qkv, probe_grid_out, probe_mlp_in, probe_mlp_out,
        ),
        "middle",
        48,
    )
    mid_got = lax.ppermute(mid_send, "core", swap)
    back = exchange(back)
    keep, send = call(
        block_back_kernel,
        [shaped(BF16, 512, 256), shaped(BF16, 512, 256)],
        masks
        + [
            pltpu.VMEM((count, 256), BF16),
            pltpu.VMEM((count, 256), BF16),
            pltpu.VMEM((count, 768), BF16),
            pltpu.VMEM((4, 256, 256), BF16),
        ],
        True,
        (core, back, h0, qkv, qkvd, a, ad, o, od, block_out, so),
        "block_back",
        32,
    )
    got = lax.ppermute(send, "core", swap)
    (parts,) = call(
        pair_sum_kernel,
        [shaped(BF16, 2048, 256)],
        [],
        False,
        (mid_keep, mid_got, keep, got),
        "pair_sum",
        32,
    )
    parts = exchange(parts.reshape(peers, 2048 // peers, 256))
    (copies,) = call(
        peer_sum_kernel,
        [shaped(BF16, peers, 2048 // peers, 256)],
        [],
        False,
        (parts,),
        "peer_sum",
        32,
    )
    mine = exchange(copies).reshape(2048, 256)
    other = lax.ppermute(mine, "core", swap)
    results = call(
        finish_kernel,
        [
            shaped(F32, 256, 768),
            shaped(F32, 256, 256),
            shaped(F32, 256, 768),
            shaped(F32, 256, 256),
            shaped(F32, 256, 1024),
            shaped(F32, 1024, 256),
            shaped(F32, 1, 128),
        ],
        [pltpu.VMEM((1024, 1024), BF16)],
        True,
        (
            core, mine, other, probe_block_qkv, probe_block_out, probe_grid_qkv,
            probe_grid_out, probe_mlp_in, probe_mlp_out,
        ),
        "finish",
        32,
    )
    return (*results[:6], results[6][0, :6])


def solution(mesh):
    fine = Mesh(mesh.devices.reshape(2, 4, 4, 2, 2), ("y_lo", "x", "z", "y_hi", "core"))
    placed = P(("y_lo", "x"), ("z", "y_hi", "core"), None)
    return jax.shard_map(
        body,
        mesh=fine,
        in_specs=(placed, placed) + (P(),) * 12,
        out_specs=(P(),) * 7,
        check_vma=False,
    )
```

profile of v0, /device:TPU:1, one launch (start us, length us, event | category | flops | bytes accessed | tf_op | source)
XLA Modules:
  0.0 160.9 jit_solution(4872444619070468408)
XLA Ops:
  0.6 0.0 copy-start
  0.6 0.9 copy-done
  1.5 0.0 copy-start.4
  1.5 1.0 copy-done.4
  2.5 0.0 copy-start.6
  2.5 0.9 copy-done.6
  3.5 0.0 copy-start.7
  3.5 0.9 copy-done.7
  4.4 0.0 copy-start.15
  4.4 0.8 copy-done.15
  5.2 0.0 copy-start.22
  5.2 0.7 copy-done.22
  6.0 9.8 %block_forward.1 = (bf16[64,16,384]{2,1,0:T(8,128)(2,1)}, bf16[512,256]{1,0:T(8,128)(2,1)S(1)}, bf16[512,768]{1,0:T(8,128)(2,1)S(1)}, bf16[512,768]{1,0:T(8,128)...) custom-call(bf16[16,32,256]{2,1,0:T(8,128)(2,1)S(1)} %copy-done.6, ...), custom_call_target="tpu_custom_call" | custom-call | tf_op jit(solution)/shard_map/block_forward/pallas_call | solution.py:421
  15.8 0.7 copy-done.8
  16.5 0.0 copy-start.10
  16.5 0.7 copy-done.10
  17.2 0.0 copy-start.12
  17.2 0.7 copy-done.12
  17.9 0.0 copy-start.20
  17.9 0.7 copy-done.20
  18.5 0.0 copy-start.14
  18.6 0.0 copy-start.17
  18.6 0.0 copy-start.24
  18.6 12.1 %all-to-all-start = ((bf16[64,16,384]{2,1,0:T(8,128)(2,1)}), bf16[64,16,384]{2,1,0:T(8,128)(2,1)S(1)}, u32[]{:S(2)}, u32[]{:S(2)}) async-start(bf16[64,16,384]{2,1,0:T(8,128)(2,1)} %get-tuple-element.28), calls=%async_computation | async-start | bytes 1572864 | tf_op jit(solution)/shard_map/all_to_all | solution.py:444
  30.7 14.3 %all-to-all-done.pack_ref = bf16[64,16,384]{2,1,0:T(8,128)(2,1)S(1)} async-done(((bf16[64,16,384]{2,1,0:T(8,128)(2,1)}), bf16[64,16,384]{2,1,0:T(8,128)(2,1)S(1)}, u32[]{:S(2)}, u32[]{:S(2)}) %all-to-all-start) | async-done | bytes 786464 | tf_op jit(solution)/shard_map/all_to_all | solution.py:444
  45.0 0.0 copy-done.14
  45.0 0.0 copy-done.17
  45.0 0.0 copy-done.24
  45.0 0.0 copy-start.2
  45.0 1.0 copy-done.2
  46.1 0.0 copy-start.3
  46.1 1.0 copy-done.3
  47.1 0.0 copy-start.5
  47.1 1.0 copy-done.5
  48.1 0.0 copy-start.18
  48.1 0.8 copy-done.18
  48.9 0.0 copy-start.19
  48.9 0.9 copy-done.19
  49.8 27.2 %middle.1 = (bf16[64,16,256]{2,1,0:T(8,128)(2,1)S(1)}, bf16[1536,256]{1,0:T(8,128)(2,1)S(1)}, bf16[1536,256]{1,0:T(8,128)(2,1)S(1)}) custom-call(s32[1]{0:T(128)} %bitcast.core_ref, bf16[64,16,384]{2,1,0:T(8,128)(2,1)S(1)} %all-to-all-done.pack_ref, bf16[256,768]{1,0:T(8,128)(2,1)S(1)} %copy-done.5, bf16[256,256]{1,0:T(8,128)(2,1)S(1)} %copy-done.19, ...), custom_call_target="tpu_custom_call" | custom-call | tf_op jit(solution)/shard_map/middle/pallas_call | solution.py:421
  77.0 2.6 %collective-permute-start = (bf16[1536,256]{1,0:T(8,128)(2,1)S(1)}, bf16[1536,256]{1,0:T(8,128)(2,1)S(1)}, u32[]{:S(2)}, u32[]{:S(2)}) collective-permute-start(bf16[1536,256]{1,0:T(8,128)(2,1)S(1)} %get-tuple-element.30), channel_id=1, source_target_pairs={{0,1},{1,0},{2,3},{3,2},{4,5},{5,4},{6,7},{7,6},{8,9},{9,8},{10,11... | collective-permute-start | bytes 2359304 | tf_op jit(solution)/shard_map/ppermute | solution.py:505
  79.6 0.0 copy-start.1
  79.6 0.0 copy-start.21
  79.6 16.9 %all_to_all.20.back_ref = bf16[64,16,256]{2,1,0:T(8,128)(2,1)S(1)} all-to-all(bf16[64,16,256]{2,1,0:T(8,128)(2,1)S(1)} %get-tuple-element.31), channel_id=1, replica_groups=mesh['y_lo'=2,'x'=4,'z'=4,'y_hi'=2,'core'=2] {'y_lo','x','z','y_hi'}, dimensions={0} | all-to-all | bytes 1048576 | tf_op jit(solution)/shard_map/all_to_all | solution.py:444
  96.5 0.0 copy-done.1
  96.5 0.0 copy-done.9
  96.5 0.0 copy-done.11
  96.5 0.0 copy-done.13
  96.5 0.0 copy-done.21
  96.6 8.3 %block_back.1 = (bf16[512,256]{1,0:T(8,128)(2,1)S(1)}, bf16[512,256]{1,0:T(8,128)(2,1)S(1)}) custom-call(s32[1]{0:T(128)} %bitcast.core_ref, bf16[64,16,256]{2,1,0:T(8,128)(2,1)S(1)} %all_to_all.20.back_ref, bf16[512,256]{1,0:T(8,128)(2,1)S(1)} %copy-done.9, bf16[512,768]{1,0:T(8,128)(2,1)S(1)} %get-tuple-element.33.qkv_ref, ...), custom_call_target="tpu_custom_call" | custom-call | tf_op jit(solution)/shard_map/block_back/pallas_call | solution.py:421
  104.8 1.7 %collective-permute-start.1 = (bf16[512,256]{1,0:T(8,128)(2,1)S(1)}, bf16[512,256]{1,0:T(8,128)(2,1)S(1)}, u32[]{:S(2)}, u32[]{:S(2)}) collective-permute-start(bf16[512,256]{1,0:T(8,128)(2,1)S(1)} %get-tuple-element.41), channel_id=1, source_target_pairs={{0,1},{1,0},{2,3},{3,2},{4,5},{5,4},{6,7},{7,6},{8,9},{9,8},{10,11... | collective-permute-start | bytes 786440 | tf_op jit(solution)/shard_map/ppermute | solution.py:522
  106.6 1.2 collective-permute-done.1.got_ref
  107.7 0.0 collective-permute-done.mid_got_ref
  107.7 0.2 pair_sum.1
  108.0 21.6 %all_to_all.21.parts_ref = bf16[64,32,256]{2,1,0:T(8,128)(2,1)S(1)} all-to-all(bf16[64,32,256]{2,1,0:T(8,128)(2,1)S(1)} %bitcast.5), channel_id=1, replica_groups=mesh['y_lo'=2,'x'=4,'z'=4,'y_hi'=2,'core'=2] {'y_lo','x','z','y_hi'}, dimensions={0} | all-to-all | bytes 2097152 | tf_op jit(solution)/shard_map/all_to_all | solution.py:444
  129.6 0.2 peer_sum.1
  129.9 0.0 copy-start.16
  129.9 0.0 copy-start.23
  129.9 21.9 %all_to_all.22 = bf16[64,32,256]{2,1,0:T(8,128)(2,1)S(1)} all-to-all(bf16[64,32,256]{2,1,0:T(8,128)(2,1)S(1)} %peer_sum.1), channel_id=1, replica_groups=mesh['y_lo'=2,'x'=4,'z'=4,'y_hi'=2,'core'=2] {'y_lo','x','z','y_hi'}, dimensions={0} | all-to-all | bytes 2097152 | tf_op jit(solution)/shard_map/all_to_all | solution.py:444
  151.8 3.0 %collective-permute-start.2 = (bf16[2048,256]{1,0:T(8,128)(2,1)S(1)}, bf16[2048,256]{1,0:T(8,128)(2,1)S(1)}, u32[]{:S(2)}, u32[]{:S(2)}) collective-permute-start(bf16[2048,256]{1,0:T(8,128)(2,1)S(1)} %bitcast.6), channel_id=1, source_target_pairs={{0,1},{1,0},{2,3},{3,2},{4,5},{5,4},{6,7},{7,6},{8,9},{9,8},{10,11... | collective-permute-start | bytes 3145736 | tf_op jit(solution)/shard_map/ppermute | solution.py:543
  154.9 2.3 %collective-permute-done.2.other_ref = bf16[2048,256]{1,0:T(8,128)(2,1)S(1)} collective-permute-done((bf16[2048,256]{1,0:T(8,128)(2,1)S(1)}, bf16[2048,256]{1,0:T(8,128)(2,1)S(1)}, u32[]{:S(2)}, u32[]{:S(2)}) %collective-permute-start.2) | collective-permute-done | bytes 1048608 | tf_op jit(solution)/shard_map/ppermute | solution.py:543
  157.1 0.0 copy-done.16
  157.1 0.0 copy-done.23
  157.2 3.3 %finish.1 = (f32[256,768]{1,0:T(8,128)}, f32[256,256]{1,0:T(8,128)}, f32[256,768]{1,0:T(8,128)}, f32[256,256]{1,0:T(8,128)}, f32[256,1024]{1,0:T(8,128)}, /*index=5*/f32[1024,256]{1,0:T(8,128)}, f32[1,128]{1,0:T(1,128)S(1)}) custom-call(s32[1]{0:T(128)} %bitcast.core_ref, bf16[2048,256]{1,0:T(8,128)(2,1)S(1)} %bitcast.7, ...), custom_call_target="tpu_custom_call" | custom-call | tf_op jit(solution)/shard_map/finish/pallas_call | solution.py:421
  160.4 0.5 slice_bitcast_fusion
  (4 shorter events, 0.0 us)
Async XLA Ops:
  0.6 0.9 copy-start
  1.5 1.0 copy-start.4
  2.5 0.9 copy-start.6
  3.5 0.9 copy-start.7
  4.4 0.8 copy-start.15
  5.2 0.7 copy-start.22
  15.8 0.7 copy-start.8
  16.5 0.7 copy-start.10
  17.2 0.7 copy-start.12
  17.9 0.7 copy-start.20
  18.5 26.5 %copy-start.14 = (s32[9,1024]{1,0:T(8,128)S(1)}, s32[9,1024]{1,0:T(8,128)}, u32[]{:S(2)}) copy-start(s32[9,1024]{1,0:T(8,128)} %pmi_ref.1) | copy-start | bytes 110596
  18.6 26.5 %copy-start.17 = (s32[9,768]{1,0:T(8,128)S(1)}, s32[9,768]{1,0:T(8,128)}, u32[]{:S(2)}) copy-start(s32[9,768]{1,0:T(8,128)} %pgq_ref.1) | copy-start | bytes 82948
  18.6 26.5 %copy-start.24 = (s32[9,256]{1,0:T(8,128)S(1)}, s32[9,256]{1,0:T(8,128)}, u32[]{:S(2)}) copy-start(s32[9,256]{1,0:T(8,128)} %pgo_ref.1) | copy-start | bytes 27652
  18.6 26.5 %all-to-all-start = ((bf16[64,16,384]{2,1,0:T(8,128)(2,1)}), bf16[64,16,384]{2,1,0:T(8,128)(2,1)S(1)}, u32[]{:S(2)}, u32[]{:S(2)}) async-start(bf16[64,16,384]{2,1,0:T(8,128)(2,1)} %get-tuple-element.28), calls=%async_computation | async-start | bytes 1572864 | tf_op jit(solution)/shard_map/all_to_all | solution.py:444
  45.0 1.0 copy-start.2
  46.1 1.0 copy-start.3
  47.1 1.0 copy-start.5
  48.1 0.8 copy-start.18
  48.9 0.9 copy-start.19
  77.0 30.7 %collective-permute-start = (bf16[1536,256]{1,0:T(8,128)(2,1)S(1)}, bf16[1536,256]{1,0:T(8,128)(2,1)S(1)}, u32[]{:S(2)}, u32[]{:S(2)}) collective-permute-start(bf16[1536,256]{1,0:T(8,128)(2,1)S(1)} %get-tuple-element.30), channel_id=1, source_target_pairs={{0,1},{1,0},{2,3},{3,2},{4,5},{5,4},{6,7},{7,6},{8,9},{9,8},{10,11... | collective-permute-start | bytes 2359304 | tf_op jit(solution)/shard_map/ppermute | solution.py:505
  79.6 16.9 %copy-start.1 = (bf16[256,256]{1,0:T(8,128)(2,1)S(1)}, bf16[256,256]{1,0:T(8,128)(2,1)}, u32[]{:S(2)}) copy-start(bf16[256,256]{1,0:T(8,128)(2,1)} %wo_ref.5) | copy-start | bytes 393220
  79.6 16.9 %copy-start.9 = (bf16[512,256]{1,0:T(8,128)(2,1)S(1)}, bf16[512,256]{1,0:T(8,128)(2,1)}, u32[]{:S(2)}) copy-start(bf16[512,256]{1,0:T(8,128)(2,1)} %copy-done.8) | copy-start | bytes 786436
  79.6 16.9 %copy-start.11 = (bf16[512,256]{1,0:T(8,128)(2,1)S(1)}, bf16[512,256]{1,0:T(8,128)(2,1)}, u32[]{:S(2)}) copy-start(bf16[512,256]{1,0:T(8,128)(2,1)} %copy-done.10) | copy-start | bytes 786436
  79.6 16.9 %copy-start.13 = (bf16[512,256]{1,0:T(8,128)(2,1)S(1)}, bf16[512,256]{1,0:T(8,128)(2,1)}, u32[]{:S(2)}) copy-start(bf16[512,256]{1,0:T(8,128)(2,1)} %copy-done.12) | copy-start | bytes 786436
  79.6 16.9 %copy-start.21 = (bf16[256,256]{1,0:T(8,128)(2,1)S(1)}, bf16[256,256]{1,0:T(8,128)(2,1)}, u32[]{:S(2)}) copy-start(bf16[256,256]{1,0:T(8,128)(2,1)} %copy-done.20) | copy-start | bytes 393220
  104.8 2.9 %collective-permute-start.1 = (bf16[512,256]{1,0:T(8,128)(2,1)S(1)}, bf16[512,256]{1,0:T(8,128)(2,1)S(1)}, u32[]{:S(2)}, u32[]{:S(2)}) collective-permute-start(bf16[512,256]{1,0:T(8,128)(2,1)S(1)} %get-tuple-element.41), channel_id=1, source_target_pairs={{0,1},{1,0},{2,3},{3,2},{4,5},{5,4},{6,7},{7,6},{8,9},{9,8},{10,11... | collective-permute-start | bytes 786440 | tf_op jit(solution)/shard_map/ppermute | solution.py:522
  129.9 27.3 %copy-start.16 = (s32[9,768]{1,0:T(8,128)S(1)}, s32[9,768]{1,0:T(8,128)}, u32[]{:S(2)}) copy-start(s32[9,768]{1,0:T(8,128)} %pbq_ref.1) | copy-start | bytes 82948
  129.9 27.3 %copy-start.23 = (s32[9,256]{1,0:T(8,128)S(1)}, s32[9,256]{1,0:T(8,128)}, u32[]{:S(2)}) copy-start(s32[9,256]{1,0:T(8,128)} %pbo_ref.1) | copy-start | bytes 27652
  151.8 5.3 %collective-permute-start.2 = (bf16[2048,256]{1,0:T(8,128)(2,1)S(1)}, bf16[2048,256]{1,0:T(8,128)(2,1)S(1)}, u32[]{:S(2)}, u32[]{:S(2)}) collective-permute-start(bf16[2048,256]{1,0:T(8,128)(2,1)S(1)} %bitcast.6), channel_id=1, source_target_pairs={{0,1},{1,0},{2,3},{3,2},{4,5},{5,4},{6,7},{7,6},{8,9},{9,8},{10,11... | collective-permute-start | bytes 3145736 | tf_op jit(solution)/shard_map/ppermute | solution.py:543
where the time goes:
time: 162 us; the launch traced here: 161 us
  blocking collectives  60.5 us (37%)
  Pallas kernels  49.1 us (30%)
  starting transfers between devices  19.5 us (12%)
  waiting for transfers between devices  17.8 us (11%)
  local copies, waits for them, and re-layouts  13.4 us (8%)
    all_to_all x3, blocking collectives, exchange(): return lax.all_to_all(values, PEERS, 0, 0, tiled=True)  60.5 us
    pallas_call x6, Pallas kernels, call(): pl.pallas_call(kernel, out_shape=outs, in_specs=[pl.BlockSpec(memory_spac...  49.1 us
    all_to_all x1, waiting for transfers between devices, exchange(): return lax.all_to_all(values, PEERS, 0, 0, tiled=True)  14.3 us
    unnamed x50, local copies, waits for them, and re-layouts  12.9 us
    all_to_all x1, starting transfers between devices, exchange(): return lax.all_to_all(values, PEERS, 0, 0, tiled=True)  12.1 us
  transfers between devices with their start and end apart: 4, of which 3 were waited for; matrix products, arithmetic and copies ran while one was open for 0% of the time, Pallas kernels for 5%

commit v1 on v0

--- a/solution.py
+++ b/solution.py
@@ -59,6 +59,16 @@
     second_dot = mean(dyd * h + dy * hd)
     dxd = slope * dx + inverse * (dyd - mean(dyd) - hd * second - h * second_dot)
     return dx, dxd
+
+
+def fetch(sources, buffers, sems):
+    copies = [
+        pltpu.make_async_copy(source, buffer, sems.at[i])
+        for i, (source, buffer) in enumerate(zip(sources, buffers))
+    ]
+    for copy in copies:
+        copy.start()
+    return lambda *places: [copies[place].wait() for place in places]
 
 
 def unpack_signs(words_ref, out_ref):
@@ -165,13 +175,19 @@
 
 
 def block_forward_kernel(
-    tok_ref, tgt_ref, wq_ref, wo_ref, pq_ref, po_ref,
-    pack_ref, h_ref, qkv_ref, qkvd_ref, a_ref, ad_ref, o_ref, od_ref, so_ref,
-    sq_ref, x_ref, ones_ref, mask_ref,
+    pq_hbm, tok_hbm, wq_hbm, po_hbm, wo_hbm, tgt_hbm,
+    pack_ref, h_ref, qkv_ref, qkvd_ref, a_ref, ad_ref, o_ref, od_ref, sq_ref, so_ref,
+    pq_ref, tok_ref, wq_ref, po_ref, wo_ref, tgt_ref, sems, x_ref, ones_ref, mask_ref,
 ):
+    wait = fetch(
+        (pq_hbm, tok_hbm, wq_hbm, po_hbm, wo_hbm, tgt_hbm),
+        (pq_ref, tok_ref, wq_ref, po_ref, wo_ref, tgt_ref),
+        sems,
+    )
     fill_masks(ones_ref, mask_ref)
+    wait(0)
     unpack_signs(pq_ref, sq_ref)
-    unpack_signs(po_ref, so_ref)
+    wait(1, 2)
     for half in range(2):
         at = pl.ds(256 * half, 256)
         slab = tok_ref[8 * half : 8 * half + 8].astype(F32)
@@ -183,6 +199,8 @@
         qkv_ref[at, :] = nn(h, wq_ref[...]).astype(BF16)
         qkvd_ref[at, :] = nn(h, sq_ref[...]).astype(BF16)
     attend(qkv_ref, qkvd_ref, a_ref, ad_ref, o_ref, od_ref, ones_ref, mask_ref)
+    wait(3, 4, 5)
+    unpack_signs(po_ref, so_ref)
     for half in range(2):
         at = pl.ds(256 * half, 256)
         out = pl.ds(32 * half, 32)
@@ -199,18 +217,14 @@
 
 def middle_kernel(
     factor,
-    core_ref, pack_ref, wq_ref, wo_ref, wi_ref, wf_ref, pq_ref, po_ref, pi_ref, pf_ref,
-    back_ref, keep_ref, send_ref,
-    sq_ref, so_ref, si_ref, sf_ref, ones_ref, mask_ref, mix_ref, mixd_ref, mixt_ref,
+    core_ref, pack_ref, pq_ref, wq_ref, po_ref, wo_ref, pi_ref, wi_ref, pf_ref, wf_ref,
+    back_ref, keep_ref, send_ref, sq_ref, so_ref, si_ref, sf_ref,
+    ones_ref, mask_ref, mix_ref, mixd_ref, mixt_ref,
     x_ref, xd_ref, t_ref, h1_ref, h2_ref, qkv_ref, qkvd_ref, a_ref, ad_ref, o_ref,
     ud_ref, dz_ref, dx_ref, dxd_ref, dg_ref, do_ref, dod_ref, dqkv_ref, hv_ref,
 ):
     tokens = x_ref.shape[0]
     fill_masks(ones_ref, mask_ref)
-    unpack_signs(pq_ref, sq_ref)
-    unpack_signs(po_ref, so_ref)
-    unpack_signs(pi_ref, si_ref)
-    unpack_signs(pf_ref, sf_ref)
     arrived = pack_ref[:, :, 0:256].astype(F32)
     for c in range(2):
         mix_ref[c] = arrived[:, 0:8, 128 * c : 128 * c + 128].reshape(tokens, 128)
@@ -225,6 +239,10 @@
             x_ref[at, cols] = mix_ref[c, pl.ds(w, WINDOW, stride=8), :]
             xd_ref[at, cols] = mixd_ref[c, pl.ds(w, WINDOW, stride=8), :]
             t_ref[at, cols] = mixt_ref[c, pl.ds(w, WINDOW, stride=8), :].astype(BF16)
+    unpack_signs(pq_ref, sq_ref)
+    unpack_signs(po_ref, so_ref)
+    unpack_signs(pi_ref, si_ref)
+    unpack_signs(pf_ref, sf_ref)
 
     def first(i, carry):
         at = pl.ds(pl.multiple_of(i * 256, 256), 256)
@@ -379,22 +397,21 @@
 
 
 def finish_kernel(
-    core_ref, mine_ref, other_ref, pbq_ref, pbo_ref, pgq_ref, pgo_ref, pmi_ref, pmo_ref,
+    core_ref, mine_ref, other_ref, sbq_ref, sbo_ref, sgq_ref, sgo_ref, smi_ref, smo_ref,
     bq_ref, bo_ref, gq_ref, go_ref, mi_ref, mo_ref, trace_ref,
-    sign_ref,
 ):
     core = core_ref[0]
     lane = lax.broadcasted_iota(jnp.int32, (1, 128), 1)
     traces = jnp.zeros((1, 128), F32)
     plan = (
-        (bq_ref, pbq_ref, 12, 0),
-        (bo_ref, pbo_ref, 15, 1),
-        (gq_ref, pgq_ref, 0, 2),
-        (go_ref, pgo_ref, 3, 3),
-        (mi_ref, pmi_ref, 4, 4),
-        (mo_ref, pmo_ref, 8, 5),
-    )
-    for out_ref, words_ref, base, place in plan:
+        (bq_ref, sbq_ref, 12, 0),
+        (bo_ref, sbo_ref, 15, 1),
+        (gq_ref, sgq_ref, 0, 2),
+        (go_ref, sgo_ref, 3, 3),
+        (mi_ref, smi_ref, 4, 4),
+        (mo_ref, smo_ref, 8, 5),
+    )
+    for out_ref, sign_ref, base, place in plan:
         height, width = out_ref.shape
         across = width // 256
         for block in range(height * width // 65536):
@@ -404,9 +421,7 @@
                 start = pl.multiple_of(down + who * 128, 128)
                 value = source_ref[128 * (base + block) : 128 * (base + block) + 128, :]
                 out_ref[pl.ds(start, 128), cols] = value.astype(F32)
-        signs = sign_ref.at[0:height, 0:width]
-        unpack_signs(words_ref, signs)
-        total = jnp.sum(out_ref[...] * signs[...].astype(F32), axis=0, keepdims=True)
+        total = jnp.sum(out_ref[...] * sign_ref[...].astype(F32), axis=0, keepdims=True)
         total = jnp.sum(total, axis=1, keepdims=True) / math.sqrt(height * width)
         traces = jnp.where(lane == place, total, traces)
     trace_ref[...] = traces
@@ -416,8 +431,14 @@
     return jax.ShapeDtypeStruct(shape, dtype)
 
 
-def call(kernel, outs, scratch, smem_first, operands, name, limit):
-    spaces = [pltpu.SMEM if (smem_first and i == 0) else pltpu.VMEM for i in range(len(operands))]
+def held(*arrays):
+    buffers = [pltpu.VMEM(array.shape, array.dtype) for array in arrays]
+    return buffers + [pltpu.SemaphoreType.DMA((len(arrays),))]
+
+
+def call(kernel, outs, scratch, places, operands, name, limit):
+    kinds = {"s": pltpu.SMEM, "v": pltpu.VMEM, "h": pltpu.HBM}
+    spaces = [kinds[place] for place in places]
     return pl.pallas_call(
         kernel,
         out_shape=outs,
@@ -443,7 +464,9 @@
     def exchange(values):
         return lax.all_to_all(values, PEERS, 0, 0, tiled=True)
 
-    pack, h0, qkv, qkvd, a, ad, o, od, so = call(
+    sources = (probe_block_qkv, tokens, block_qkv, probe_block_out, block_out, target)
+    sources = [pltpu.with_memory_space_constraint(source, pltpu.HBM) for source in sources]
+    pack, h0, qkv, qkvd, a, ad, o, od, sq, so = call(
         block_forward_kernel,
         [
             shaped(BF16, peers, 16, 384),
@@ -454,25 +477,25 @@
             shaped(BF16, count, 512),
             shaped(BF16, count, 256),
             shaped(BF16, count, 256),
+            shaped(BF16, 256, 768),
             shaped(BF16, 256, 256),
         ],
-        [pltpu.VMEM((256, 768), BF16), pltpu.VMEM((count, 256), F32)] + masks,
-        False,
-        (tokens, target, block_qkv, block_out, probe_block_qkv, probe_block_out),
+        held(*sources) + [pltpu.VMEM((count, 256), F32)] + masks,
+        "hhhhhh",
+        sources,
         "block_forward",
-        32,
+        16,
     )
     pack = exchange(pack)
-    back, mid_keep, mid_send = call(
+    sources = (
+        probe_grid_qkv, grid_qkv, probe_grid_out, grid_out,
+        probe_mlp_in, mlp_in, probe_mlp_out, mlp_out,
+    )
+    back, mid_keep, mid_send, sgq, sgo, smi, smo = call(
         functools.partial(middle_kernel, factor),
-        [shaped(BF16, peers, 16, 256), shaped(BF16, 1536, 256), shaped(BF16, 1536, 256)],
-        [
-            pltpu.VMEM((256, 768), BF16),
-            pltpu.VMEM((256, 256), BF16),
-            pltpu.VMEM((256, 1024), BF16),
-            pltpu.VMEM((1024, 256), BF16),
-        ]
-        + masks
+        [shaped(BF16, peers, 16, 256), shaped(BF16, 1536, 256), shaped(BF16, 1536, 256)]
+        + [shaped(BF16, *weight.shape) for weight in sources[1::2]],
+        masks
         + [pltpu.VMEM((2, count, 128), F32)] * 3
         + [pltpu.VMEM((count, 256), F32)] * 2
         + [
@@ -494,13 +517,10 @@
             pltpu.VMEM((2 * count, 768), BF16),
             pltpu.VMEM((12, 256, 256), BF16),
         ],
-        True,
-        (
-            core, pack, grid_qkv, grid_out, mlp_in, mlp_out,
-            probe_grid_qkv, probe_grid_out, probe_mlp_in, probe_mlp_out,
-        ),
+        "svvvvvvvvv",
+        (core, pack, *sources),
         "middle",
-        48,
+        28,
     )
     mid_got = lax.ppermute(mid_send, "core", swap)
     back = exchange(back)
@@ -514,30 +534,30 @@
             pltpu.VMEM((count, 768), BF16),
             pltpu.VMEM((4, 256, 256), BF16),
         ],
-        True,
+        "s" + "v" * 10,
         (core, back, h0, qkv, qkvd, a, ad, o, od, block_out, so),
         "block_back",
-        32,
+        12,
     )
     got = lax.ppermute(send, "core", swap)
     (parts,) = call(
         pair_sum_kernel,
         [shaped(BF16, 2048, 256)],
         [],
-        False,
+        "vvvv",
         (mid_keep, mid_got, keep, got),
         "pair_sum",
-        32,
+        8,
     )
     parts = exchange(parts.reshape(peers, 2048 // peers, 256))
     (copies,) = call(
         peer_sum_kernel,
         [shaped(BF16, peers, 2048 // peers, 256)],
         [],
-        False,
+        "v",
         (parts,),
         "peer_sum",
-        32,
+        8,
     )
     mine = exchange(copies).reshape(2048, 256)
     other = lax.ppermute(mine, "core", swap)
@@ -552,14 +572,11 @@
             shaped(F32, 1024, 256),
             shaped(F32, 1, 128),
         ],
-        [pltpu.VMEM((1024, 1024), BF16)],
-        True,
-        (
-            core, mine, other, probe_block_qkv, probe_block_out, probe_grid_qkv,
-            probe_grid_out, probe_mlp_in, probe_mlp_out,
-        ),
+        [],
+        "s" + "v" * 8,
+        (core, mine, other, sq, so, sgq, sgo, smi, smo),
         "finish",
-        32,
+        24,
     )
     return (*results[:6], results[6][0, :6])
 

time: 162 us -> 159 us (0.981)
  local copies, waits for them, and re-layouts: 13.4 us -> 9.78 us
    unnamed x50 -> x34, local copies, waits for them, and re-layouts: 12.9 us -> 9.27 us
where the time goes in v1:
time: 159 us; the launch traced here: 158 us
  blocking collectives  60.5 us (38%)
  Pallas kernels  49.7 us (31%)
  starting transfers between devices  19.5 us (12%)
  waiting for transfers between devices  17.8 us (11%)
  local copies, waits for them, and re-layouts  9.78 us (6%)
    all_to_all x3, blocking collectives, exchange(): return lax.all_to_all(values, PEERS, 0, 0, tiled=True)  60.5 us
    pallas_call x6, Pallas kernels, call(): pl.pallas_call(kernel, out_shape=outs, in_specs=[pl.BlockSpec(memory_spac...  49.7 us
    all_to_all x1, waiting for transfers between devices, exchange(): return lax.all_to_all(values, PEERS, 0, 0, tiled=True)  14.3 us
    all_to_all x1, starting transfers between devices, exchange(): return lax.all_to_all(values, PEERS, 0, 0, tiled=True)  12.1 us
    unnamed x34, local copies, waits for them, and re-layouts  9.27 us
  transfers between devices with their start and end apart: 4, of which 3 were waited for; matrix products, arithmetic and copies ran while one was open for 0% of the time, Pallas kernels for 5%

profile of v1, /device:TPU:1, one launch (start us, length us, event | category | flops | bytes accessed | tf_op | source)
XLA Modules:
  0.0 157.9 jit_solution(6982307562172565390)
XLA Ops:
  0.6 10.9 %block_forward.1 = (bf16[64,16,384]{2,1,0:T(8,128)(2,1)}, bf16[512,256]{1,0:T(8,128)(2,1)S(1)}, bf16[512,768]{1,0:T(8,128)(2,1)S(1)}, bf16[512,768]{1,0:T(8,128)...) custom-call(s32[9,768]{1,0:T(8,128)} %pq_hbm.1, ...), custom_call_target="tpu_custom_call" | custom-call | tf_op jit(solution)/shard_map/block_forward/pallas_call | solution.py:442
  11.5 0.0 copy-start.3
  11.5 0.7 copy-done.3
  12.3 0.0 copy-start.6
  12.3 0.7 copy-done.6
  13.0 0.0 copy-start.8
  13.0 0.7 copy-done.8
  13.7 0.0 copy-start.10
  13.7 0.7 copy-done.10
  14.4 0.0 copy-start.16
  14.4 12.1 %all-to-all-start = ((bf16[64,16,384]{2,1,0:T(8,128)(2,1)}), bf16[64,16,384]{2,1,0:T(8,128)(2,1)S(1)}, u32[]{:S(2)}, u32[]{:S(2)}) async-start(bf16[64,16,384]{2,1,0:T(8,128)(2,1)} %get-tuple-element.33), calls=%async_computation | async-start | bytes 1572864 | tf_op jit(solution)/shard_map/all_to_all | solution.py:465
  26.5 14.3 %all-to-all-done.pack_ref = bf16[64,16,384]{2,1,0:T(8,128)(2,1)S(1)} async-done(((bf16[64,16,384]{2,1,0:T(8,128)(2,1)}), bf16[64,16,384]{2,1,0:T(8,128)(2,1)S(1)}, u32[]{:S(2)}, u32[]{:S(2)}) %all-to-all-start) | async-done | bytes 786464 | tf_op jit(solution)/shard_map/all_to_all | solution.py:465
  40.8 0.0 copy-done.16
  40.8 0.0 copy-start.1
  40.8 1.0 copy-done.1
  41.9 0.0 copy-start.2
  41.9 1.0 copy-done.2
  42.9 0.0 copy-start.5
  42.9 1.0 copy-done.5
  43.9 0.0 copy-start.12
  43.9 0.9 copy-done.12
  44.8 0.0 copy-start.13
  44.8 0.8 copy-done.13
  45.6 0.0 copy-start.14
  45.6 0.8 copy-done.14
  46.4 0.0 copy-start.15
  46.4 0.8 copy-done.15
  47.2 27.4 %middle.1 = (bf16[64,16,256]{2,1,0:T(8,128)(2,1)S(1)}, bf16[1536,256]{1,0:T(8,128)(2,1)S(1)}, bf16[1536,256]{1,0:T(8,128)(2,1)S(1)}, bf16[256,768]{1,0:T(8,128)(...) custom-call(s32[1]{0:T(128)} %bitcast.core_ref, ...), custom_call_target="tpu_custom_call" | custom-call | tf_op jit(solution)/shard_map/middle/pallas_call | solution.py:442
  74.6 2.6 %collective-permute-start = (bf16[1536,256]{1,0:T(8,128)(2,1)S(1)}, bf16[1536,256]{1,0:T(8,128)(2,1)S(1)}, u32[]{:S(2)}, u32[]{:S(2)}) collective-permute-start(bf16[1536,256]{1,0:T(8,128)(2,1)S(1)} %get-tuple-element.35), channel_id=1, source_target_pairs={{0,1},{1,0},{2,3},{3,2},{4,5},{5,4},{6,7},{7,6},{8,9},{9,8},{10,11... | collective-permute-start | bytes 2359304 | tf_op jit(solution)/shard_map/ppermute | solution.py:525
  77.2 0.0 copy-start
  77.2 0.0 copy-start.7
  77.2 0.0 copy-start.9
  77.2 0.0 copy-start.11
  77.2 16.9 %all_to_all.20.back_ref = bf16[64,16,256]{2,1,0:T(8,128)(2,1)S(1)} all-to-all(bf16[64,16,256]{2,1,0:T(8,128)(2,1)S(1)} %get-tuple-element.36), channel_id=1, replica_groups=mesh['y_lo'=2,'x'=4,'z'=4,'y_hi'=2,'core'=2] {'y_lo','x','z','y_hi'}, dimensions={0} | all-to-all | bytes 1048576 | tf_op jit(solution)/shard_map/all_to_all | solution.py:465
  94.1 0.0 copy-done
  94.1 0.0 copy-done.7
  94.1 0.0 copy-done.9
  94.1 0.0 copy-done.11
  94.1 8.3 %block_back.1 = (bf16[512,256]{1,0:T(8,128)(2,1)S(1)}, bf16[512,256]{1,0:T(8,128)(2,1)S(1)}) custom-call(s32[1]{0:T(128)} %bitcast.core_ref, bf16[64,16,256]{2,1,0:T(8,128)(2,1)S(1)} %all_to_all.20.back_ref, bf16[512,256]{1,0:T(8,128)(2,1)S(1)} %copy-done.7, bf16[512,768]{1,0:T(8,128)(2,1)S(1)} %get-tuple-element.38.qkv_ref, ...), custom_call_target="tpu_custom_call" | custom-call | tf_op jit(solution)/shard_map/block_back/pallas_call | solution.py:442
  102.4 1.7 %collective-permute-start.1 = (bf16[512,256]{1,0:T(8,128)(2,1)S(1)}, bf16[512,256]{1,0:T(8,128)(2,1)S(1)}, u32[]{:S(2)}, u32[]{:S(2)}) collective-permute-start(bf16[512,256]{1,0:T(8,128)(2,1)S(1)} %get-tuple-element.46), channel_id=1, source_target_pairs={{0,1},{1,0},{2,3},{3,2},{4,5},{5,4},{6,7},{7,6},{8,9},{9,8},{10,11... | collective-permute-start | bytes 786440 | tf_op jit(solution)/shard_map/ppermute | solution.py:542
  104.1 1.2 collective-permute-done.1.got_ref
  105.3 0.0 collective-permute-done.mid_got_ref
  105.3 0.2 pair_sum.1
  105.5 21.6 %all_to_all.21.parts_ref = bf16[64,32,256]{2,1,0:T(8,128)(2,1)S(1)} all-to-all(bf16[64,32,256]{2,1,0:T(8,128)(2,1)S(1)} %bitcast.7), channel_id=1, replica_groups=mesh['y_lo'=2,'x'=4,'z'=4,'y_hi'=2,'core'=2] {'y_lo','x','z','y_hi'}, dimensions={0} | all-to-all | bytes 2097152 | tf_op jit(solution)/shard_map/all_to_all | solution.py:465
  127.2 0.2 peer_sum.1
  127.4 0.0 copy-start.4
  127.4 21.9 %all_to_all.22 = bf16[64,32,256]{2,1,0:T(8,128)(2,1)S(1)} all-to-all(bf16[64,32,256]{2,1,0:T(8,128)(2,1)S(1)} %peer_sum.1), channel_id=1, replica_groups=mesh['y_lo'=2,'x'=4,'z'=4,'y_hi'=2,'core'=2] {'y_lo','x','z','y_hi'}, dimensions={0} | all-to-all | bytes 2097152 | tf_op jit(solution)/shard_map/all_to_all | solution.py:465
  149.4 3.0 %collective-permute-start.2 = (bf16[2048,256]{1,0:T(8,128)(2,1)S(1)}, bf16[2048,256]{1,0:T(8,128)(2,1)S(1)}, u32[]{:S(2)}, u32[]{:S(2)}) collective-permute-start(bf16[2048,256]{1,0:T(8,128)(2,1)S(1)} %bitcast.5), channel_id=1, source_target_pairs={{0,1},{1,0},{2,3},{3,2},{4,5},{5,4},{6,7},{7,6},{8,9},{9,8},{10,11... | collective-permute-start | bytes 3145736 | tf_op jit(solution)/shard_map/ppermute | solution.py:563
  152.4 2.3 %collective-permute-done.2.other_ref = bf16[2048,256]{1,0:T(8,128)(2,1)S(1)} collective-permute-done((bf16[2048,256]{1,0:T(8,128)(2,1)S(1)}, bf16[2048,256]{1,0:T(8,128)(2,1)S(1)}, u32[]{:S(2)}, u32[]{:S(2)}) %collective-permute-start.2) | collective-permute-done | bytes 1048608 | tf_op jit(solution)/shard_map/ppermute | solution.py:563
  154.7 0.0 copy-done.4
  154.7 2.7 %finish.1 = (f32[256,768]{1,0:T(8,128)}, f32[256,256]{1,0:T(8,128)}, f32[256,768]{1,0:T(8,128)}, f32[256,256]{1,0:T(8,128)}, f32[256,1024]{1,0:T(8,128)}, /*index=5*/f32[1024,256]{1,0:T(8,128)}, f32[1,128]{1,0:T(1,128)S(1)}) custom-call(s32[1]{0:T(128)} %bitcast.core_ref, bf16[2048,256]{1,0:T(8,128)(2,1)S(1)} %bitcast.6, ...), custom_call_target="tpu_custom_call" | custom-call | tf_op jit(solution)/shard_map/finish/pallas_call | solution.py:442
  157.4 0.5 slice_bitcast_fusion
Async XLA Ops:
  11.5 0.7 copy-start.3
  12.3 0.7 copy-start.6
  13.0 0.7 copy-start.8
  13.7 0.7 copy-start.10
  14.4 26.5 %copy-start.16 = (s32[9,256]{1,0:T(8,128)S(1)}, s32[9,256]{1,0:T(8,128)}, u32[]{:S(2)}) copy-start(s32[9,256]{1,0:T(8,128)} %po_ref.1) | copy-start | bytes 27652
  14.4 26.5 %all-to-all-start = ((bf16[64,16,384]{2,1,0:T(8,128)(2,1)}), bf16[64,16,384]{2,1,0:T(8,128)(2,1)S(1)}, u32[]{:S(2)}, u32[]{:S(2)}) async-start(bf16[64,16,384]{2,1,0:T(8,128)(2,1)} %get-tuple-element.33), calls=%async_computation | async-start | bytes 1572864 | tf_op jit(solution)/shard_map/all_to_all | solution.py:465
  40.8 1.0 copy-start.1
  41.9 1.0 copy-start.2
  42.9 1.0 copy-start.5
  43.9 0.9 copy-start.12
  44.8 0.8 copy-start.13
  45.6 0.8 copy-start.14
  46.4 0.8 copy-start.15
  74.6 30.7 %collective-permute-start = (bf16[1536,256]{1,0:T(8,128)(2,1)S(1)}, bf16[1536,256]{1,0:T(8,128)(2,1)S(1)}, u32[]{:S(2)}, u32[]{:S(2)}) collective-permute-start(bf16[1536,256]{1,0:T(8,128)(2,1)S(1)} %get-tuple-element.35), channel_id=1, source_target_pairs={{0,1},{1,0},{2,3},{3,2},{4,5},{5,4},{6,7},{7,6},{8,9},{9,8},{10,11... | collective-permute-start | bytes 2359304 | tf_op jit(solution)/shard_map/ppermute | solution.py:525
  77.2 16.9 %copy-start = (bf16[256,256]{1,0:T(8,128)(2,1)S(1)}, bf16[256,256]{1,0:T(8,128)(2,1)}, u32[]{:S(2)}) copy-start(bf16[256,256]{1,0:T(8,128)(2,1)} %wo_ref.3) | copy-start | bytes 393220
  77.2 16.9 %copy-start.7 = (bf16[512,256]{1,0:T(8,128)(2,1)S(1)}, bf16[512,256]{1,0:T(8,128)(2,1)}, u32[]{:S(2)}) copy-start(bf16[512,256]{1,0:T(8,128)(2,1)} %copy-done.6) | copy-start | bytes 786436
  77.2 16.9 %copy-start.9 = (bf16[512,256]{1,0:T(8,128)(2,1)S(1)}, bf16[512,256]{1,0:T(8,128)(2,1)}, u32[]{:S(2)}) copy-start(bf16[512,256]{1,0:T(8,128)(2,1)} %copy-done.8) | copy-start | bytes 786436
  77.2 16.9 %copy-start.11 = (bf16[512,256]{1,0:T(8,128)(2,1)S(1)}, bf16[512,256]{1,0:T(8,128)(2,1)}, u32[]{:S(2)}) copy-start(bf16[512,256]{1,0:T(8,128)(2,1)} %copy-done.10) | copy-start | bytes 786436
  102.4 2.9 %collective-permute-start.1 = (bf16[512,256]{1,0:T(8,128)(2,1)S(1)}, bf16[512,256]{1,0:T(8,128)(2,1)S(1)}, u32[]{:S(2)}, u32[]{:S(2)}) collective-permute-start(bf16[512,256]{1,0:T(8,128)(2,1)S(1)} %get-tuple-element.46), channel_id=1, source_target_pairs={{0,1},{1,0},{2,3},{3,2},{4,5},{5,4},{6,7},{7,6},{8,9},{9,8},{10,11... | collective-permute-start | bytes 786440 | tf_op jit(solution)/shard_map/ppermute | solution.py:542
  127.4 27.3 %copy-start.4 = (bf16[256,768]{1,0:T(8,128)(2,1)S(1)}, bf16[256,768]{1,0:T(8,128)(2,1)}, u32[]{:S(2)}) copy-start(bf16[256,768]{1,0:T(8,128)(2,1)} %copy-done.3) | copy-start | bytes 1179652
  149.4 5.3 %collective-permute-start.2 = (bf16[2048,256]{1,0:T(8,128)(2,1)S(1)}, bf16[2048,256]{1,0:T(8,128)(2,1)S(1)}, u32[]{:S(2)}, u32[]{:S(2)}) collective-permute-start(bf16[2048,256]{1,0:T(8,128)(2,1)S(1)} %bitcast.5), channel_id=1, source_target_pairs={{0,1},{1,0},{2,3},{3,2},{4,5},{5,4},{6,7},{7,6},{8,9},{9,8},{10,11... | collective-permute-start | bytes 3145736 | tf_op jit(solution)/shard_map/ppermute | solution.py:563

commit v2 on v1

--- a/solution.py
+++ b/solution.py
@@ -108,60 +108,92 @@
     return jnp.where(lane < 2 * HD, low, high)
 
 
+BATCH = 8
+
+
+def per_batch(windows, step):
+    def some(i, carry):
+        step(
+            [
+                pl.ds(pl.multiple_of((i * BATCH + n) * WINDOW, WINDOW), WINDOW)
+                for n in range(BATCH)
+            ]
+        )
+        return carry
+
+    lax.fori_loop(0, windows // BATCH, some, 0)
+
+
+def heads_of(ref, at, kind, g):
+    return ref[at, pl.ds(256 * kind + GROUP * g, GROUP)]
+
+
 def attend(qkv_ref, qkvd_ref, a_ref, ad_ref, o_ref, od_ref, ones_ref, mask_ref):
-    windows = qkv_ref.shape[0] // WINDOW
-
-    def step(w, carry):
-        at = pl.ds(pl.multiple_of(w * WINDOW, WINDOW), WINDOW)
+    def step(spots):
         ones = ones_ref[...]
         mask = mask_ref[...]
-        for g in range(2):
-            qs, ks, vs = (pl.ds(256 * i + GROUP * g, GROUP) for i in range(3))
-            q, qd = qkv_ref[at, qs], qkvd_ref[at, qs]
-            kb, kdb = spread(qkv_ref[at, ks], mask), spread(qkvd_ref[at, ks], mask)
-            vb, vdb = spread(qkv_ref[at, vs], mask), spread(qkvd_ref[at, vs], mask)
-            raised = jnp.exp(nt(q, kb) * SCALE)
-            scores_dot = nt(lanes(qd, q), lanes(kb, kdb)) * SCALE
-            weights = raised / nn(raised.astype(BF16), ones)
-            moved = weights * scores_dot
-            weights_dot = moved - weights * nn(moved.astype(BF16), ones)
-            a, ad = weights.astype(BF16), weights_dot.astype(BF16)
+        units = [(at, g) for at in spots for g in range(2)]
+        raised, scores_dot = [], []
+        for at, g in units:
+            q, qd = heads_of(qkv_ref, at, 0, g), heads_of(qkvd_ref, at, 0, g)
+            kb = spread(heads_of(qkv_ref, at, 1, g), mask)
+            kdb = spread(heads_of(qkvd_ref, at, 1, g), mask)
+            raised.append(jnp.exp(nt(q, kb) * SCALE))
+            scores_dot.append(nt(lanes(qd, q), lanes(kb, kdb)) * SCALE)
+        sums = [nn(e.astype(BF16), ones) for e in raised]
+        weights = [e / total for e, total in zip(raised, sums)]
+        moved = [w * sd for w, sd in zip(weights, scores_dot)]
+        sums = [nn(m.astype(BF16), ones) for m in moved]
+        weights_dot = [m - w * total for m, w, total in zip(moved, weights, sums)]
+        for (at, g), w, wd in zip(units, weights, weights_dot):
+            a, ad = w.astype(BF16), wd.astype(BF16)
             spot = pl.ds(256 * g, 256)
             a_ref[at, spot] = a
             ad_ref[at, spot] = ad
+            vb = spread(heads_of(qkv_ref, at, 2, g), mask)
+            vdb = spread(heads_of(qkvd_ref, at, 2, g), mask)
             here = pl.ds(GROUP * g, GROUP)
             o_ref[at, here] = nn(a, vb).astype(BF16)
             od_ref[at, here] = nn(lanes(ad, a), rows(vb, vdb)).astype(BF16)
-        return carry
-
-    lax.fori_loop(0, windows, step, 0)
+
+    per_batch(qkv_ref.shape[0] // WINDOW, step)
 
 
 def attend_back(
     qkv_ref, qkvd_ref, a_ref, ad_ref, do_ref, dod_ref, dqkv_ref, dqkvd_ref, ones_ref, mask_ref
 ):
-    windows = qkv_ref.shape[0] // WINDOW
-
-    def step(w, carry):
-        at = pl.ds(pl.multiple_of(w * WINDOW, WINDOW), WINDOW)
+    def step(spots):
         ones = ones_ref[...]
         mask = mask_ref[...]
-        for g in range(2):
+        units = [(at, g) for at in spots for g in range(2)]
+        da, dad, first, second = [], [], [], []
+        for at, g in units:
+            here = pl.ds(GROUP * g, GROUP)
+            do, dod = do_ref[at, here], dod_ref[at, here]
+            vb = spread(heads_of(qkv_ref, at, 2, g), mask)
+            vdb = spread(heads_of(qkvd_ref, at, 2, g), mask)
+            da.append(nt(do, vb))
+            dad.append(nt(lanes(dod, do), lanes(vb, vdb)))
+        for (at, g), x, xd in zip(units, da, dad):
+            spot = pl.ds(256 * g, 256)
+            a, ad = a_ref[at, spot].astype(F32), ad_ref[at, spot].astype(F32)
+            first.append((a * x).astype(BF16))
+            second.append((ad * x + a * xd).astype(BF16))
+        first = [nn(x, ones) for x in first]
+        second = [nn(x, ones) for x in second]
+        for (at, g), x, xd, total, total_dot in zip(units, da, dad, first, second):
+            spot = pl.ds(256 * g, 256)
+            here = pl.ds(GROUP * g, GROUP)
             qs, ks, vs = (pl.ds(256 * i + GROUP * g, GROUP) for i in range(3))
+            ab, adb = a_ref[at, spot], ad_ref[at, spot]
+            a, ad = ab.astype(F32), adb.astype(F32)
+            rest = x - total
+            rest_dot = xd - total_dot
+            ds = (a * rest * SCALE).astype(BF16)
+            dsd = ((ad * rest + a * rest_dot) * SCALE).astype(BF16)
+            do, dod = do_ref[at, here], dod_ref[at, here]
             q, qd = qkv_ref[at, qs], qkvd_ref[at, qs]
             kb, kdb = spread(qkv_ref[at, ks], mask), spread(qkvd_ref[at, ks], mask)
-            vb, vdb = spread(qkv_ref[at, vs], mask), spread(qkvd_ref[at, vs], mask)
-            here = pl.ds(GROUP * g, GROUP)
-            do, dod = do_ref[at, here], dod_ref[at, here]
-            spot = pl.ds(256 * g, 256)
-            ab, adb = a_ref[at, spot], ad_ref[at, spot]
-            a, ad = ab.astype(F32), adb.astype(F32)
-            da = nt(do, vb)
-            dad = nt(lanes(dod, do), lanes(vb, vdb))
-            rest = da - nn((a * da).astype(BF16), ones)
-            rest_dot = dad - nn((ad * da + a * dad).astype(BF16), ones)
-            ds = (a * rest * SCALE).astype(BF16)
-            dsd = ((ad * rest + a * rest_dot) * SCALE).astype(BF16)
             dqkvd_ref[at, qs] = nn(lanes(dsd, ds), rows(kb, kdb)).astype(BF16)
             dqkvd_ref[at, ks] = collect(tn(rows(dsd, ds), rows(q, qd))).astype(BF16)
             dqkvd_ref[at, vs] = collect(tn(rows(adb, ab), rows(do, dod))).astype(BF16)
@@ -169,15 +201,15 @@
                 dqkv_ref[at, qs] = nn(ds, kb).astype(BF16)
                 dqkv_ref[at, ks] = collect(tn(ds, q)).astype(BF16)
                 dqkv_ref[at, vs] = collect(tn(ab, do)).astype(BF16)
-        return carry
-
-    lax.fori_loop(0, windows, step, 0)
+
+    per_batch(qkv_ref.shape[0] // WINDOW, step)
 
 
 def block_forward_kernel(
     pq_hbm, tok_hbm, wq_hbm, po_hbm, wo_hbm, tgt_hbm,
-    pack_ref, h_ref, qkv_ref, qkvd_ref, a_ref, ad_ref, o_ref, od_ref, sq_ref, so_ref,
-    pq_ref, tok_ref, wq_ref, po_ref, wo_ref, tgt_ref, sems, x_ref, ones_ref, mask_ref,
+    pack_ref, qkv_ref, qkvd_ref, a_ref, ad_ref, h_hbm, o_hbm, od_hbm, sq_hbm, so_hbm,
+    pq_ref, tok_ref, wq_ref, po_ref, wo_ref, tgt_ref, sems,
+    h_ref, o_ref, od_ref, sq_ref, so_ref, out_sems, x_ref, ones_ref, mask_ref,
 ):
     wait = fetch(
         (pq_hbm, tok_hbm, wq_hbm, po_hbm, wo_hbm, tgt_hbm),
@@ -201,6 +233,9 @@
     attend(qkv_ref, qkvd_ref, a_ref, ad_ref, o_ref, od_ref, ones_ref, mask_ref)
     wait(3, 4, 5)
     unpack_signs(po_ref, so_ref)
+    saved = fetch(
+        (h_ref, o_ref, od_ref, sq_ref, so_ref), (h_hbm, o_hbm, od_hbm, sq_hbm, so_hbm), out_sems
+    )
     for half in range(2):
         at = pl.ds(256 * half, 256)
         out = pl.ds(32 * half, 32)
@@ -213,17 +248,24 @@
         t = jnp.concatenate([slab[:, 8 * i : 8 * i + 8, :] for i in range(4)], axis=0)
         both = jnp.concatenate([t[:, :, 0:128], t[:, :, 128:256]], axis=1)
         pack_ref[out, :, 256:384] = both.astype(BF16)
+    saved(0, 1, 2, 3, 4)
 
 
 def middle_kernel(
     factor,
-    core_ref, pack_ref, pq_ref, wq_ref, po_ref, wo_ref, pi_ref, wi_ref, pf_ref, wf_ref,
-    back_ref, keep_ref, send_ref, sq_ref, so_ref, si_ref, sf_ref,
-    ones_ref, mask_ref, mix_ref, mixd_ref, mixt_ref,
+    core_ref, pack_ref, pq_hbm, wq_hbm, po_hbm, wo_hbm, pi_hbm, wi_hbm, pf_hbm, wf_hbm,
+    back_ref, keep_ref, send_ref, sq_hbm, so_hbm, si_hbm, sf_hbm,
+    pq_ref, wq_ref, po_ref, wo_ref, pi_ref, wi_ref, pf_ref, wf_ref, sems,
+    sq_ref, so_ref, si_ref, sf_ref, out_sems, ones_ref, mask_ref, mix_ref, mixd_ref, mixt_ref,
     x_ref, xd_ref, t_ref, h1_ref, h2_ref, qkv_ref, qkvd_ref, a_ref, ad_ref, o_ref,
     ud_ref, dz_ref, dx_ref, dxd_ref, dg_ref, do_ref, dod_ref, dqkv_ref, hv_ref,
 ):
     tokens = x_ref.shape[0]
+    wait = fetch(
+        (pq_hbm, wq_hbm, po_hbm, wo_hbm, pi_hbm, wi_hbm, pf_hbm, wf_hbm),
+        (pq_ref, wq_ref, po_ref, wo_ref, pi_ref, wi_ref, pf_ref, wf_ref),
+        sems,
+    )
     fill_masks(ones_ref, mask_ref)
     arrived = pack_ref[:, :, 0:256].astype(F32)
     for c in range(2):
@@ -239,10 +281,9 @@
             x_ref[at, cols] = mix_ref[c, pl.ds(w, WINDOW, stride=8), :]
             xd_ref[at, cols] = mixd_ref[c, pl.ds(w, WINDOW, stride=8), :]
             t_ref[at, cols] = mixt_ref[c, pl.ds(w, WINDOW, stride=8), :].astype(BF16)
+    wait(0)
     unpack_signs(pq_ref, sq_ref)
-    unpack_signs(po_ref, so_ref)
-    unpack_signs(pi_ref, si_ref)
-    unpack_signs(pf_ref, sf_ref)
+    wait(1)
 
     def first(i, carry):
         at = pl.ds(pl.multiple_of(i * 256, 256), 256)
@@ -258,6 +299,13 @@
     lax.fori_loop(0, tokens // 256, first, 0)
     o_part, od_part = o_ref.at[pl.ds(tokens, tokens), :], o_ref.at[pl.ds(0, tokens), :]
     attend(qkv_ref, qkvd_ref, a_ref, ad_ref, o_part, od_part, ones_ref, mask_ref)
+    wait(2, 3, 4, 5, 6, 7)
+    unpack_signs(po_ref, so_ref)
+    unpack_signs(pi_ref, si_ref)
+    unpack_signs(pf_ref, sf_ref)
+    saved = fetch(
+        (sq_ref, so_ref, si_ref, sf_ref), (sq_hbm, so_hbm, si_hbm, sf_hbm), out_sems
+    )
 
     def second(i, carry):
         at = pl.ds(pl.multiple_of(i * 256, 256), 256)
@@ -347,6 +395,7 @@
     t = t_ref[...]
     for c in range(4):
         put(8 + c, tn(ud_ref[:, 256 * c : 256 * c + 256], t))
+    saved(0, 1, 2, 3)
     split_halves(core_ref, hv_ref, keep_ref, send_ref)
 
 
@@ -360,17 +409,23 @@
 
 
 def block_back_kernel(
-    core_ref, back_ref, h_ref, qkv_ref, qkvd_ref, a_ref, ad_ref, o_ref, od_ref, wo_ref, so_ref,
+    core_ref, back_ref, qkv_ref, qkvd_ref, a_ref, ad_ref, wo_hbm, so_hbm, o_hbm, od_hbm, h_hbm,
     keep_ref, send_ref,
+    wo_ref, so_ref, o_ref, od_ref, h_ref, sems,
     ones_ref, mask_ref, do_ref, dod_ref, dqkvd_ref, hv_ref,
 ):
     tokens = h_ref.shape[0]
+    wait = fetch(
+        (wo_hbm, so_hbm, o_hbm, od_hbm, h_hbm), (wo_ref, so_ref, o_ref, od_ref, h_ref), sems
+    )
     fill_masks(ones_ref, mask_ref)
     arrived = back_ref[...].astype(F32)
     dx = arrived[:, 0:8, :].reshape(tokens, 256).astype(BF16)
     dxd = arrived[:, 8:16, :].reshape(tokens, 256).astype(BF16)
+    wait(0, 1)
     do_ref[...] = nt(dx, wo_ref[...]).astype(BF16)
     dod_ref[...] = nt(lanes(dxd, dx), lanes(wo_ref[...], so_ref[...])).astype(BF16)
+    wait(2, 3, 4)
     hv_ref[3] = tn(rows(od_ref[...], o_ref[...]), rows(dx, dxd)).astype(BF16)
     attend_back(
         qkv_ref, qkvd_ref, a_ref, ad_ref, do_ref, dod_ref, None, dqkvd_ref, ones_ref, mask_ref
@@ -436,66 +491,69 @@
     return buffers + [pltpu.SemaphoreType.DMA((len(arrays),))]
 
 
-def call(kernel, outs, scratch, places, operands, name, limit):
+def call(kernel, outs, spaces, scratch, operands, places, name, limit):
     kinds = {"s": pltpu.SMEM, "v": pltpu.VMEM, "h": pltpu.HBM}
-    spaces = [kinds[place] for place in places]
+    pinned = [
+        pltpu.with_memory_space_constraint(operand, pltpu.HBM) if place == "h" else operand
+        for operand, place in zip(operands, places)
+    ]
     return pl.pallas_call(
         kernel,
-        out_shape=outs,
-        in_specs=[pl.BlockSpec(memory_space=space) for space in spaces],
-        out_specs=[pl.BlockSpec(memory_space=pltpu.VMEM) for _ in outs],
+        out_shape=[
+            pltpu.HBM(out.shape, out.dtype) if space == "h" else out
+            for out, space in zip(outs, spaces)
+        ],
+        in_specs=[pl.BlockSpec(memory_space=kinds[place]) for place in places],
+        out_specs=[pl.BlockSpec(memory_space=kinds[space]) for space in spaces],
         scratch_shapes=scratch,
         compiler_params=pltpu.CompilerParams(vmem_limit_bytes=limit * 2**20),
         name=name,
-    )(*operands)
-
-
-def body(
-    tokens, target, block_qkv, block_out, grid_qkv, grid_out, mlp_in, mlp_out,
-    probe_block_qkv, probe_block_out, probe_grid_qkv, probe_grid_out, probe_mlp_in, probe_mlp_out,
-):
+    )(*pinned)
+
+
+MASKS = [pltpu.VMEM((256, 256), BF16), pltpu.VMEM((256, GROUP), BF16)]
+
+
+def stage_forward(tokens, target, weight_qkv, weight_out, words_qkv, words_out, peers):
     count = tokens.shape[0] * tokens.shape[1]
-    peers = lax.axis_size(PEERS)
-    factor = 1.0 / math.sqrt(count * peers * lax.axis_size("core"))
-    core = lax.axis_index("core").astype(jnp.int32).reshape(1)
-    swap = [(0, 1), (1, 0)]
-    masks = [pltpu.VMEM((256, 256), BF16), pltpu.VMEM((256, GROUP), BF16)]
-
-    def exchange(values):
-        return lax.all_to_all(values, PEERS, 0, 0, tiled=True)
-
-    sources = (probe_block_qkv, tokens, block_qkv, probe_block_out, block_out, target)
-    sources = [pltpu.with_memory_space_constraint(source, pltpu.HBM) for source in sources]
-    pack, h0, qkv, qkvd, a, ad, o, od, sq, so = call(
+    sources = (words_qkv, tokens, weight_qkv, words_out, weight_out, target)
+    late = [
+        shaped(BF16, count, 256),
+        shaped(BF16, count, 256),
+        shaped(BF16, count, 256),
+        shaped(BF16, 256, 768),
+        shaped(BF16, 256, 256),
+    ]
+    return call(
         block_forward_kernel,
         [
             shaped(BF16, peers, 16, 384),
-            shaped(BF16, count, 256),
             shaped(BF16, count, 768),
             shaped(BF16, count, 768),
             shaped(BF16, count, 512),
             shaped(BF16, count, 512),
-            shaped(BF16, count, 256),
-            shaped(BF16, count, 256),
-            shaped(BF16, 256, 768),
-            shaped(BF16, 256, 256),
-        ],
-        held(*sources) + [pltpu.VMEM((count, 256), F32)] + masks,
+        ]
+        + late,
+        "v" * 5 + "h" * 5,
+        held(*sources) + held(*late) + [pltpu.VMEM((count, 256), F32)] + MASKS,
+        sources,
         "hhhhhh",
-        sources,
         "block_forward",
-        16,
-    )
-    pack = exchange(pack)
-    sources = (
-        probe_grid_qkv, grid_qkv, probe_grid_out, grid_out,
-        probe_mlp_in, mlp_in, probe_mlp_out, mlp_out,
-    )
-    back, mid_keep, mid_send, sgq, sgo, smi, smo = call(
+        24,
+    )
+
+
+def stage_middle(core, pack, factor, sources):
+    peers = pack.shape[0]
+    count = peers * 8
+    signs = [shaped(BF16, *weight.shape) for weight in sources[1::2]]
+    return call(
         functools.partial(middle_kernel, factor),
-        [shaped(BF16, peers, 16, 256), shaped(BF16, 1536, 256), shaped(BF16, 1536, 256)]
-        + [shaped(BF16, *weight.shape) for weight in sources[1::2]],
-        masks
+        [shaped(BF16, peers, 16, 256), shaped(BF16, 1536, 256), shaped(BF16, 1536, 256)] + signs,
+        "vvvhhhh",
+        held(*sources)
+        + held(*signs)
+        + MASKS
         + [pltpu.VMEM((2, count, 128), F32)] * 3
         + [pltpu.VMEM((count, 256), F32)] * 2
         + [
@@ -517,35 +575,67 @@
             pltpu.VMEM((2 * count, 768), BF16),
             pltpu.VMEM((12, 256, 256), BF16),
         ],
-        "svvvvvvvvv",
         (core, pack, *sources),
+        "sv" + "h" * 8,
         "middle",
-        28,
-    )
-    mid_got = lax.ppermute(mid_send, "core", swap)
-    back = exchange(back)
-    keep, send = call(
+        40,
+    )
+
+
+def stage_back(core, back, saved, weight_out):
+    qkv, qkvd, a, ad, h, o, od, _, so = saved
+    count = qkv.shape[0]
+    late = (weight_out, so, o, od, h)
+    return call(
         block_back_kernel,
         [shaped(BF16, 512, 256), shaped(BF16, 512, 256)],
-        masks
+        "vv",
+        held(*late)
+        + MASKS
         + [
             pltpu.VMEM((count, 256), BF16),
             pltpu.VMEM((count, 256), BF16),
             pltpu.VMEM((count, 768), BF16),
             pltpu.VMEM((4, 256, 256), BF16),
         ],
-        "s" + "v" * 10,
-        (core, back, h0, qkv, qkvd, a, ad, o, od, block_out, so),
+        (core, back, qkv, qkvd, a, ad, *late),
+        "svvvvv" + "h" * 5,
         "block_back",
-        12,
-    )
+        20,
+    )
+
+
+def body(
+    tokens, target, block_qkv, block_out, grid_qkv, grid_out, mlp_in, mlp_out,
+    probe_block_qkv, probe_block_out, probe_grid_qkv, probe_grid_out, probe_mlp_in, probe_mlp_out,
+):
+    peers = lax.axis_size(PEERS)
+    count = tokens.shape[0] * tokens.shape[1]
+    factor = 1.0 / math.sqrt(count * peers * lax.axis_size("core"))
+    core = lax.axis_index("core").astype(jnp.int32).reshape(1)
+    swap = [(0, 1), (1, 0)]
+
+    def exchange(values):
+        return lax.all_to_all(values, PEERS, 0, 0, tiled=True)
+
+    pack, *saved = stage_forward(
+        tokens, target, block_qkv, block_out, probe_block_qkv, probe_block_out, peers
+    )
+    sources = (
+        probe_grid_qkv, grid_qkv, probe_grid_out, grid_out,
+        probe_mlp_in, mlp_in, probe_mlp_out, mlp_out,
+    )
+    back, mid_keep, mid_send, *signs = stage_middle(core, exchange(pack), factor, sources)
+    mid_got = lax.ppermute(mid_send, "core", swap)
+    keep, send = stage_back(core, exchange(back), saved, block_out)
     got = lax.ppermute(send, "core", swap)
     (parts,) = call(
         pair_sum_kernel,
         [shaped(BF16, 2048, 256)],
+        "v",
         [],
+        (mid_keep, mid_got, keep, got),
         "vvvv",
-        (mid_keep, mid_got, keep, got),
         "pair_sum",
         8,
     )
@@ -553,28 +643,23 @@
     (copies,) = call(
         peer_sum_kernel,
         [shaped(BF16, peers, 2048 // peers, 256)],
+        "v",
         [],
+        (parts,),
         "v",
-        (parts,),
         "peer_sum",
         8,
     )
     mine = exchange(copies).reshape(2048, 256)
     other = lax.ppermute(mine, "core", swap)
+    weights = (block_qkv, block_out, grid_qkv, grid_out, mlp_in, mlp_out)
     results = call(
         finish_kernel,
-        [
-            shaped(F32, 256, 768),
-            shaped(F32, 256, 256),
-            shaped(F32, 256, 768),
-            shaped(F32, 256, 256),
-            shaped(F32, 256, 1024),
-            shaped(F32, 1024, 256),
-            shaped(F32, 1, 128),
-        ],
+        [shaped(F32, *weight.shape) for weight in weights] + [shaped(F32, 1, 128)],
+        "v" * 7,
         [],
+        (core, mine, other, *saved[7:9], *signs),
         "s" + "v" * 8,
-        (core, mine, other, sq, so, sgq, sgo, smi, smo),
         "finish",
         24,
     )

time: 159 us -> 130 us (0.82)
  Pallas kernels: 49.7 us -> 30.6 us
  local copies, waits for them, and re-layouts: 9.78 us -> 0.54 us
    pallas_call x6, Pallas kernels: 49.7 us -> 30.6 us  [call(): pl.pallas_call(kernel, out_shape=[pltpu.HBM(out.shape, out.dtype) if spac...]
    unnamed x34 -> x12, local copies, waits for them, and re-layouts: 9.27 us -> 0.03 us
  transfers between devices with their start and end apart: 4 -> 4, of which waited for: 3 -> 3; matrix products, arithmetic and copies ran while one was open for 0% -> 0% of each run, Pallas kernels for 5% -> 4%
where the time goes in v2:
time: 130 us
  blocking collectives  60.6 us (47%)
  Pallas kernels  30.6 us (24%)
  starting transfers between devices  19.5 us (15%)
  waiting for transfers between devices  17.6 us (14%)
    all_to_all x3, blocking collectives, exchange(): return lax.all_to_all(values, PEERS, 0, 0, tiled=True)  60.6 us
    pallas_call x6, Pallas kernels, call(): pl.pallas_call(kernel, out_shape=[pltpu.HBM(out.shape, out.dtype) if spac...  30.6 us
    all_to_all x1, waiting for transfers between devices, exchange(): return lax.all_to_all(values, PEERS, 0, 0, tiled=True)  14.2 us
    all_to_all x1, starting transfers between devices, exchange(): return lax.all_to_all(values, PEERS, 0, 0, tiled=True)  12.2 us
    ppermute x1, starting transfers between devices, body(): other = lax.ppermute(mine, 'core', swap)  3.05 us
  transfers between devices with their start and end apart: 4, of which 3 were waited for; matrix products, arithmetic and copies ran while one was open for 0% of the time, Pallas kernels for 4%

profile of v2, /device:TPU:1, one launch (start us, length us, event | category | flops | bytes accessed | tf_op | source)
XLA Modules:
  0.0 129.5 jit_solution(17451373116252354663)
XLA Ops:
  0.6 5.8 %block_forward.1 = (bf16[64,16,384]{2,1,0:T(8,128)(2,1)}, bf16[512,768]{1,0:T(8,128)(2,1)S(1)}, bf16[512,768]{1,0:T(8,128)(2,1)S(1)}, bf16[512,512]{1,0:T(8,128)...) custom-call(s32[9,768]{1,0:T(8,128)} %pq_hbm.2, ...), custom_call_target="tpu_custom_call" | custom-call | tf_op jit(solution)/shard_map/block_forward/pallas_call | solution.py:500
  6.4 12.2 %all-to-all-start = ((bf16[64,16,384]{2,1,0:T(8,128)(2,1)}), bf16[64,16,384]{2,1,0:T(8,128)(2,1)S(1)}, u32[]{:S(2)}, u32[]{:S(2)}) async-start(bf16[64,16,384]{2,1,0:T(8,128)(2,1)} %get-tuple-element.33), calls=%async_computation | async-start | bytes 1572864 | tf_op jit(solution)/shard_map/all_to_all | solution.py:619
  18.6 14.2 %all-to-all-done.pack_ref = bf16[64,16,384]{2,1,0:T(8,128)(2,1)S(1)} async-done(((bf16[64,16,384]{2,1,0:T(8,128)(2,1)}), bf16[64,16,384]{2,1,0:T(8,128)(2,1)S(1)}, u32[]{:S(2)}, u32[]{:S(2)}) %all-to-all-start) | async-done | bytes 786464 | tf_op jit(solution)/shard_map/all_to_all | solution.py:619
  32.8 17.0 %middle.1 = (bf16[64,16,256]{2,1,0:T(8,128)(2,1)S(1)}, bf16[1536,256]{1,0:T(8,128)(2,1)S(1)}, bf16[1536,256]{1,0:T(8,128)(2,1)S(1)}, bf16[256,768]{1,0:T(8,128)(...) custom-call(s32[1]{0:T(128)} %bitcast.core_ref, ...), custom_call_target="tpu_custom_call" | custom-call | tf_op jit(solution)/shard_map/middle/pallas_call | solution.py:500
  49.8 2.6 %collective-permute-start = (bf16[1536,256]{1,0:T(8,128)(2,1)S(1)}, bf16[1536,256]{1,0:T(8,128)(2,1)S(1)}, u32[]{:S(2)}, u32[]{:S(2)}) collective-permute-start(bf16[1536,256]{1,0:T(8,128)(2,1)S(1)} %get-tuple-element.35), channel_id=1, source_target_pairs={{0,1},{1,0},{2,3},{3,2},{4,5},{5,4},{6,7},{7,6},{8,9},{9,8},{10,11... | collective-permute-start | bytes 2359304 | tf_op jit(solution)/shard_map/ppermute | solution.py:629
  52.4 17.0 %all_to_all.20.back_ref = bf16[64,16,256]{2,1,0:T(8,128)(2,1)S(1)} all-to-all(bf16[64,16,256]{2,1,0:T(8,128)(2,1)S(1)} %get-tuple-element.36), channel_id=1, replica_groups=mesh['y_lo'=2,'x'=4,'z'=4,'y_hi'=2,'core'=2] {'y_lo','x','z','y_hi'}, dimensions={0} | all-to-all | bytes 1048576 | tf_op jit(solution)/shard_map/all_to_all | solution.py:619
  69.4 4.6 %block_back.1 = (bf16[512,256]{1,0:T(8,128)(2,1)S(1)}, bf16[512,256]{1,0:T(8,128)(2,1)S(1)}) custom-call(s32[1]{0:T(128)} %bitcast.core_ref, bf16[64,16,256]{2,1,0:T(8,128)(2,1)S(1)} %all_to_all.20.back_ref, bf16[512,768]{1,0:T(8,128)(2,1)S(1)} %get-tuple-element.37.qkv_ref, bf16[512,768]{1,0:T(8,128)(2,1)S(1)} %get-tuple-element.38.qkvd_ref, ...), custom_call_target="tpu_custom_call" | custom-call | tf_op jit(solution)/shard_map/block_back/pallas_call | solution.py:500
  73.9 1.7 %collective-permute-start.1 = (bf16[512,256]{1,0:T(8,128)(2,1)S(1)}, bf16[512,256]{1,0:T(8,128)(2,1)S(1)}, u32[]{:S(2)}, u32[]{:S(2)}) collective-permute-start(bf16[512,256]{1,0:T(8,128)(2,1)S(1)} %get-tuple-element.46), channel_id=1, source_target_pairs={{0,1},{1,0},{2,3},{3,2},{4,5},{5,4},{6,7},{7,6},{8,9},{9,8},{10,11... | collective-permute-start | bytes 786440 | tf_op jit(solution)/shard_map/ppermute | solution.py:631
  75.6 1.2 collective-permute-done.1.got_ref
  76.8 0.0 collective-permute-done.mid_got_ref
  76.8 0.2 pair_sum.1
  77.0 21.6 %all_to_all.21.parts_ref = bf16[64,32,256]{2,1,0:T(8,128)(2,1)S(1)} all-to-all(bf16[64,32,256]{2,1,0:T(8,128)(2,1)S(1)} %bitcast.7), channel_id=1, replica_groups=mesh['y_lo'=2,'x'=4,'z'=4,'y_hi'=2,'core'=2] {'y_lo','x','z','y_hi'}, dimensions={0} | all-to-all | bytes 2097152 | tf_op jit(solution)/shard_map/all_to_all | solution.py:619
  98.7 0.2 peer_sum.1
  98.9 0.0 copy-start
  99.0 0.0 copy-start.1
  99.0 0.0 copy-start.2
  99.0 0.0 copy-start.3
  99.0 0.0 copy-start.4
  99.0 0.0 copy-start.5
  99.0 21.9 %all_to_all.22 = bf16[64,32,256]{2,1,0:T(8,128)(2,1)S(1)} all-to-all(bf16[64,32,256]{2,1,0:T(8,128)(2,1)S(1)} %peer_sum.1), channel_id=1, replica_groups=mesh['y_lo'=2,'x'=4,'z'=4,'y_hi'=2,'core'=2] {'y_lo','x','z','y_hi'}, dimensions={0} | all-to-all | bytes 2097152 | tf_op jit(solution)/shard_map/all_to_all | solution.py:619
  120.9 3.0 %collective-permute-start.2 = (bf16[2048,256]{1,0:T(8,128)(2,1)S(1)}, bf16[2048,256]{1,0:T(8,128)(2,1)S(1)}, u32[]{:S(2)}, u32[]{:S(2)}) collective-permute-start(bf16[2048,256]{1,0:T(8,128)(2,1)S(1)} %bitcast.5), channel_id=1, source_target_pairs={{0,1},{1,0},{2,3},{3,2},{4,5},{5,4},{6,7},{7,6},{8,9},{9,8},{10,11... | collective-permute-start | bytes 3145736 | tf_op jit(solution)/shard_map/ppermute | solution.py:654
  124.0 2.3 %collective-permute-done.2.other_ref = bf16[2048,256]{1,0:T(8,128)(2,1)S(1)} collective-permute-done((bf16[2048,256]{1,0:T(8,128)(2,1)S(1)}, bf16[2048,256]{1,0:T(8,128)(2,1)S(1)}, u32[]{:S(2)}, u32[]{:S(2)}) %collective-permute-start.2) | collective-permute-done | bytes 1048608 | tf_op jit(solution)/shard_map/ppermute | solution.py:654
  126.3 0.0 copy-done
  126.3 0.0 copy-done.1
  126.3 0.0 copy-done.2
  126.3 0.0 copy-done.3
  126.3 0.0 copy-done.4
  126.3 0.0 copy-done.5
  126.3 2.7 %finish.1 = (f32[256,768]{1,0:T(8,128)}, f32[256,256]{1,0:T(8,128)}, f32[256,768]{1,0:T(8,128)}, f32[256,256]{1,0:T(8,128)}, f32[256,1024]{1,0:T(8,128)}, /*index=5*/f32[1024,256]{1,0:T(8,128)}, f32[1,128]{1,0:T(1,128)S(1)}) custom-call(s32[1]{0:T(128)} %bitcast.core_ref, bf16[2048,256]{1,0:T(8,128)(2,1)S(1)} %bitcast.6, ...), custom_call_target="tpu_custom_call" | custom-call | tf_op jit(solution)/shard_map/finish/pallas_call | solution.py:500
  129.0 0.5 slice_bitcast_fusion
Async XLA Ops:
  6.4 26.3 %all-to-all-start = ((bf16[64,16,384]{2,1,0:T(8,128)(2,1)}), bf16[64,16,384]{2,1,0:T(8,128)(2,1)S(1)}, u32[]{:S(2)}, u32[]{:S(2)}) async-start(bf16[64,16,384]{2,1,0:T(8,128)(2,1)} %get-tuple-element.33), calls=%async_computation | async-start | bytes 1572864 | tf_op jit(solution)/shard_map/all_to_all | solution.py:619
  49.8 27.0 %collective-permute-start = (bf16[1536,256]{1,0:T(8,128)(2,1)S(1)}, bf16[1536,256]{1,0:T(8,128)(2,1)S(1)}, u32[]{:S(2)}, u32[]{:S(2)}) collective-permute-start(bf16[1536,256]{1,0:T(8,128)(2,1)S(1)} %get-tuple-element.35), channel_id=1, source_target_pairs={{0,1},{1,0},{2,3},{3,2},{4,5},{5,4},{6,7},{7,6},{8,9},{9,8},{10,11... | collective-permute-start | bytes 2359304 | tf_op jit(solution)/shard_map/ppermute | solution.py:629
  73.9 2.9 %collective-permute-start.1 = (bf16[512,256]{1,0:T(8,128)(2,1)S(1)}, bf16[512,256]{1,0:T(8,128)(2,1)S(1)}, u32[]{:S(2)}, u32[]{:S(2)}) collective-permute-start(bf16[512,256]{1,0:T(8,128)(2,1)S(1)} %get-tuple-element.46), channel_id=1, source_target_pairs={{0,1},{1,0},{2,3},{3,2},{4,5},{5,4},{6,7},{7,6},{8,9},{9,8},{10,11... | collective-permute-start | bytes 786440 | tf_op jit(solution)/shard_map/ppermute | solution.py:631
  98.9 27.3 %copy-start = (bf16[256,1024]{1,0:T(8,128)(2,1)S(1)}, bf16[256,1024]{1,0:T(8,128)(2,1)}, u32[]{:S(2)}) copy-start(bf16[256,1024]{1,0:T(8,128)(2,1)} %get-tuple-element.50.smi_ref) | copy-start | bytes 1572868
  99.0 27.3 %copy-start.1 = (bf16[1024,256]{1,0:T(8,128)(2,1)S(1)}, bf16[1024,256]{1,0:T(8,128)(2,1)}, u32[]{:S(2)}) copy-start(bf16[1024,256]{1,0:T(8,128)(2,1)} %get-tuple-element.51.smo_ref) | copy-start | bytes 1572868
  99.0 27.3 %copy-start.2 = (bf16[256,256]{1,0:T(8,128)(2,1)S(1)}, bf16[256,256]{1,0:T(8,128)(2,1)}, u32[]{:S(2)}) copy-start(bf16[256,256]{1,0:T(8,128)(2,1)} %get-tuple-element.41.so_hbm.sbo_ref) | copy-start | bytes 393220
  99.0 27.3 %copy-start.3 = (bf16[256,768]{1,0:T(8,128)(2,1)S(1)}, bf16[256,768]{1,0:T(8,128)(2,1)}, u32[]{:S(2)}) copy-start(bf16[256,768]{1,0:T(8,128)(2,1)} %get-tuple-element.47.sbq_ref) | copy-start | bytes 1179652
  99.0 27.3 %copy-start.4 = (bf16[256,768]{1,0:T(8,128)(2,1)S(1)}, bf16[256,768]{1,0:T(8,128)(2,1)}, u32[]{:S(2)}) copy-start(bf16[256,768]{1,0:T(8,128)(2,1)} %get-tuple-element.48.sgq_ref) | copy-start | bytes 1179652
  99.0 27.3 %copy-start.5 = (bf16[256,256]{1,0:T(8,128)(2,1)S(1)}, bf16[256,256]{1,0:T(8,128)(2,1)}, u32[]{:S(2)}) copy-start(bf16[256,256]{1,0:T(8,128)(2,1)} %get-tuple-element.49.sgo_ref) | copy-start | bytes 393220
  120.9 5.3 %collective-permute-start.2 = (bf16[2048,256]{1,0:T(8,128)(2,1)S(1)}, bf16[2048,256]{1,0:T(8,128)(2,1)S(1)}, u32[]{:S(2)}, u32[]{:S(2)}) collective-permute-start(bf16[2048,256]{1,0:T(8,128)(2,1)S(1)} %bitcast.5), channel_id=1, source_target_pairs={{0,1},{1,0},{2,3},{3,2},{4,5},{5,4},{6,7},{7,6},{8,9},{9,8},{10,11... | collective-permute-start | bytes 3145736 | tf_op jit(solution)/shard_map/ppermute | solution.py:654

commit v3 on v2

--- a/solution.py
+++ b/solution.py
@@ -206,7 +206,7 @@
 
 
 def block_forward_kernel(
-    pq_hbm, tok_hbm, wq_hbm, po_hbm, wo_hbm, tgt_hbm,
+    core_ref, pq_hbm, tok_hbm, wq_hbm, po_hbm, wo_hbm, tgt_hbm,
     pack_ref, qkv_ref, qkvd_ref, a_ref, ad_ref, h_hbm, o_hbm, od_hbm, sq_hbm, so_hbm,
     pq_ref, tok_ref, wq_ref, po_ref, wo_ref, tgt_ref, sems,
     h_ref, o_ref, od_ref, sq_ref, so_ref, out_sems, x_ref, ones_ref, mask_ref,
@@ -285,18 +285,18 @@
     unpack_signs(pq_ref, sq_ref)
     wait(1)
 
-    def first(i, carry):
-        at = pl.ds(pl.multiple_of(i * 256, 256), 256)
-        low = pl.ds(pl.multiple_of(i * 256 + tokens, 256), 256)
+    def first(i):
+        at = pl.ds(i * 256, 256)
+        low = pl.ds(i * 256 + tokens, 256)
         h, hd, _, _ = norm_pair(x_ref[at, :], xd_ref[at, :])
         h, hd = h.astype(BF16), hd.astype(BF16)
         h1_ref[at, :] = hd
         h1_ref[low, :] = h
         qkv_ref[at, :] = nn(h, wq_ref[...]).astype(BF16)
         qkvd_ref[at, :] = nn(lanes(hd, h), rows(wq_ref[...], sq_ref[...])).astype(BF16)
-        return carry
-
-    lax.fori_loop(0, tokens // 256, first, 0)
+
+    for i in range(tokens // 256):
+        first(i)
     o_part, od_part = o_ref.at[pl.ds(tokens, tokens), :], o_ref.at[pl.ds(0, tokens), :]
     attend(qkv_ref, qkvd_ref, a_ref, ad_ref, o_part, od_part, ones_ref, mask_ref)
     wait(2, 3, 4, 5, 6, 7)
@@ -307,9 +307,9 @@
         (sq_ref, so_ref, si_ref, sf_ref), (sq_hbm, so_hbm, si_hbm, sf_hbm), out_sems
     )
 
-    def second(i, carry):
-        at = pl.ds(pl.multiple_of(i * 256, 256), 256)
-        low = pl.ds(pl.multiple_of(i * 256 + tokens, 256), 256)
+    def second(i):
+        at = pl.ds(i * 256, 256)
+        low = pl.ds(i * 256 + tokens, 256)
         od, o = o_ref[at, :], o_ref[low, :]
         g = nn(o, wo_ref[...]).astype(BF16).astype(F32)
         gd = nn(lanes(od, o), rows(wo_ref[...], so_ref[...])).astype(BF16).astype(F32)
@@ -352,9 +352,9 @@
         dg_ref[low, :] = dgd
         do_ref[at, :] = nt(dg, wo_ref[...]).astype(BF16)
         dod_ref[at, :] = nt(lanes(dgd, dg), lanes(wo_ref[...], so_ref[...])).astype(BF16)
-        return carry
-
-    lax.fori_loop(0, tokens // 256, second, 0)
+
+    for i in range(tokens // 256):
+        second(i)
     dqkv, dqkvd = dqkv_ref.at[pl.ds(0, tokens), :], dqkv_ref.at[pl.ds(tokens, tokens), :]
     attend_back(
         qkv_ref, qkvd_ref, a_ref, ad_ref, do_ref, dod_ref, dqkv, dqkvd, ones_ref, mask_ref
@@ -451,35 +451,49 @@
         out_ref[i] = total
 
 
-def finish_kernel(
-    core_ref, mine_ref, other_ref, sbq_ref, sbo_ref, sgq_ref, sgo_ref, smi_ref, smo_ref,
-    bq_ref, bo_ref, gq_ref, go_ref, mi_ref, mo_ref, trace_ref,
-):
-    core = core_ref[0]
-    lane = lax.broadcasted_iota(jnp.int32, (1, 128), 1)
-    traces = jnp.zeros((1, 128), F32)
-    plan = (
-        (bq_ref, sbq_ref, 12, 0),
-        (bo_ref, sbo_ref, 15, 1),
-        (gq_ref, sgq_ref, 0, 2),
-        (go_ref, sgo_ref, 3, 3),
-        (mi_ref, smi_ref, 4, 4),
-        (mo_ref, smo_ref, 8, 5),
-    )
-    for out_ref, sign_ref, base, place in plan:
-        height, width = out_ref.shape
+PLACES = (12, 15, 0, 3, 4, 8)
+
+
+def write_half(who, half_ref, sign_refs, out_hbms, wide_refs, sems):
+    copies, sums = [], []
+    for n, (base, sign_ref, out_hbm, wide_ref) in enumerate(
+        zip(PLACES, sign_refs, out_hbms, wide_refs)
+    ):
+        height, width = out_hbm.shape
         across = width // 256
+        total = jnp.zeros((8, 256), F32)
         for block in range(height * width // 65536):
             cols = pl.ds(256 * (block % across), 256)
-            down = 256 * (block // across)
-            for source_ref, who in ((mine_ref, core), (other_ref, 1 - core)):
-                start = pl.multiple_of(down + who * 128, 128)
-                value = source_ref[128 * (base + block) : 128 * (base + block) + 128, :]
-                out_ref[pl.ds(start, 128), cols] = value.astype(F32)
-        total = jnp.sum(out_ref[...] * sign_ref[...].astype(F32), axis=0, keepdims=True)
-        total = jnp.sum(total, axis=1, keepdims=True) / math.sqrt(height * width)
-        traces = jnp.where(lane == place, total, traces)
-    trace_ref[...] = traces
+            down = block // across
+            at = pl.ds(pl.multiple_of(256 * down + who * 128, 128), 128)
+            value = half_ref[128 * (base + block) : 128 * (base + block) + 128, :].astype(F32)
+            wide_ref[128 * down : 128 * down + 128, cols] = value
+            signed = value * sign_ref[at, cols].astype(F32)
+            total = total + jnp.sum(signed.reshape(16, 8, 256), axis=0)
+        for down in range(height // 256):
+            at = pl.ds(pl.multiple_of(256 * down + who * 128, 128), 128)
+            copies.append(
+                pltpu.make_async_copy(
+                    wide_ref.at[pl.ds(128 * down, 128), :], out_hbm.at[at, :], sems.at[len(copies)]
+                )
+            )
+            copies[-1].start()
+        sums.append(jnp.sum(total, axis=0, keepdims=True))
+    for copy in copies:
+        copy.wait()
+    return rows(*sums, jnp.zeros((2, 256), F32))
+
+
+def finish_mine_kernel(core_ref, half_ref, *refs):
+    signs, outs, sum_ref, wides, sems = refs[:6], refs[6:12], refs[12], refs[13:19], refs[19]
+    sum_ref[...] = write_half(core_ref[0], half_ref, signs, outs, wides, sems)
+
+
+def finish_other_kernel(core_ref, half_ref, sum_ref, *refs):
+    signs, outs, trace_ref, wides, sems = refs[:6], refs[12:18], refs[18], refs[19:25], refs[25]
+    sums = sum_ref[...] + write_half(1 - core_ref[0], half_ref, signs, outs, wides, sems)
+    for n, out in enumerate(outs):
+        trace_ref[n] = jnp.sum(sums[n : n + 1, :]) / math.sqrt(out.shape[0] * out.shape[1])
 
 
 def shaped(dtype, *shape):
@@ -491,7 +505,7 @@
     return buffers + [pltpu.SemaphoreType.DMA((len(arrays),))]
 
 
-def call(kernel, outs, spaces, scratch, operands, places, name, limit):
+def call(kernel, outs, spaces, scratch, operands, places, name, limit, aliases=None):
     kinds = {"s": pltpu.SMEM, "v": pltpu.VMEM, "h": pltpu.HBM}
     pinned = [
         pltpu.with_memory_space_constraint(operand, pltpu.HBM) if place == "h" else operand
@@ -506,6 +520,7 @@
         in_specs=[pl.BlockSpec(memory_space=kinds[place]) for place in places],
         out_specs=[pl.BlockSpec(memory_space=kinds[space]) for space in spaces],
         scratch_shapes=scratch,
+        input_output_aliases=aliases or {},
         compiler_params=pltpu.CompilerParams(vmem_limit_bytes=limit * 2**20),
         name=name,
     )(*pinned)
@@ -514,7 +529,7 @@
 MASKS = [pltpu.VMEM((256, 256), BF16), pltpu.VMEM((256, GROUP), BF16)]
 
 
-def stage_forward(tokens, target, weight_qkv, weight_out, words_qkv, words_out, peers):
+def stage_forward(core, tokens, target, weight_qkv, weight_out, words_qkv, words_out, peers):
     count = tokens.shape[0] * tokens.shape[1]
     sources = (words_qkv, tokens, weight_qkv, words_out, weight_out, target)
     late = [
@@ -536,8 +551,8 @@
         + late,
         "v" * 5 + "h" * 5,
         held(*sources) + held(*late) + [pltpu.VMEM((count, 256), F32)] + MASKS,
-        sources,
-        "hhhhhh",
+        (core, *sources),
+        "shhhhhh",
         "block_forward",
         24,
     )
@@ -619,7 +634,7 @@
         return lax.all_to_all(values, PEERS, 0, 0, tiled=True)
 
     pack, *saved = stage_forward(
-        tokens, target, block_qkv, block_out, probe_block_qkv, probe_block_out, peers
+        core, tokens, target, block_qkv, block_out, probe_block_qkv, probe_block_out, peers
     )
     sources = (
         probe_grid_qkv, grid_qkv, probe_grid_out, grid_out,
@@ -653,17 +668,31 @@
     mine = exchange(copies).reshape(2048, 256)
     other = lax.ppermute(mine, "core", swap)
     weights = (block_qkv, block_out, grid_qkv, grid_out, mlp_in, mlp_out)
-    results = call(
-        finish_kernel,
-        [shaped(F32, *weight.shape) for weight in weights] + [shaped(F32, 1, 128)],
-        "v" * 7,
-        [],
-        (core, mine, other, *saved[7:9], *signs),
-        "s" + "v" * 8,
-        "finish",
-        24,
-    )
-    return (*results[:6], results[6][0, :6])
+    signs = (*saved[7:9], *signs)
+    outs = [shaped(F32, *weight.shape) for weight in weights]
+    wides = [pltpu.VMEM((out.shape[0] // 2, out.shape[1]), F32) for out in outs]
+    wides.append(pltpu.SemaphoreType.DMA((9,)))
+    *halves, sums = call(
+        finish_mine_kernel,
+        outs + [shaped(F32, 8, 256)],
+        "hhhhhhv",
+        wides,
+        (core, mine, *signs),
+        "s" + "v" * 7,
+        "finish_mine",
+        16,
+    )
+    return call(
+        finish_other_kernel,
+        outs + [shaped(F32, 6)],
+        "hhhhhhs",
+        wides,
+        (core, other, sums, *signs, *halves),
+        "s" + "v" * 8 + "h" * 6,
+        "finish_other",
+        16,
+        {9 + n: n for n in range(6)},
+    )
 
 
 def solution(mesh):

time: 130 us -> 126 us (0.969)
  blocking collectives: 60.6 us -> 86.4 us
  waiting for transfers between devices: 17.6 us -> 1.98 us
  starting transfers between devices: 19.5 us -> 7.36 us
  Pallas kernels: 30.6 us -> 29.1 us
    all_to_all x3 -> x4, blocking collectives: 60.6 us -> 86.4 us  [exchange(): return lax.all_to_all(values, PEERS, 0, 0, tiled=True)]
    all_to_all x1 -> x0, waiting for transfers between devices: 14.2 us -> none  [exchange(): return lax.all_to_all(values, PEERS, 0, 0, tiled=True)]
    all_to_all x1 -> x0, starting transfers between devices: 12.2 us -> none  [exchange(): return lax.all_to_all(values, PEERS, 0, 0, tiled=True)]
    pallas_call x6 -> x7, Pallas kernels: 30.6 us -> 29.1 us  [call(): pl.pallas_call(kernel, out_shape=[pltpu.HBM(out.shape, out.dtype) if spac...]
    ppermute x1, waiting for transfers between devices: 2.29 us -> 0.82 us  [body(): other = lax.ppermute(mine, 'core', swap)]
  transfers between devices with their start and end apart: 4 -> 3, of which waited for: 3 -> 2; matrix products, arithmetic and copies ran while one was open for 0% -> 0% of each run, Pallas kernels for 4% -> 5%
where the time goes in v3:
time: 126 us
  blocking collectives  86.4 us (69%)
  Pallas kernels  29.1 us (23%)
  starting transfers between devices  7.36 us (6%)
  waiting for transfers between devices  1.98 us (2%)
    all_to_all x4, blocking collectives, exchange(): return lax.all_to_all(values, PEERS, 0, 0, tiled=True)  86.4 us
    pallas_call x7, Pallas kernels, call(): pl.pallas_call(kernel, out_shape=[pltpu.HBM(out.shape, out.dtype) if spac...  29.1 us
    ppermute x1, starting transfers between devices, body(): other = lax.ppermute(mine, 'core', swap)  3.05 us
    ppermute x1, starting transfers between devices, body(): mid_got = lax.ppermute(mid_send, 'core', swap)  2.59 us
  transfers between devices with their start and end apart: 3, of which 2 were waited for; matrix products, arithmetic and copies ran while one was open for 0% of the time, Pallas kernels for 5%

profile of v3, /device:TPU:1, one launch (start us, length us, event | category | flops | bytes accessed | tf_op | source)
XLA Modules:
  0.0 125.8 jit_solution(16609037472193298154)
XLA Ops:
  0.6 5.0 %block_forward.1 = (bf16[64,16,384]{2,1,0:T(8,128)(2,1)S(1)}, bf16[512,768]{1,0:T(8,128)(2,1)S(1)}, bf16[512,768]{1,0:T(8,128)(2,1)S(1)}, bf16[512,512]{1,0:T(8,...) custom-call(s32[1]{0:T(128)} %bitcast.core_ref, ...), custom_call_target="tpu_custom_call" | custom-call | tf_op jit(solution)/shard_map/block_forward/pallas_call | solution.py:514
  5.6 26.1 %all_to_all.20.pack_ref = bf16[64,16,384]{2,1,0:T(8,128)(2,1)S(1)} all-to-all(bf16[64,16,384]{2,1,0:T(8,128)(2,1)S(1)} %get-tuple-element.33), channel_id=1, replica_groups=mesh['y_lo'=2,'x'=4,'z'=4,'y_hi'=2,'core'=2] {'y_lo','x','z','y_hi'}, dimensions={0} | all-to-all | bytes 1572864 | tf_op jit(solution)/shard_map/all_to_all | solution.py:634
  31.7 15.4 %middle.1 = (bf16[64,16,256]{2,1,0:T(8,128)(2,1)S(1)}, bf16[1536,256]{1,0:T(8,128)(2,1)S(1)}, bf16[1536,256]{1,0:T(8,128)(2,1)S(1)}, bf16[256,768]{1,0:T(8,128)(...) custom-call(s32[1]{0:T(128)} %bitcast.core_ref, ...), custom_call_target="tpu_custom_call" | custom-call | tf_op jit(solution)/shard_map/middle/pallas_call | solution.py:514
  47.2 2.6 %collective-permute-start = (bf16[1536,256]{1,0:T(8,128)(2,1)S(1)}, bf16[1536,256]{1,0:T(8,128)(2,1)S(1)}, u32[]{:S(2)}, u32[]{:S(2)}) collective-permute-start(bf16[1536,256]{1,0:T(8,128)(2,1)S(1)} %get-tuple-element.35), channel_id=1, source_target_pairs={{0,1},{1,0},{2,3},{3,2},{4,5},{5,4},{6,7},{7,6},{8,9},{9,8},{10,11... | collective-permute-start | bytes 2359304 | tf_op jit(solution)/shard_map/ppermute | solution.py:644
  49.8 16.8 %all_to_all.21.back_ref = bf16[64,16,256]{2,1,0:T(8,128)(2,1)S(1)} all-to-all(bf16[64,16,256]{2,1,0:T(8,128)(2,1)S(1)} %get-tuple-element.36), channel_id=1, replica_groups=mesh['y_lo'=2,'x'=4,'z'=4,'y_hi'=2,'core'=2] {'y_lo','x','z','y_hi'}, dimensions={0} | all-to-all | bytes 1048576 | tf_op jit(solution)/shard_map/all_to_all | solution.py:634
  66.5 4.7 %block_back.1 = (bf16[512,256]{1,0:T(8,128)(2,1)S(1)}, bf16[512,256]{1,0:T(8,128)(2,1)S(1)}) custom-call(s32[1]{0:T(128)} %bitcast.core_ref, bf16[64,16,256]{2,1,0:T(8,128)(2,1)S(1)} %all_to_all.21.back_ref, bf16[512,768]{1,0:T(8,128)(2,1)S(1)} %get-tuple-element.37.qkv_ref, bf16[512,768]{1,0:T(8,128)(2,1)S(1)} %get-tuple-element.38.qkvd_ref, ...), custom_call_target="tpu_custom_call" | custom-call | tf_op jit(solution)/shard_map/block_back/pallas_call | solution.py:514
  71.2 1.7 %collective-permute-start.1 = (bf16[512,256]{1,0:T(8,128)(2,1)S(1)}, bf16[512,256]{1,0:T(8,128)(2,1)S(1)}, u32[]{:S(2)}, u32[]{:S(2)}) collective-permute-start(bf16[512,256]{1,0:T(8,128)(2,1)S(1)} %get-tuple-element.46), channel_id=1, source_target_pairs={{0,1},{1,0},{2,3},{3,2},{4,5},{5,4},{6,7},{7,6},{8,9},{9,8},{10,11... | collective-permute-start | bytes 786440 | tf_op jit(solution)/shard_map/ppermute | solution.py:646
  72.9 1.2 collective-permute-done.1.got_ref
  74.1 0.0 collective-permute-done.mid_got_ref
  74.1 0.2 pair_sum.1
  74.3 21.6 %all_to_all.22.parts_ref = bf16[64,32,256]{2,1,0:T(8,128)(2,1)S(1)} all-to-all(bf16[64,32,256]{2,1,0:T(8,128)(2,1)S(1)} %bitcast.3), channel_id=1, replica_groups=mesh['y_lo'=2,'x'=4,'z'=4,'y_hi'=2,'core'=2] {'y_lo','x','z','y_hi'}, dimensions={0} | all-to-all | bytes 2097152 | tf_op jit(solution)/shard_map/all_to_all | solution.py:634
  96.0 0.2 peer_sum.1
  96.2 0.0 copy-start
  96.2 0.0 copy-start.1
  96.3 0.0 copy-start.2
  96.3 0.0 copy-start.3
  96.3 0.0 copy-start.4
  96.3 0.0 copy-start.5
  96.3 21.9 %all_to_all.23 = bf16[64,32,256]{2,1,0:T(8,128)(2,1)S(1)} all-to-all(bf16[64,32,256]{2,1,0:T(8,128)(2,1)S(1)} %peer_sum.1), channel_id=1, replica_groups=mesh['y_lo'=2,'x'=4,'z'=4,'y_hi'=2,'core'=2] {'y_lo','x','z','y_hi'}, dimensions={0} | all-to-all | bytes 2097152 | tf_op jit(solution)/shard_map/all_to_all | solution.py:634
  118.2 3.0 %collective-permute-start.2 = (bf16[2048,256]{1,0:T(8,128)(2,1)S(1)}, bf16[2048,256]{1,0:T(8,128)(2,1)S(1)}, u32[]{:S(2)}, u32[]{:S(2)}) collective-permute-start(bf16[2048,256]{1,0:T(8,128)(2,1)S(1)} %bitcast.4), channel_id=1, source_target_pairs={{0,1},{1,0},{2,3},{3,2},{4,5},{5,4},{6,7},{7,6},{8,9},{9,8},{10,11... | collective-permute-start | bytes 3145736 | tf_op jit(solution)/shard_map/ppermute | solution.py:669
  121.3 0.0 copy-done
  121.3 0.0 copy-done.1
  121.3 0.0 copy-done.2
  121.3 0.0 copy-done.3
  121.3 0.0 copy-done.4
  121.3 0.0 copy-done.5
  121.3 1.4 %finish_mine.1 = (f32[256,768]{1,0:T(8,128)}, f32[256,256]{1,0:T(8,128)}, f32[256,768]{1,0:T(8,128)}, f32[256,256]{1,0:T(8,128)}, f32[256,1024]{1,0:T(8,128)}, /...) custom-call(s32[1]{0:T(128)} %bitcast.core_ref, bf16[2048,256]{1,0:T(8,128)(2,1)S(1)} %bitcast.5, ...), custom_call_target="tpu_custom_call" | custom-call | tf_op jit(solution)/shard_map/finish_mine/pallas_call | solution.py:514
  122.7 0.8 collective-permute-done.2.half_ref
  123.6 2.1 %finish_other.1 = (f32[256,768]{1,0:T(8,128)}, f32[256,256]{1,0:T(8,128)}, f32[256,768]{1,0:T(8,128)}, f32[256,256]{1,0:T(8,128)}, f32[256,1024]{1,0:T(8,128)}, /*index=5*/f32[1024,256]{1,0:T(8,128)}, f32[6]{0:T(128)}) custom-call(s32[1]{0:T(128)} %bitcast.core_ref, ...), custom_call_target="tpu_custom_call", output_to_operand_aliasing={{0}: (9, {}), {1}: (10, {}), {2}: (11, {}), {3}: (12, {}), ... | custom-call | tf_op jit(solution)/shard_map/finish_other/pallas_call | solution.py:514
Async XLA Ops:
  47.2 26.9 %collective-permute-start = (bf16[1536,256]{1,0:T(8,128)(2,1)S(1)}, bf16[1536,256]{1,0:T(8,128)(2,1)S(1)}, u32[]{:S(2)}, u32[]{:S(2)}) collective-permute-start(bf16[1536,256]{1,0:T(8,128)(2,1)S(1)} %get-tuple-element.35), channel_id=1, source_target_pairs={{0,1},{1,0},{2,3},{3,2},{4,5},{5,4},{6,7},{7,6},{8,9},{9,8},{10,11... | collective-permute-start | bytes 2359304 | tf_op jit(solution)/shard_map/ppermute | solution.py:644
  71.2 2.9 %collective-permute-start.1 = (bf16[512,256]{1,0:T(8,128)(2,1)S(1)}, bf16[512,256]{1,0:T(8,128)(2,1)S(1)}, u32[]{:S(2)}, u32[]{:S(2)}) collective-permute-start(bf16[512,256]{1,0:T(8,128)(2,1)S(1)} %get-tuple-element.46), channel_id=1, source_target_pairs={{0,1},{1,0},{2,3},{3,2},{4,5},{5,4},{6,7},{7,6},{8,9},{9,8},{10,11... | collective-permute-start | bytes 786440 | tf_op jit(solution)/shard_map/ppermute | solution.py:646
  96.2 25.0 %copy-start = (bf16[256,1024]{1,0:T(8,128)(2,1)S(1)}, bf16[256,1024]{1,0:T(8,128)(2,1)}, u32[]{:S(2)}) copy-start(bf16[256,1024]{1,0:T(8,128)(2,1)} %get-tuple-element.50.refs_4_) | copy-start | bytes 1572868
  96.2 25.0 %copy-start.1 = (bf16[1024,256]{1,0:T(8,128)(2,1)S(1)}, bf16[1024,256]{1,0:T(8,128)(2,1)}, u32[]{:S(2)}) copy-start(bf16[1024,256]{1,0:T(8,128)(2,1)} %get-tuple-element.51.refs_5_) | copy-start | bytes 1572868
  96.3 25.0 %copy-start.2 = (bf16[256,768]{1,0:T(8,128)(2,1)S(1)}, bf16[256,768]{1,0:T(8,128)(2,1)}, u32[]{:S(2)}) copy-start(bf16[256,768]{1,0:T(8,128)(2,1)} %get-tuple-element.47.refs_0_) | copy-start | bytes 1179652
  96.3 25.0 %copy-start.3 = (bf16[256,768]{1,0:T(8,128)(2,1)S(1)}, bf16[256,768]{1,0:T(8,128)(2,1)}, u32[]{:S(2)}) copy-start(bf16[256,768]{1,0:T(8,128)(2,1)} %get-tuple-element.48.refs_2_) | copy-start | bytes 1179652
  96.3 25.0 %copy-start.4 = (bf16[256,256]{1,0:T(8,128)(2,1)S(1)}, bf16[256,256]{1,0:T(8,128)(2,1)}, u32[]{:S(2)}) copy-start(bf16[256,256]{1,0:T(8,128)(2,1)} %get-tuple-element.41.so_hbm.refs_1_) | copy-start | bytes 393220
  96.3 25.0 %copy-start.5 = (bf16[256,256]{1,0:T(8,128)(2,1)S(1)}, bf16[256,256]{1,0:T(8,128)(2,1)}, u32[]{:S(2)}) copy-start(bf16[256,256]{1,0:T(8,128)(2,1)} %get-tuple-element.49.refs_3_) | copy-start | bytes 393220
  118.2 5.3 %collective-permute-start.2 = (bf16[2048,256]{1,0:T(8,128)(2,1)S(1)}, bf16[2048,256]{1,0:T(8,128)(2,1)S(1)}, u32[]{:S(2)}, u32[]{:S(2)}) collective-permute-start(bf16[2048,256]{1,0:T(8,128)(2,1)S(1)} %bitcast.4), channel_id=1, source_target_pairs={{0,1},{1,0},{2,3},{3,2},{4,5},{5,4},{6,7},{7,6},{8,9},{9,8},{10,11... | collective-permute-start | bytes 3145736 | tf_op jit(solution)/shard_map/ppermute | solution.py:669

commit v4 on v3

--- a/solution.py
+++ b/solution.py
@@ -128,6 +128,15 @@
     return ref[at, pl.ds(256 * kind + GROUP * g, GROUP)]
 
 
+def twice(values, dots):
+    return rows(lanes(values, jnp.zeros_like(values)), lanes(dots, values))
+
+
+def segment_sums(values, ones):
+    total = nn(rows(*[value.astype(BF16) for value in values]), ones)
+    return [total[WINDOW * i : WINDOW * (i + 1), :] for i in range(len(values))]
+
+
 def attend(qkv_ref, qkvd_ref, a_ref, ad_ref, o_ref, od_ref, ones_ref, mask_ref):
     def step(spots):
         ones = ones_ref[...]
@@ -138,12 +147,12 @@
             q, qd = heads_of(qkv_ref, at, 0, g), heads_of(qkvd_ref, at, 0, g)
             kb = spread(heads_of(qkv_ref, at, 1, g), mask)
             kdb = spread(heads_of(qkvd_ref, at, 1, g), mask)
-            raised.append(jnp.exp(nt(q, kb) * SCALE))
-            scores_dot.append(nt(lanes(qd, q), lanes(kb, kdb)) * SCALE)
-        sums = [nn(e.astype(BF16), ones) for e in raised]
-        weights = [e / total for e, total in zip(raised, sums)]
+            both = nt(twice(q, qd), lanes(kb, kdb)) * SCALE
+            raised.append(jnp.exp(both[:WINDOW]))
+            scores_dot.append(both[WINDOW:])
+        weights = [e / total for e, total in zip(raised, segment_sums(raised, ones))]
         moved = [w * sd for w, sd in zip(weights, scores_dot)]
-        sums = [nn(m.astype(BF16), ones) for m in moved]
+        sums = segment_sums(moved, ones)
         weights_dot = [m - w * total for m, w, total in zip(moved, weights, sums)]
         for (at, g), w, wd in zip(units, weights, weights_dot):
             a, ad = w.astype(BF16), wd.astype(BF16)
@@ -153,8 +162,9 @@
             vb = spread(heads_of(qkv_ref, at, 2, g), mask)
             vdb = spread(heads_of(qkvd_ref, at, 2, g), mask)
             here = pl.ds(GROUP * g, GROUP)
-            o_ref[at, here] = nn(a, vb).astype(BF16)
-            od_ref[at, here] = nn(lanes(ad, a), rows(vb, vdb)).astype(BF16)
+            both = nn(twice(a, ad), rows(vb, vdb)).astype(BF16)
+            o_ref[at, here] = both[:WINDOW]
+            od_ref[at, here] = both[WINDOW:]
 
     per_batch(qkv_ref.shape[0] // WINDOW, step)
 
@@ -169,38 +179,44 @@
         da, dad, first, second = [], [], [], []
         for at, g in units:
             here = pl.ds(GROUP * g, GROUP)
-            do, dod = do_ref[at, here], dod_ref[at, here]
             vb = spread(heads_of(qkv_ref, at, 2, g), mask)
             vdb = spread(heads_of(qkvd_ref, at, 2, g), mask)
-            da.append(nt(do, vb))
-            dad.append(nt(lanes(dod, do), lanes(vb, vdb)))
+            both = nt(twice(do_ref[at, here], dod_ref[at, here]), lanes(vb, vdb))
+            da.append(both[:WINDOW])
+            dad.append(both[WINDOW:])
         for (at, g), x, xd in zip(units, da, dad):
             spot = pl.ds(256 * g, 256)
             a, ad = a_ref[at, spot].astype(F32), ad_ref[at, spot].astype(F32)
-            first.append((a * x).astype(BF16))
-            second.append((ad * x + a * xd).astype(BF16))
-        first = [nn(x, ones) for x in first]
-        second = [nn(x, ones) for x in second]
+            first.append(a * x)
+            second.append(ad * x + a * xd)
+        first, second = segment_sums(first, ones), segment_sums(second, ones)
         for (at, g), x, xd, total, total_dot in zip(units, da, dad, first, second):
             spot = pl.ds(256 * g, 256)
             here = pl.ds(GROUP * g, GROUP)
             qs, ks, vs = (pl.ds(256 * i + GROUP * g, GROUP) for i in range(3))
             ab, adb = a_ref[at, spot], ad_ref[at, spot]
-            a, ad = ab.astype(F32), adb.astype(F32)
+            a, ad = ab.astype(F32) * SCALE, adb.astype(F32) * SCALE
             rest = x - total
             rest_dot = xd - total_dot
-            ds = (a * rest * SCALE).astype(BF16)
-            dsd = ((ad * rest + a * rest_dot) * SCALE).astype(BF16)
+            ds = (a * rest).astype(BF16)
+            dsd = (ad * rest + a * rest_dot).astype(BF16)
             do, dod = do_ref[at, here], dod_ref[at, here]
             q, qd = qkv_ref[at, qs], qkvd_ref[at, qs]
             kb, kdb = spread(qkv_ref[at, ks], mask), spread(qkvd_ref[at, ks], mask)
-            dqkvd_ref[at, qs] = nn(lanes(dsd, ds), rows(kb, kdb)).astype(BF16)
-            dqkvd_ref[at, ks] = collect(tn(rows(dsd, ds), rows(q, qd))).astype(BF16)
-            dqkvd_ref[at, vs] = collect(tn(rows(adb, ab), rows(do, dod))).astype(BF16)
-            if dqkv_ref is not None:
-                dqkv_ref[at, qs] = nn(ds, kb).astype(BF16)
-                dqkv_ref[at, ks] = collect(tn(ds, q)).astype(BF16)
-                dqkv_ref[at, vs] = collect(tn(ab, do)).astype(BF16)
+            if dqkv_ref is None:
+                dqkvd_ref[at, qs] = nn(lanes(dsd, ds), rows(kb, kdb)).astype(BF16)
+                dqkvd_ref[at, ks] = collect(tn(rows(dsd, ds), rows(q, qd))).astype(BF16)
+                dqkvd_ref[at, vs] = collect(tn(rows(adb, ab), rows(do, dod))).astype(BF16)
+            else:
+                both = nn(twice(ds, dsd), rows(kb, kdb)).astype(BF16)
+                dqkv_ref[at, qs] = both[:WINDOW]
+                dqkvd_ref[at, qs] = both[WINDOW:]
+                both = tn(rows(dsd, ds), twice(q, qd))
+                dqkvd_ref[at, ks] = collect(both[:, :GROUP]).astype(BF16)
+                dqkv_ref[at, ks] = collect(both[:, GROUP:]).astype(BF16)
+                both = tn(rows(adb, ab), twice(do, dod))
+                dqkvd_ref[at, vs] = collect(both[:, :GROUP]).astype(BF16)
+                dqkv_ref[at, vs] = collect(both[:, GROUP:]).astype(BF16)
 
     per_batch(qkv_ref.shape[0] // WINDOW, step)
 
@@ -253,19 +269,13 @@
 
 def middle_kernel(
     factor,
-    core_ref, pack_ref, pq_hbm, wq_hbm, po_hbm, wo_hbm, pi_hbm, wi_hbm, pf_hbm, wf_hbm,
+    core_ref, pack_ref, pq_ref, wq_ref, po_ref, wo_ref, pi_ref, wi_ref, pf_ref, wf_ref,
     back_ref, keep_ref, send_ref, sq_hbm, so_hbm, si_hbm, sf_hbm,
-    pq_ref, wq_ref, po_ref, wo_ref, pi_ref, wi_ref, pf_ref, wf_ref, sems,
     sq_ref, so_ref, si_ref, sf_ref, out_sems, ones_ref, mask_ref, mix_ref, mixd_ref, mixt_ref,
     x_ref, xd_ref, t_ref, h1_ref, h2_ref, qkv_ref, qkvd_ref, a_ref, ad_ref, o_ref,
     ud_ref, dz_ref, dx_ref, dxd_ref, dg_ref, do_ref, dod_ref, dqkv_ref, hv_ref,
 ):
     tokens = x_ref.shape[0]
-    wait = fetch(
-        (pq_hbm, wq_hbm, po_hbm, wo_hbm, pi_hbm, wi_hbm, pf_hbm, wf_hbm),
-        (pq_ref, wq_ref, po_ref, wo_ref, pi_ref, wi_ref, pf_ref, wf_ref),
-        sems,
-    )
     fill_masks(ones_ref, mask_ref)
     arrived = pack_ref[:, :, 0:256].astype(F32)
     for c in range(2):
@@ -281,9 +291,7 @@
             x_ref[at, cols] = mix_ref[c, pl.ds(w, WINDOW, stride=8), :]
             xd_ref[at, cols] = mixd_ref[c, pl.ds(w, WINDOW, stride=8), :]
             t_ref[at, cols] = mixt_ref[c, pl.ds(w, WINDOW, stride=8), :].astype(BF16)
-    wait(0)
     unpack_signs(pq_ref, sq_ref)
-    wait(1)
 
     def first(i):
         at = pl.ds(i * 256, 256)
@@ -299,7 +307,6 @@
         first(i)
     o_part, od_part = o_ref.at[pl.ds(tokens, tokens), :], o_ref.at[pl.ds(0, tokens), :]
     attend(qkv_ref, qkvd_ref, a_ref, ad_ref, o_part, od_part, ones_ref, mask_ref)
-    wait(2, 3, 4, 5, 6, 7)
     unpack_signs(po_ref, so_ref)
     unpack_signs(pi_ref, si_ref)
     unpack_signs(pf_ref, sf_ref)
@@ -308,8 +315,8 @@
     )
 
     def second(i):
-        at = pl.ds(i * 256, 256)
-        low = pl.ds(i * 256 + tokens, 256)
+        at = pl.ds(i * 512, 512)
+        low = pl.ds(i * 512 + tokens, 512)
         od, o = o_ref[at, :], o_ref[low, :]
         g = nn(o, wo_ref[...]).astype(BF16).astype(F32)
         gd = nn(lanes(od, o), rows(wo_ref[...], so_ref[...])).astype(BF16).astype(F32)
@@ -318,8 +325,8 @@
         h2_ref[at, :] = hdb
         h2_ref[low, :] = hb
         t = t_ref[at, :]
-        dh = jnp.zeros((256, 256), F32)
-        dhd = jnp.zeros((256, 256), F32)
+        dh = jnp.zeros((512, 256), F32)
+        dhd = jnp.zeros((512, 256), F32)
         for c in range(4):
             cols = pl.ds(256 * c, 256)
             wi, si = wi_ref[:, cols], si_ref[:, cols]
@@ -353,7 +360,7 @@
         do_ref[at, :] = nt(dg, wo_ref[...]).astype(BF16)
         dod_ref[at, :] = nt(lanes(dgd, dg), lanes(wo_ref[...], so_ref[...])).astype(BF16)
 
-    for i in range(tokens // 256):
+    for i in range(tokens // 512):
         second(i)
     dqkv, dqkvd = dqkv_ref.at[pl.ds(0, tokens), :], dqkv_ref.at[pl.ds(tokens, tokens), :]
     attend_back(
@@ -409,23 +416,17 @@
 
 
 def block_back_kernel(
-    core_ref, back_ref, qkv_ref, qkvd_ref, a_ref, ad_ref, wo_hbm, so_hbm, o_hbm, od_hbm, h_hbm,
+    core_ref, back_ref, qkv_ref, qkvd_ref, a_ref, ad_ref, wo_ref, so_ref, o_ref, od_ref, h_ref,
     keep_ref, send_ref,
-    wo_ref, so_ref, o_ref, od_ref, h_ref, sems,
     ones_ref, mask_ref, do_ref, dod_ref, dqkvd_ref, hv_ref,
 ):
     tokens = h_ref.shape[0]
-    wait = fetch(
-        (wo_hbm, so_hbm, o_hbm, od_hbm, h_hbm), (wo_ref, so_ref, o_ref, od_ref, h_ref), sems
-    )
     fill_masks(ones_ref, mask_ref)
     arrived = back_ref[...].astype(F32)
     dx = arrived[:, 0:8, :].reshape(tokens, 256).astype(BF16)
     dxd = arrived[:, 8:16, :].reshape(tokens, 256).astype(BF16)
-    wait(0, 1)
     do_ref[...] = nt(dx, wo_ref[...]).astype(BF16)
     dod_ref[...] = nt(lanes(dxd, dx), lanes(wo_ref[...], so_ref[...])).astype(BF16)
-    wait(2, 3, 4)
     hv_ref[3] = tn(rows(od_ref[...], o_ref[...]), rows(dx, dxd)).astype(BF16)
     attend_back(
         qkv_ref, qkvd_ref, a_ref, ad_ref, do_ref, dod_ref, None, dqkvd_ref, ones_ref, mask_ref
@@ -566,8 +567,7 @@
         functools.partial(middle_kernel, factor),
         [shaped(BF16, peers, 16, 256), shaped(BF16, 1536, 256), shaped(BF16, 1536, 256)] + signs,
         "vvvhhhh",
-        held(*sources)
-        + held(*signs)
+        held(*signs)
         + MASKS
         + [pltpu.VMEM((2, count, 128), F32)] * 3
         + [pltpu.VMEM((count, 256), F32)] * 2
@@ -591,7 +591,7 @@
             pltpu.VMEM((12, 256, 256), BF16),
         ],
         (core, pack, *sources),
-        "sv" + "h" * 8,
+        "s" + "v" * 9,
         "middle",
         40,
     )
@@ -605,8 +605,7 @@
         block_back_kernel,
         [shaped(BF16, 512, 256), shaped(BF16, 512, 256)],
         "vv",
-        held(*late)
-        + MASKS
+        MASKS
         + [
             pltpu.VMEM((count, 256), BF16),
             pltpu.VMEM((count, 256), BF16),
@@ -614,7 +613,7 @@
             pltpu.VMEM((4, 256, 256), BF16),
         ],
         (core, back, qkv, qkvd, a, ad, *late),
-        "svvvvv" + "h" * 5,
+        "s" + "v" * 10,
         "block_back",
         20,
     )

time: 126 us -> 122 us (0.968)
  Pallas kernels: 29.1 us -> 24.9 us
    pallas_call x7, Pallas kernels: 29.1 us -> 24.9 us  [call(): pl.pallas_call(kernel, out_shape=[pltpu.HBM(out.shape, out.dtype) if spac...]
  transfers between devices with their start and end apart: 3 -> 3, of which waited for: 2 -> 2; matrix products, arithmetic and copies ran while one was open for 0% -> 0% of each run, Pallas kernels for 5% -> 4%
where the time goes in v4:
time: 122 us
  blocking collectives  86.7 us (71%)
  Pallas kernels  24.9 us (20%)
  starting transfers between devices  7.37 us (6%)
  waiting for transfers between devices  1.99 us (2%)
    all_to_all x4, blocking collectives, exchange(): return lax.all_to_all(values, PEERS, 0, 0, tiled=True)  86.7 us
    pallas_call x7, Pallas kernels, call(): pl.pallas_call(kernel, out_shape=[pltpu.HBM(out.shape, out.dtype) if spac...  24.9 us
    ppermute x1, starting transfers between devices, body(): other = lax.ppermute(mine, 'core', swap)  3.05 us
    ppermute x1, starting transfers between devices, body(): mid_got = lax.ppermute(mid_send, 'core', swap)  2.59 us
  transfers between devices with their start and end apart: 3, of which 2 were waited for; matrix products, arithmetic and copies ran while one was open for 0% of the time, Pallas kernels for 4%

profile of v4, /device:TPU:1, one launch (start us, length us, event | category | flops | bytes accessed | tf_op | source)
XLA Modules:
  0.0 122.1 jit_solution(2101296170046845765)
XLA Ops:
  0.6 0.0 copy-start.14
  0.6 0.0 copy-start.15
  0.7 0.0 copy-start.16
  0.7 0.0 copy-start.17
  0.7 4.6 %block_forward.1 = (bf16[64,16,384]{2,1,0:T(8,128)(2,1)S(1)}, bf16[512,768]{1,0:T(8,128)(2,1)S(1)}, bf16[512,768]{1,0:T(8,128)(2,1)S(1)}, bf16[512,512]{1,0:T(8,...) custom-call(s32[1]{0:T(128)} %bitcast.core_ref, ...), custom_call_target="tpu_custom_call" | custom-call | tf_op jit(solution)/shard_map/block_forward/pallas_call | solution.py:515
  5.3 0.0 copy-start.6
  5.3 0.0 copy-start.7
  5.3 0.0 copy-start.9
  5.3 0.0 copy-start.13
  5.3 26.2 %all_to_all.20.pack_ref = bf16[64,16,384]{2,1,0:T(8,128)(2,1)S(1)} all-to-all(bf16[64,16,384]{2,1,0:T(8,128)(2,1)S(1)} %get-tuple-element.33), channel_id=1, replica_groups=mesh['y_lo'=2,'x'=4,'z'=4,'y_hi'=2,'core'=2] {'y_lo','x','z','y_hi'}, dimensions={0} | all-to-all | bytes 1572864 | tf_op jit(solution)/shard_map/all_to_all | solution.py:633
  31.6 0.0 copy-done.14
  31.6 0.0 copy-done.15
  31.6 0.0 copy-done.16
  31.6 0.0 copy-done.17
  31.6 0.0 copy-done.6
  31.6 0.0 copy-done.7
  31.6 0.0 copy-done.9
  31.6 0.0 copy-done.13
  31.6 13.2 %middle.1 = (bf16[64,16,256]{2,1,0:T(8,128)(2,1)S(1)}, bf16[1536,256]{1,0:T(8,128)(2,1)S(1)}, bf16[1536,256]{1,0:T(8,128)(2,1)S(1)}, bf16[256,768]{1,0:T(8,128)(...) custom-call(s32[1]{0:T(128)} %bitcast.core_ref, ...), custom_call_target="tpu_custom_call" | custom-call | tf_op jit(solution)/shard_map/middle/pallas_call | solution.py:515
  44.9 2.6 %collective-permute-start = (bf16[1536,256]{1,0:T(8,128)(2,1)S(1)}, bf16[1536,256]{1,0:T(8,128)(2,1)S(1)}, u32[]{:S(2)}, u32[]{:S(2)}) collective-permute-start(bf16[1536,256]{1,0:T(8,128)(2,1)S(1)} %get-tuple-element.35), channel_id=1, source_target_pairs={{0,1},{1,0},{2,3},{3,2},{4,5},{5,4},{6,7},{7,6},{8,9},{9,8},{10,11... | collective-permute-start | bytes 2359304 | tf_op jit(solution)/shard_map/ppermute | solution.py:643
  47.5 0.0 copy-start.4
  47.5 0.0 copy-start.8
  47.5 0.0 copy-start.10
  47.5 0.0 copy-start.11
  47.5 0.0 copy-start.12
  47.5 16.9 %all_to_all.21.back_ref = bf16[64,16,256]{2,1,0:T(8,128)(2,1)S(1)} all-to-all(bf16[64,16,256]{2,1,0:T(8,128)(2,1)S(1)} %get-tuple-element.36), channel_id=1, replica_groups=mesh['y_lo'=2,'x'=4,'z'=4,'y_hi'=2,'core'=2] {'y_lo','x','z','y_hi'}, dimensions={0} | all-to-all | bytes 1048576 | tf_op jit(solution)/shard_map/all_to_all | solution.py:633
  64.3 0.0 copy-done.4
  64.4 0.0 copy-done.8
  64.4 0.0 copy-done.10
  64.4 0.0 copy-done.11
  64.4 0.0 copy-done.12
  64.4 3.1 %block_back.1 = (bf16[512,256]{1,0:T(8,128)(2,1)S(1)}, bf16[512,256]{1,0:T(8,128)(2,1)S(1)}) custom-call(s32[1]{0:T(128)} %bitcast.core_ref, bf16[64,16,256]{2,1,0:T(8,128)(2,1)S(1)} %all_to_all.21.back_ref, bf16[512,768]{1,0:T(8,128)(2,1)S(1)} %get-tuple-element.37.qkv_ref, bf16[512,768]{1,0:T(8,128)(2,1)S(1)} %get-tuple-element.38.qkvd_ref, ...), custom_call_target="tpu_custom_call" | custom-call | tf_op jit(solution)/shard_map/block_back/pallas_call | solution.py:515
  67.5 1.7 %collective-permute-start.1 = (bf16[512,256]{1,0:T(8,128)(2,1)S(1)}, bf16[512,256]{1,0:T(8,128)(2,1)S(1)}, u32[]{:S(2)}, u32[]{:S(2)}) collective-permute-start(bf16[512,256]{1,0:T(8,128)(2,1)S(1)} %get-tuple-element.46), channel_id=1, source_target_pairs={{0,1},{1,0},{2,3},{3,2},{4,5},{5,4},{6,7},{7,6},{8,9},{9,8},{10,11... | collective-permute-start | bytes 786440 | tf_op jit(solution)/shard_map/ppermute | solution.py:645
  69.2 1.2 collective-permute-done.1.got_ref
  70.3 0.0 collective-permute-done.mid_got_ref
  70.4 0.2 pair_sum.1
  70.6 21.7 %all_to_all.22.parts_ref = bf16[64,32,256]{2,1,0:T(8,128)(2,1)S(1)} all-to-all(bf16[64,32,256]{2,1,0:T(8,128)(2,1)S(1)} %bitcast.3), channel_id=1, replica_groups=mesh['y_lo'=2,'x'=4,'z'=4,'y_hi'=2,'core'=2] {'y_lo','x','z','y_hi'}, dimensions={0} | all-to-all | bytes 2097152 | tf_op jit(solution)/shard_map/all_to_all | solution.py:633
  92.2 0.2 peer_sum.1
  92.5 0.0 copy-start
  92.5 0.0 copy-start.1
  92.5 0.0 copy-start.2
  92.5 0.0 copy-start.3
  92.5 0.0 copy-start.5
  92.6 21.9 %all_to_all.23 = bf16[64,32,256]{2,1,0:T(8,128)(2,1)S(1)} all-to-all(bf16[64,32,256]{2,1,0:T(8,128)(2,1)S(1)} %peer_sum.1), channel_id=1, replica_groups=mesh['y_lo'=2,'x'=4,'z'=4,'y_hi'=2,'core'=2] {'y_lo','x','z','y_hi'}, dimensions={0} | all-to-all | bytes 2097152 | tf_op jit(solution)/shard_map/all_to_all | solution.py:633
  114.5 3.0 %collective-permute-start.2 = (bf16[2048,256]{1,0:T(8,128)(2,1)S(1)}, bf16[2048,256]{1,0:T(8,128)(2,1)S(1)}, u32[]{:S(2)}, u32[]{:S(2)}) collective-permute-start(bf16[2048,256]{1,0:T(8,128)(2,1)S(1)} %bitcast.4), channel_id=1, source_target_pairs={{0,1},{1,0},{2,3},{3,2},{4,5},{5,4},{6,7},{7,6},{8,9},{9,8},{10,11... | collective-permute-start | bytes 3145736 | tf_op jit(solution)/shard_map/ppermute | solution.py:668
  117.5 0.0 copy-done
  117.5 0.0 copy-done.1
  117.5 0.0 copy-done.2
  117.5 0.0 copy-done.3
  117.5 0.0 copy-done.5
  117.5 1.4 %finish_mine.1 = (f32[256,768]{1,0:T(8,128)}, f32[256,256]{1,0:T(8,128)}, f32[256,768]{1,0:T(8,128)}, f32[256,256]{1,0:T(8,128)}, f32[256,1024]{1,0:T(8,128)}, /...) custom-call(s32[1]{0:T(128)} %bitcast.core_ref, bf16[2048,256]{1,0:T(8,128)(2,1)S(1)} %bitcast.5, ...), custom_call_target="tpu_custom_call" | custom-call | tf_op jit(solution)/shard_map/finish_mine/pallas_call | solution.py:515
  119.0 0.8 collective-permute-done.2.half_ref
  119.8 2.1 %finish_other.1 = (f32[256,768]{1,0:T(8,128)}, f32[256,256]{1,0:T(8,128)}, f32[256,768]{1,0:T(8,128)}, f32[256,256]{1,0:T(8,128)}, f32[256,1024]{1,0:T(8,128)}, /*index=5*/f32[1024,256]{1,0:T(8,128)}, f32[6]{0:T(128)}) custom-call(s32[1]{0:T(128)} %bitcast.core_ref, ...), custom_call_target="tpu_custom_call", output_to_operand_aliasing={{0}: (9, {}), {1}: (10, {}), {2}: (11, {}), {3}: (12, {}), ... | custom-call | tf_op jit(solution)/shard_map/finish_other/pallas_call | solution.py:515
Async XLA Ops:
  0.6 30.9 %copy-start.14 = (s32[9,1024]{1,0:T(8,128)S(1)}, s32[9,1024]{1,0:T(8,128)}, u32[]{:S(2)}) copy-start(s32[9,1024]{1,0:T(8,128)} %pi_ref.1) | copy-start | bytes 110596
  0.6 30.9 %copy-start.15 = (s32[9,768]{1,0:T(8,128)S(1)}, s32[9,768]{1,0:T(8,128)}, u32[]{:S(2)}) copy-start(s32[9,768]{1,0:T(8,128)} %pq_ref.1) | copy-start | bytes 82948
  0.7 30.9 %copy-start.16 = (s32[35,256]{1,0:T(8,128)S(1)}, s32[35,256]{1,0:T(8,128)}, u32[]{:S(2)}) copy-start(s32[35,256]{1,0:T(8,128)} %pf_ref.1) | copy-start | bytes 107524
  0.7 30.9 %copy-start.17 = (s32[9,256]{1,0:T(8,128)S(1)}, s32[9,256]{1,0:T(8,128)}, u32[]{:S(2)}) copy-start(s32[9,256]{1,0:T(8,128)} %po_ref.1) | copy-start | bytes 27652
  5.3 26.3 %copy-start.6 = (bf16[256,1024]{1,0:T(8,128)(2,1)S(1)}, bf16[256,1024]{1,0:T(8,128)(2,1)}, u32[]{:S(2)}) copy-start(bf16[256,1024]{1,0:T(8,128)(2,1)} %wi_ref.1) | copy-start | bytes 1572868
  5.3 26.3 %copy-start.7 = (bf16[1024,256]{1,0:T(8,128)(2,1)S(1)}, bf16[1024,256]{1,0:T(8,128)(2,1)}, u32[]{:S(2)}) copy-start(bf16[1024,256]{1,0:T(8,128)(2,1)} %wf_ref.1) | copy-start | bytes 1572868
  5.3 26.3 %copy-start.9 = (bf16[256,768]{1,0:T(8,128)(2,1)S(1)}, bf16[256,768]{1,0:T(8,128)(2,1)}, u32[]{:S(2)}) copy-start(bf16[256,768]{1,0:T(8,128)(2,1)} %wq_ref.1) | copy-start | bytes 1179652
  5.3 26.3 %copy-start.13 = (bf16[256,256]{1,0:T(8,128)(2,1)S(1)}, bf16[256,256]{1,0:T(8,128)(2,1)}, u32[]{:S(2)}) copy-start(bf16[256,256]{1,0:T(8,128)(2,1)} %wo_ref.2) | copy-start | bytes 393220
  44.9 25.5 %collective-permute-start = (bf16[1536,256]{1,0:T(8,128)(2,1)S(1)}, bf16[1536,256]{1,0:T(8,128)(2,1)S(1)}, u32[]{:S(2)}, u32[]{:S(2)}) collective-permute-start(bf16[1536,256]{1,0:T(8,128)(2,1)S(1)} %get-tuple-element.35), channel_id=1, source_target_pairs={{0,1},{1,0},{2,3},{3,2},{4,5},{5,4},{6,7},{7,6},{8,9},{9,8},{10,11... | collective-permute-start | bytes 2359304 | tf_op jit(solution)/shard_map/ppermute | solution.py:643
  47.5 16.9 %copy-start.4 = (bf16[256,256]{1,0:T(8,128)(2,1)S(1)}, bf16[256,256]{1,0:T(8,128)(2,1)}, u32[]{:S(2)}) copy-start(bf16[256,256]{1,0:T(8,128)(2,1)} %get-tuple-element.41.so_ref.refs_1_) | copy-start | bytes 393220
  47.5 16.9 %copy-start.8 = (bf16[256,256]{1,0:T(8,128)(2,1)S(1)}, bf16[256,256]{1,0:T(8,128)(2,1)}, u32[]{:S(2)}) copy-start(bf16[256,256]{1,0:T(8,128)(2,1)} %wo_ref.3) | copy-start | bytes 393220
  47.5 16.9 %copy-start.10 = (bf16[512,256]{1,0:T(8,128)(2,1)S(1)}, bf16[512,256]{1,0:T(8,128)(2,1)}, u32[]{:S(2)}) copy-start(bf16[512,256]{1,0:T(8,128)(2,1)} %get-tuple-element.44.h_ref) | copy-start | bytes 786436
  47.5 16.9 %copy-start.11 = (bf16[512,256]{1,0:T(8,128)(2,1)S(1)}, bf16[512,256]{1,0:T(8,128)(2,1)}, u32[]{:S(2)}) copy-start(bf16[512,256]{1,0:T(8,128)(2,1)} %get-tuple-element.42.o_ref) | copy-start | bytes 786436
  47.5 16.9 %copy-start.12 = (bf16[512,256]{1,0:T(8,128)(2,1)S(1)}, bf16[512,256]{1,0:T(8,128)(2,1)}, u32[]{:S(2)}) copy-start(bf16[512,256]{1,0:T(8,128)(2,1)} %get-tuple-element.43.od_ref) | copy-start | bytes 786436
  67.5 2.9 %collective-permute-start.1 = (bf16[512,256]{1,0:T(8,128)(2,1)S(1)}, bf16[512,256]{1,0:T(8,128)(2,1)S(1)}, u32[]{:S(2)}, u32[]{:S(2)}) collective-permute-start(bf16[512,256]{1,0:T(8,128)(2,1)S(1)} %get-tuple-element.46), channel_id=1, source_target_pairs={{0,1},{1,0},{2,3},{3,2},{4,5},{5,4},{6,7},{7,6},{8,9},{9,8},{10,11... | collective-permute-start | bytes 786440 | tf_op jit(solution)/shard_map/ppermute | solution.py:645
  92.5 25.0 %copy-start = (bf16[256,1024]{1,0:T(8,128)(2,1)S(1)}, bf16[256,1024]{1,0:T(8,128)(2,1)}, u32[]{:S(2)}) copy-start(bf16[256,1024]{1,0:T(8,128)(2,1)} %get-tuple-element.50.refs_4_) | copy-start | bytes 1572868
  92.5 25.0 %copy-start.1 = (bf16[1024,256]{1,0:T(8,128)(2,1)S(1)}, bf16[1024,256]{1,0:T(8,128)(2,1)}, u32[]{:S(2)}) copy-start(bf16[1024,256]{1,0:T(8,128)(2,1)} %get-tuple-element.51.refs_5_) | copy-start | bytes 1572868
  92.5 25.0 %copy-start.2 = (bf16[256,768]{1,0:T(8,128)(2,1)S(1)}, bf16[256,768]{1,0:T(8,128)(2,1)}, u32[]{:S(2)}) copy-start(bf16[256,768]{1,0:T(8,128)(2,1)} %get-tuple-element.47.refs_0_) | copy-start | bytes 1179652
  92.5 25.0 %copy-start.3 = (bf16[256,768]{1,0:T(8,128)(2,1)S(1)}, bf16[256,768]{1,0:T(8,128)(2,1)}, u32[]{:S(2)}) copy-start(bf16[256,768]{1,0:T(8,128)(2,1)} %get-tuple-element.48.refs_2_) | copy-start | bytes 1179652
  92.5 25.0 %copy-start.5 = (bf16[256,256]{1,0:T(8,128)(2,1)S(1)}, bf16[256,256]{1,0:T(8,128)(2,1)}, u32[]{:S(2)}) copy-start(bf16[256,256]{1,0:T(8,128)(2,1)} %get-tuple-element.49.refs_3_) | copy-start | bytes 393220
  114.5 5.3 %collective-permute-start.2 = (bf16[2048,256]{1,0:T(8,128)(2,1)S(1)}, bf16[2048,256]{1,0:T(8,128)(2,1)S(1)}, u32[]{:S(2)}, u32[]{:S(2)}) collective-permute-start(bf16[2048,256]{1,0:T(8,128)(2,1)S(1)} %bitcast.4), channel_id=1, source_target_pairs={{0,1},{1,0},{2,3},{3,2},{4,5},{5,4},{6,7},{7,6},{8,9},{9,8},{10,11... | collective-permute-start | bytes 3145736 | tf_op jit(solution)/shard_map/ppermute | solution.py:668

commit v5 on v4

--- a/solution.py
+++ b/solution.py
@@ -17,7 +17,7 @@
 SCALE = HD ** (-0.5)
 GELU_K = math.sqrt(2.0 / math.pi)
 GELU_C = 0.044715
-PEERS = ("y_lo", "x", "z", "y_hi")
+PEERS = ("x", "z", "y_hi", "y_lo")
 
 
 def nn(a, b):
@@ -130,6 +130,12 @@
 
 def twice(values, dots):
     return rows(lanes(values, jnp.zeros_like(values)), lanes(dots, values))
+
+
+def stacked(values, dots, weight, weight_dot):
+    both = nn(rows(values, dots), lanes(weight, weight_dot))
+    width = weight.shape[1]
+    return both[:WINDOW, :width], both[WINDOW:, :width] + both[:WINDOW, width:]
 
 
 def segment_sums(values, ones):
@@ -162,9 +168,9 @@
             vb = spread(heads_of(qkv_ref, at, 2, g), mask)
             vdb = spread(heads_of(qkvd_ref, at, 2, g), mask)
             here = pl.ds(GROUP * g, GROUP)
-            both = nn(twice(a, ad), rows(vb, vdb)).astype(BF16)
-            o_ref[at, here] = both[:WINDOW]
-            od_ref[at, here] = both[WINDOW:]
+            o, od = stacked(a, ad, vb, vdb)
+            o_ref[at, here] = o.astype(BF16)
+            od_ref[at, here] = od.astype(BF16)
 
     per_batch(qkv_ref.shape[0] // WINDOW, step)
 
@@ -203,14 +209,13 @@
             do, dod = do_ref[at, here], dod_ref[at, here]
             q, qd = qkv_ref[at, qs], qkvd_ref[at, qs]
             kb, kdb = spread(qkv_ref[at, ks], mask), spread(qkvd_ref[at, ks], mask)
+            dq, dqd = stacked(ds, dsd, kb, kdb)
+            dqkvd_ref[at, qs] = dqd.astype(BF16)
             if dqkv_ref is None:
-                dqkvd_ref[at, qs] = nn(lanes(dsd, ds), rows(kb, kdb)).astype(BF16)
                 dqkvd_ref[at, ks] = collect(tn(rows(dsd, ds), rows(q, qd))).astype(BF16)
                 dqkvd_ref[at, vs] = collect(tn(rows(adb, ab), rows(do, dod))).astype(BF16)
             else:
-                both = nn(twice(ds, dsd), rows(kb, kdb)).astype(BF16)
-                dqkv_ref[at, qs] = both[:WINDOW]
-                dqkvd_ref[at, qs] = both[WINDOW:]
+                dqkv_ref[at, qs] = dq.astype(BF16)
                 both = tn(rows(dsd, ds), twice(q, qd))
                 dqkvd_ref[at, ks] = collect(both[:, :GROUP]).astype(BF16)
                 dqkv_ref[at, ks] = collect(both[:, GROUP:]).astype(BF16)
@@ -335,17 +340,15 @@
             du = nt(t, wf_ref[cols, :])
             dud = nt(t, sf_ref[cols, :])
             square = z * z
-            bend = jnp.tanh(z * (GELU_K + GELU_K * GELU_C * square))
-            inner = GELU_K + (3.0 * GELU_K * GELU_C) * square
-            flat = (1.0 - bend * bend) * inner
-            half = 0.5 * z
-            slope1 = 0.5 + 0.5 * bend + half * flat
-            slope2 = flat * (1.0 - z * bend * inner) + (1.0 - bend * bend) * (
-                3.0 * GELU_K * GELU_C
-            ) * square
+            cubic = (GELU_K * GELU_C) * square
+            bend = jnp.tanh(z * (GELU_K + cubic))
+            inner = GELU_K + 3.0 * cubic
+            level = 1.0 - bend * bend
+            slope1 = 0.5 * (1.0 + bend + (z * inner) * level)
+            slope2 = level * (GELU_K + 6.0 * cubic - (z * bend) * (inner * inner))
             ud_ref[at, cols] = (slope1 * zd).astype(BF16)
             dz = (du * slope1).astype(BF16)
-            dzd = (dud * slope1 + du * slope2 * zd).astype(BF16)
+            dzd = (dud * slope1 + (du * zd) * slope2).astype(BF16)
             dz_ref[at, cols] = dz
             dz_ref[low, cols] = dzd
             dh = dh + nt(dz, wi)
@@ -456,10 +459,9 @@
 
 
 def write_half(who, half_ref, sign_refs, out_hbms, wide_refs, sems):
-    copies, sums = [], []
-    for n, (base, sign_ref, out_hbm, wide_ref) in enumerate(
-        zip(PLACES, sign_refs, out_hbms, wide_refs)
-    ):
+    copies, sums = [], {}
+    for n in (4, 5, 0, 2, 1, 3):
+        base, sign_ref, out_hbm, wide_ref = PLACES[n], sign_refs[n], out_hbms[n], wide_refs[n]
         height, width = out_hbm.shape
         across = width // 256
         total = jnp.zeros((8, 256), F32)
@@ -479,10 +481,10 @@
                 )
             )
             copies[-1].start()
-        sums.append(jnp.sum(total, axis=0, keepdims=True))
+        sums[n] = jnp.sum(total, axis=0, keepdims=True)
     for copy in copies:
         copy.wait()
-    return rows(*sums, jnp.zeros((2, 256), F32))
+    return rows(*[sums[n] for n in range(6)], jnp.zeros((2, 256), F32))
 
 
 def finish_mine_kernel(core_ref, half_ref, *refs):

time: 122 us -> 122 us (level)
  no operation moved by 1% of the time
where the time goes in v5:
time: 122 us; the launch traced here: 121 us
  blocking collectives  85.8 us (70%)
  Pallas kernels  24.2 us (20%)
  starting transfers between devices  8.27 us (7%)
  waiting for transfers between devices  1.96 us (2%)
    all_to_all x4, blocking collectives, exchange(): return lax.all_to_all(values, PEERS, 0, 0, tiled=True)  85.8 us
    pallas_call x7, Pallas kernels, call(): pl.pallas_call(kernel, out_shape=[pltpu.HBM(out.shape, out.dtype) if spac...  24.2 us
    ppermute x1, starting transfers between devices, body(): other = lax.ppermute(mine, 'core', swap)  3.28 us
    ppermute x1, starting transfers between devices, body(): mid_got = lax.ppermute(mid_send, 'core', swap)  3.04 us
  transfers between devices with their start and end apart: 3, of which 2 were waited for; matrix products, arithmetic and copies ran while one was open for 0% of the time, Pallas kernels for 4%

profile of v5, /device:TPU:1, one launch (start us, length us, event | category | flops | bytes accessed | tf_op | source)
XLA Modules:
  0.0 121.3 jit_solution(1875892712566118877)
XLA Ops:
  0.6 0.0 copy-start.14
  0.6 0.0 copy-start.15
  0.7 0.0 copy-start.16
  0.7 0.0 copy-start.17
  0.7 4.4 %block_forward.1 = (bf16[64,16,384]{2,1,0:T(8,128)(2,1)S(1)}, bf16[512,768]{1,0:T(8,128)(2,1)S(1)}, bf16[512,768]{1,0:T(8,128)(2,1)S(1)}, bf16[512,512]{1,0:T(8,...) custom-call(s32[1]{0:T(128)} %bitcast.core_ref, ...), custom_call_target="tpu_custom_call" | custom-call | tf_op jit(solution)/shard_map/block_forward/pallas_call | solution.py:517
  5.0 0.0 copy-start.6
  5.1 0.0 copy-start.7
  5.1 0.0 copy-start.9
  5.1 0.0 copy-start.13
  5.1 26.0 %all_to_all.20.pack_ref = bf16[64,16,384]{2,1,0:T(8,128)(2,1)S(1)} all-to-all(bf16[64,16,384]{2,1,0:T(8,128)(2,1)S(1)} %get-tuple-element.33), channel_id=1, replica_groups=mesh['y_lo'=2,'x'=4,'z'=4,'y_hi'=2,'core'=2] {'x','z','y_hi','y_lo'}, dimensions={0} | all-to-all | bytes 1572864 | tf_op jit(solution)/shard_map/all_to_all | solution.py:635
  31.1 0.0 copy-done.14
  31.1 0.0 copy-done.15
  31.1 0.0 copy-done.16
  31.1 0.0 copy-done.17
  31.1 0.0 copy-done.6
  31.1 0.0 copy-done.7
  31.1 0.0 copy-done.9
  31.1 0.0 copy-done.13
  31.1 12.6 %middle.1 = (bf16[64,16,256]{2,1,0:T(8,128)(2,1)S(1)}, bf16[1536,256]{1,0:T(8,128)(2,1)S(1)}, bf16[1536,256]{1,0:T(8,128)(2,1)S(1)}, bf16[256,768]{1,0:T(8,128)(...) custom-call(s32[1]{0:T(128)} %bitcast.core_ref, ...), custom_call_target="tpu_custom_call" | custom-call | tf_op jit(solution)/shard_map/middle/pallas_call | solution.py:517
  43.8 3.0 %collective-permute-start = (bf16[1536,256]{1,0:T(8,128)(2,1)S(1)}, bf16[1536,256]{1,0:T(8,128)(2,1)S(1)}, u32[]{:S(2)}, u32[]{:S(2)}) collective-permute-start(bf16[1536,256]{1,0:T(8,128)(2,1)S(1)} %get-tuple-element.35), channel_id=1, source_target_pairs={{0,1},{1,0},{2,3},{3,2},{4,5},{5,4},{6,7},{7,6},{8,9},{9,8},{10,11... | collective-permute-start | bytes 2359304 | tf_op jit(solution)/shard_map/ppermute | solution.py:645
  46.8 0.0 copy-start.4
  46.8 0.0 copy-start.8
  46.8 0.0 copy-start.10
  46.8 0.0 copy-start.11
  46.8 0.0 copy-start.12
  46.8 16.6 %all_to_all.21.back_ref = bf16[64,16,256]{2,1,0:T(8,128)(2,1)S(1)} all-to-all(bf16[64,16,256]{2,1,0:T(8,128)(2,1)S(1)} %get-tuple-element.36), channel_id=1, replica_groups=mesh['y_lo'=2,'x'=4,'z'=4,'y_hi'=2,'core'=2] {'x','z','y_hi','y_lo'}, dimensions={0} | all-to-all | bytes 1048576 | tf_op jit(solution)/shard_map/all_to_all | solution.py:635
  63.4 0.0 copy-done.4
  63.4 0.0 copy-done.8
  63.4 0.0 copy-done.10
  63.4 0.0 copy-done.11
  63.4 0.0 copy-done.12
  63.5 3.1 %block_back.1 = (bf16[512,256]{1,0:T(8,128)(2,1)S(1)}, bf16[512,256]{1,0:T(8,128)(2,1)S(1)}) custom-call(s32[1]{0:T(128)} %bitcast.core_ref, bf16[64,16,256]{2,1,0:T(8,128)(2,1)S(1)} %all_to_all.21.back_ref, bf16[512,768]{1,0:T(8,128)(2,1)S(1)} %get-tuple-element.37.qkv_ref, bf16[512,768]{1,0:T(8,128)(2,1)S(1)} %get-tuple-element.38.qkvd_ref, ...), custom_call_target="tpu_custom_call" | custom-call | tf_op jit(solution)/shard_map/block_back/pallas_call | solution.py:517
  66.6 2.0 %collective-permute-start.1 = (bf16[512,256]{1,0:T(8,128)(2,1)S(1)}, bf16[512,256]{1,0:T(8,128)(2,1)S(1)}, u32[]{:S(2)}, u32[]{:S(2)}) collective-permute-start(bf16[512,256]{1,0:T(8,128)(2,1)S(1)} %get-tuple-element.46), channel_id=1, source_target_pairs={{0,1},{1,0},{2,3},{3,2},{4,5},{5,4},{6,7},{7,6},{8,9},{9,8},{10,11... | collective-permute-start | bytes 786440 | tf_op jit(solution)/shard_map/ppermute | solution.py:647
  68.6 1.2 collective-permute-done.1.got_ref
  69.7 0.0 collective-permute-done.mid_got_ref
  69.7 0.2 pair_sum.1
  70.0 21.5 %all_to_all.22.parts_ref = bf16[64,32,256]{2,1,0:T(8,128)(2,1)S(1)} all-to-all(bf16[64,32,256]{2,1,0:T(8,128)(2,1)S(1)} %bitcast.3), channel_id=1, replica_groups=mesh['y_lo'=2,'x'=4,'z'=4,'y_hi'=2,'core'=2] {'x','z','y_hi','y_lo'}, dimensions={0} | all-to-all | bytes 2097152 | tf_op jit(solution)/shard_map/all_to_all | solution.py:635
  91.4 0.2 peer_sum.1
  91.7 0.0 copy-start
  91.7 0.0 copy-start.1
  91.7 0.0 copy-start.2
  91.7 0.0 copy-start.3
  91.7 0.0 copy-start.5
  91.7 21.8 %all_to_all.23 = bf16[64,32,256]{2,1,0:T(8,128)(2,1)S(1)} all-to-all(bf16[64,32,256]{2,1,0:T(8,128)(2,1)S(1)} %peer_sum.1), channel_id=1, replica_groups=mesh['y_lo'=2,'x'=4,'z'=4,'y_hi'=2,'core'=2] {'x','z','y_hi','y_lo'}, dimensions={0} | all-to-all | bytes 2097152 | tf_op jit(solution)/shard_map/all_to_all | solution.py:635
  113.5 3.3 %collective-permute-start.2 = (bf16[2048,256]{1,0:T(8,128)(2,1)S(1)}, bf16[2048,256]{1,0:T(8,128)(2,1)S(1)}, u32[]{:S(2)}, u32[]{:S(2)}) collective-permute-start(bf16[2048,256]{1,0:T(8,128)(2,1)S(1)} %bitcast.4), channel_id=1, source_target_pairs={{0,1},{1,0},{2,3},{3,2},{4,5},{5,4},{6,7},{7,6},{8,9},{9,8},{10,11... | collective-permute-start | bytes 3145736 | tf_op jit(solution)/shard_map/ppermute | solution.py:670
  116.8 0.0 copy-done
  116.8 0.0 copy-done.1
  116.8 0.0 copy-done.2
  116.8 0.0 copy-done.3
  116.8 0.0 copy-done.5
  116.8 1.5 %finish_mine.1 = (f32[256,768]{1,0:T(8,128)}, f32[256,256]{1,0:T(8,128)}, f32[256,768]{1,0:T(8,128)}, f32[256,256]{1,0:T(8,128)}, f32[256,1024]{1,0:T(8,128)}, /...) custom-call(s32[1]{0:T(128)} %bitcast.core_ref, bf16[2048,256]{1,0:T(8,128)(2,1)S(1)} %bitcast.5, ...), custom_call_target="tpu_custom_call" | custom-call | tf_op jit(solution)/shard_map/finish_mine/pallas_call | solution.py:517
  118.3 0.8 collective-permute-done.2.half_ref
  119.1 2.1 %finish_other.1 = (f32[256,768]{1,0:T(8,128)}, f32[256,256]{1,0:T(8,128)}, f32[256,768]{1,0:T(8,128)}, f32[256,256]{1,0:T(8,128)}, f32[256,1024]{1,0:T(8,128)}, /*index=5*/f32[1024,256]{1,0:T(8,128)}, f32[6]{0:T(128)}) custom-call(s32[1]{0:T(128)} %bitcast.core_ref, ...), custom_call_target="tpu_custom_call", output_to_operand_aliasing={{0}: (9, {}), {1}: (10, {}), {2}: (11, {}), {3}: (12, {}), ... | custom-call | tf_op jit(solution)/shard_map/finish_other/pallas_call | solution.py:517
Async XLA Ops:
  0.6 30.4 %copy-start.14 = (s32[9,1024]{1,0:T(8,128)S(1)}, s32[9,1024]{1,0:T(8,128)}, u32[]{:S(2)}) copy-start(s32[9,1024]{1,0:T(8,128)} %pi_ref.1) | copy-start | bytes 110596
  0.6 30.4 %copy-start.15 = (s32[9,768]{1,0:T(8,128)S(1)}, s32[9,768]{1,0:T(8,128)}, u32[]{:S(2)}) copy-start(s32[9,768]{1,0:T(8,128)} %pq_ref.1) | copy-start | bytes 82948
  0.7 30.4 %copy-start.16 = (s32[35,256]{1,0:T(8,128)S(1)}, s32[35,256]{1,0:T(8,128)}, u32[]{:S(2)}) copy-start(s32[35,256]{1,0:T(8,128)} %pf_ref.1) | copy-start | bytes 107524
  0.7 30.4 %copy-start.17 = (s32[9,256]{1,0:T(8,128)S(1)}, s32[9,256]{1,0:T(8,128)}, u32[]{:S(2)}) copy-start(s32[9,256]{1,0:T(8,128)} %po_ref.1) | copy-start | bytes 27652
  5.0 26.0 %copy-start.6 = (bf16[256,1024]{1,0:T(8,128)(2,1)S(1)}, bf16[256,1024]{1,0:T(8,128)(2,1)}, u32[]{:S(2)}) copy-start(bf16[256,1024]{1,0:T(8,128)(2,1)} %wi_ref.1) | copy-start | bytes 1572868
  5.1 26.0 %copy-start.7 = (bf16[1024,256]{1,0:T(8,128)(2,1)S(1)}, bf16[1024,256]{1,0:T(8,128)(2,1)}, u32[]{:S(2)}) copy-start(bf16[1024,256]{1,0:T(8,128)(2,1)} %wf_ref.1) | copy-start | bytes 1572868
  5.1 26.0 %copy-start.9 = (bf16[256,768]{1,0:T(8,128)(2,1)S(1)}, bf16[256,768]{1,0:T(8,128)(2,1)}, u32[]{:S(2)}) copy-start(bf16[256,768]{1,0:T(8,128)(2,1)} %wq_ref.1) | copy-start | bytes 1179652
  5.1 26.0 %copy-start.13 = (bf16[256,256]{1,0:T(8,128)(2,1)S(1)}, bf16[256,256]{1,0:T(8,128)(2,1)}, u32[]{:S(2)}) copy-start(bf16[256,256]{1,0:T(8,128)(2,1)} %wo_ref.2) | copy-start | bytes 393220
  43.8 26.0 %collective-permute-start = (bf16[1536,256]{1,0:T(8,128)(2,1)S(1)}, bf16[1536,256]{1,0:T(8,128)(2,1)S(1)}, u32[]{:S(2)}, u32[]{:S(2)}) collective-permute-start(bf16[1536,256]{1,0:T(8,128)(2,1)S(1)} %get-tuple-element.35), channel_id=1, source_target_pairs={{0,1},{1,0},{2,3},{3,2},{4,5},{5,4},{6,7},{7,6},{8,9},{9,8},{10,11... | collective-permute-start | bytes 2359304 | tf_op jit(solution)/shard_map/ppermute | solution.py:645
  46.8 16.6 %copy-start.4 = (bf16[256,256]{1,0:T(8,128)(2,1)S(1)}, bf16[256,256]{1,0:T(8,128)(2,1)}, u32[]{:S(2)}) copy-start(bf16[256,256]{1,0:T(8,128)(2,1)} %get-tuple-element.41.so_ref.refs_1_) | copy-start | bytes 393220
  46.8 16.6 %copy-start.8 = (bf16[256,256]{1,0:T(8,128)(2,1)S(1)}, bf16[256,256]{1,0:T(8,128)(2,1)}, u32[]{:S(2)}) copy-start(bf16[256,256]{1,0:T(8,128)(2,1)} %wo_ref.3) | copy-start | bytes 393220
  46.8 16.6 %copy-start.10 = (bf16[512,256]{1,0:T(8,128)(2,1)S(1)}, bf16[512,256]{1,0:T(8,128)(2,1)}, u32[]{:S(2)}) copy-start(bf16[512,256]{1,0:T(8,128)(2,1)} %get-tuple-element.44.h_ref) | copy-start | bytes 786436
  46.8 16.6 %copy-start.11 = (bf16[512,256]{1,0:T(8,128)(2,1)S(1)}, bf16[512,256]{1,0:T(8,128)(2,1)}, u32[]{:S(2)}) copy-start(bf16[512,256]{1,0:T(8,128)(2,1)} %get-tuple-element.42.o_ref) | copy-start | bytes 786436
  46.8 16.6 %copy-start.12 = (bf16[512,256]{1,0:T(8,128)(2,1)S(1)}, bf16[512,256]{1,0:T(8,128)(2,1)}, u32[]{:S(2)}) copy-start(bf16[512,256]{1,0:T(8,128)(2,1)} %get-tuple-element.43.od_ref) | copy-start | bytes 786436
  66.6 3.1 %collective-permute-start.1 = (bf16[512,256]{1,0:T(8,128)(2,1)S(1)}, bf16[512,256]{1,0:T(8,128)(2,1)S(1)}, u32[]{:S(2)}, u32[]{:S(2)}) collective-permute-start(bf16[512,256]{1,0:T(8,128)(2,1)S(1)} %get-tuple-element.46), channel_id=1, source_target_pairs={{0,1},{1,0},{2,3},{3,2},{4,5},{5,4},{6,7},{7,6},{8,9},{9,8},{10,11... | collective-permute-start | bytes 786440 | tf_op jit(solution)/shard_map/ppermute | solution.py:647
  91.7 25.1 %copy-start = (bf16[256,1024]{1,0:T(8,128)(2,1)S(1)}, bf16[256,1024]{1,0:T(8,128)(2,1)}, u32[]{:S(2)}) copy-start(bf16[256,1024]{1,0:T(8,128)(2,1)} %get-tuple-element.50.refs_4_) | copy-start | bytes 1572868
  91.7 25.1 %copy-start.1 = (bf16[1024,256]{1,0:T(8,128)(2,1)S(1)}, bf16[1024,256]{1,0:T(8,128)(2,1)}, u32[]{:S(2)}) copy-start(bf16[1024,256]{1,0:T(8,128)(2,1)} %get-tuple-element.51.refs_5_) | copy-start | bytes 1572868
  91.7 25.1 %copy-start.2 = (bf16[256,768]{1,0:T(8,128)(2,1)S(1)}, bf16[256,768]{1,0:T(8,128)(2,1)}, u32[]{:S(2)}) copy-start(bf16[256,768]{1,0:T(8,128)(2,1)} %get-tuple-element.47.refs_0_) | copy-start | bytes 1179652
  91.7 25.1 %copy-start.3 = (bf16[256,768]{1,0:T(8,128)(2,1)S(1)}, bf16[256,768]{1,0:T(8,128)(2,1)}, u32[]{:S(2)}) copy-start(bf16[256,768]{1,0:T(8,128)(2,1)} %get-tuple-element.48.refs_2_) | copy-start | bytes 1179652
  91.7 25.1 %copy-start.5 = (bf16[256,256]{1,0:T(8,128)(2,1)S(1)}, bf16[256,256]{1,0:T(8,128)(2,1)}, u32[]{:S(2)}) copy-start(bf16[256,256]{1,0:T(8,128)(2,1)} %get-tuple-element.49.refs_3_) | copy-start | bytes 393220
  113.5 5.6 %collective-permute-start.2 = (bf16[2048,256]{1,0:T(8,128)(2,1)S(1)}, bf16[2048,256]{1,0:T(8,128)(2,1)S(1)}, u32[]{:S(2)}, u32[]{:S(2)}) collective-permute-start(bf16[2048,256]{1,0:T(8,128)(2,1)S(1)} %bitcast.4), channel_id=1, source_target_pairs={{0,1},{1,0},{2,3},{3,2},{4,5},{5,4},{6,7},{7,6},{8,9},{9,8},{10,11... | collective-permute-start | bytes 3145736 | tf_op jit(solution)/shard_map/ppermute | solution.py:670

commit v6 on v5

--- a/solution.py
+++ b/solution.py
@@ -441,9 +441,19 @@
 
 
 def pair_sum_kernel(mid_keep_ref, mid_got_ref, keep_ref, got_ref, out_ref):
-    count = mid_keep_ref.shape[0]
-    out_ref[0:count, :] = (mid_keep_ref[...].astype(F32) + mid_got_ref[...].astype(F32)).astype(BF16)
-    out_ref[count:, :] = (keep_ref[...].astype(F32) + got_ref[...].astype(F32)).astype(BF16)
+    peers, height, _ = out_ref.shape
+
+    def put(first, keep, got):
+        total = (keep.astype(F32) + got.astype(F32)).astype(BF16)
+        side, place = first // 1024, first % 1024 // height
+        count = total.shape[0] // height
+        out_ref[place : place + count, :, 256 * side : 256 * side + 256] = total.reshape(
+            count, height, 256
+        )
+
+    put(0, mid_keep_ref[0:1024, :], mid_got_ref[0:1024, :])
+    put(1024, mid_keep_ref[1024:1536, :], mid_got_ref[1024:1536, :])
+    put(1536, keep_ref[...], got_ref[...])
 
 
 def peer_sum_kernel(parts_ref, out_ref):
@@ -469,7 +479,9 @@
             cols = pl.ds(256 * (block % across), 256)
             down = block // across
             at = pl.ds(pl.multiple_of(256 * down + who * 128, 128), 128)
-            value = half_ref[128 * (base + block) : 128 * (base + block) + 128, :].astype(F32)
+            spot = pl.ds(128 * ((base + block) % 8), 128)
+            side = pl.ds(256 * ((base + block) // 8), 256)
+            value = half_ref[spot, side].astype(F32)
             wide_ref[128 * down : 128 * down + 128, cols] = value
             signed = value * sign_ref[at, cols].astype(F32)
             total = total + jnp.sum(signed.reshape(16, 8, 256), axis=0)
@@ -647,7 +659,7 @@
     got = lax.ppermute(send, "core", swap)
     (parts,) = call(
         pair_sum_kernel,
-        [shaped(BF16, 2048, 256)],
+        [shaped(BF16, peers, 1024 // peers, 512)],
         "v",
         [],
         (mid_keep, mid_got, keep, got),
@@ -655,10 +667,10 @@
         "pair_sum",
         8,
     )
-    parts = exchange(parts.reshape(peers, 2048 // peers, 256))
+    parts = exchange(parts)
     (copies,) = call(
         peer_sum_kernel,
-        [shaped(BF16, peers, 2048 // peers, 256)],
+        [shaped(BF16, peers, 1024 // peers, 512)],
         "v",
         [],
         (parts,),
@@ -666,7 +678,7 @@
         "peer_sum",
         8,
     )
-    mine = exchange(copies).reshape(2048, 256)
+    mine = exchange(copies).reshape(1024, 512)
     other = lax.ppermute(mine, "core", swap)
     weights = (block_qkv, block_out, grid_qkv, grid_out, mlp_in, mlp_out)
     signs = (*saved[7:9], *signs)

time: 122 us -> 122 us (level)
  no operation moved by 1% of the time
where the time goes in v6:
time: 122 us; the launch traced here: 121 us
  blocking collectives  85.8 us (70%)
  Pallas kernels  24.2 us (20%)
  starting transfers between devices  8.27 us (7%)
  waiting for transfers between devices  1.96 us (2%)
    all_to_all x4, blocking collectives, exchange(): return lax.all_to_all(values, PEERS, 0, 0, tiled=True)  85.8 us
    pallas_call x7, Pallas kernels, call(): pl.pallas_call(kernel, out_shape=[pltpu.HBM(out.shape, out.dtype) if spac...  24.2 us
    ppermute x1, starting transfers between devices, body(): other = lax.ppermute(mine, 'core', swap)  3.28 us
    ppermute x1, starting transfers between devices, body(): mid_got = lax.ppermute(mid_send, 'core', swap)  3.04 us
  transfers between devices with their start and end apart: 3, of which 2 were waited for; matrix products, arithmetic and copies ran while one was open for 0% of the time, Pallas kernels for 4%

profile of v6, /device:TPU:1, one launch (start us, length us, event | category | flops | bytes accessed | tf_op | source)
XLA Modules:
  0.0 121.3 jit_solution(12446513573312587746)
XLA Ops:
  0.6 0.0 copy-start.14
  0.6 0.0 copy-start.15
  0.7 0.0 copy-start.16
  0.7 0.0 copy-start.17
  0.7 4.4 %block_forward.1 = (bf16[64,16,384]{2,1,0:T(8,128)(2,1)S(1)}, bf16[512,768]{1,0:T(8,128)(2,1)S(1)}, bf16[512,768]{1,0:T(8,128)(2,1)S(1)}, bf16[512,512]{1,0:T(8,...) custom-call(s32[1]{0:T(128)} %bitcast.core_ref, ...), custom_call_target="tpu_custom_call" | custom-call | tf_op jit(solution)/shard_map/block_forward/pallas_call | solution.py:529
  5.0 0.0 copy-start.6
  5.1 0.0 copy-start.7
  5.1 0.0 copy-start.9
  5.1 0.0 copy-start.13
  5.1 26.0 %all_to_all.20.pack_ref = bf16[64,16,384]{2,1,0:T(8,128)(2,1)S(1)} all-to-all(bf16[64,16,384]{2,1,0:T(8,128)(2,1)S(1)} %get-tuple-element.33), channel_id=1, replica_groups=mesh['y_lo'=2,'x'=4,'z'=4,'y_hi'=2,'core'=2] {'x','z','y_hi','y_lo'}, dimensions={0} | all-to-all | bytes 1572864 | tf_op jit(solution)/shard_map/all_to_all | solution.py:647
  31.1 0.0 copy-done.14
  31.1 0.0 copy-done.15
  31.1 0.0 copy-done.16
  31.1 0.0 copy-done.17
  31.1 0.0 copy-done.6
  31.1 0.0 copy-done.7
  31.1 0.0 copy-done.9
  31.1 0.0 copy-done.13
  31.1 12.6 %middle.1 = (bf16[64,16,256]{2,1,0:T(8,128)(2,1)S(1)}, bf16[1536,256]{1,0:T(8,128)(2,1)S(1)}, bf16[1536,256]{1,0:T(8,128)(2,1)S(1)}, bf16[256,768]{1,0:T(8,128)(...) custom-call(s32[1]{0:T(128)} %bitcast.core_ref, ...), custom_call_target="tpu_custom_call" | custom-call | tf_op jit(solution)/shard_map/middle/pallas_call | solution.py:529
  43.8 3.0 %collective-permute-start = (bf16[1536,256]{1,0:T(8,128)(2,1)S(1)}, bf16[1536,256]{1,0:T(8,128)(2,1)S(1)}, u32[]{:S(2)}, u32[]{:S(2)}) collective-permute-start(bf16[1536,256]{1,0:T(8,128)(2,1)S(1)} %get-tuple-element.35), channel_id=1, source_target_pairs={{0,1},{1,0},{2,3},{3,2},{4,5},{5,4},{6,7},{7,6},{8,9},{9,8},{10,11... | collective-permute-start | bytes 2359304 | tf_op jit(solution)/shard_map/ppermute | solution.py:657
  46.8 0.0 copy-start.4
  46.8 0.0 copy-start.8
  46.8 0.0 copy-start.10
  46.8 0.0 copy-start.11
  46.8 0.0 copy-start.12
  46.8 16.6 %all_to_all.21.back_ref = bf16[64,16,256]{2,1,0:T(8,128)(2,1)S(1)} all-to-all(bf16[64,16,256]{2,1,0:T(8,128)(2,1)S(1)} %get-tuple-element.36), channel_id=1, replica_groups=mesh['y_lo'=2,'x'=4,'z'=4,'y_hi'=2,'core'=2] {'x','z','y_hi','y_lo'}, dimensions={0} | all-to-all | bytes 1048576 | tf_op jit(solution)/shard_map/all_to_all | solution.py:647
  63.4 0.0 copy-done.4
  63.4 0.0 copy-done.8
  63.4 0.0 copy-done.10
  63.4 0.0 copy-done.11
  63.4 0.0 copy-done.12
  63.5 3.1 %block_back.1 = (bf16[512,256]{1,0:T(8,128)(2,1)S(1)}, bf16[512,256]{1,0:T(8,128)(2,1)S(1)}) custom-call(s32[1]{0:T(128)} %bitcast.core_ref, bf16[64,16,256]{2,1,0:T(8,128)(2,1)S(1)} %all_to_all.21.back_ref, bf16[512,768]{1,0:T(8,128)(2,1)S(1)} %get-tuple-element.37.qkv_ref, bf16[512,768]{1,0:T(8,128)(2,1)S(1)} %get-tuple-element.38.qkvd_ref, ...), custom_call_target="tpu_custom_call" | custom-call | tf_op jit(solution)/shard_map/block_back/pallas_call | solution.py:529
  66.6 2.0 %collective-permute-start.1 = (bf16[512,256]{1,0:T(8,128)(2,1)S(1)}, bf16[512,256]{1,0:T(8,128)(2,1)S(1)}, u32[]{:S(2)}, u32[]{:S(2)}) collective-permute-start(bf16[512,256]{1,0:T(8,128)(2,1)S(1)} %get-tuple-element.46), channel_id=1, source_target_pairs={{0,1},{1,0},{2,3},{3,2},{4,5},{5,4},{6,7},{7,6},{8,9},{9,8},{10,11... | collective-permute-start | bytes 786440 | tf_op jit(solution)/shard_map/ppermute | solution.py:659
  68.6 1.2 collective-permute-done.1.got_ref
  69.7 0.0 collective-permute-done.mid_got_ref
  69.7 0.2 pair_sum.1
  70.0 21.5 %all_to_all.22.parts_ref = bf16[64,16,512]{2,1,0:T(8,128)(2,1)S(1)} all-to-all(bf16[64,16,512]{2,1,0:T(8,128)(2,1)S(1)} %pair_sum.1), channel_id=1, replica_groups=mesh['y_lo'=2,'x'=4,'z'=4,'y_hi'=2,'core'=2] {'x','z','y_hi','y_lo'}, dimensions={0} | all-to-all | bytes 2097152 | tf_op jit(solution)/shard_map/all_to_all | solution.py:647
  91.4 0.2 peer_sum.1
  91.7 0.0 copy-start
  91.7 0.0 copy-start.1
  91.7 0.0 copy-start.2
  91.7 0.0 copy-start.3
  91.7 0.0 copy-start.5
  91.7 21.8 %all_to_all.23 = bf16[64,16,512]{2,1,0:T(8,128)(2,1)S(1)} all-to-all(bf16[64,16,512]{2,1,0:T(8,128)(2,1)S(1)} %peer_sum.1), channel_id=1, replica_groups=mesh['y_lo'=2,'x'=4,'z'=4,'y_hi'=2,'core'=2] {'x','z','y_hi','y_lo'}, dimensions={0} | all-to-all | bytes 2097152 | tf_op jit(solution)/shard_map/all_to_all | solution.py:647
  113.5 3.3 %collective-permute-start.2 = (bf16[1024,512]{1,0:T(8,128)(2,1)S(1)}, bf16[1024,512]{1,0:T(8,128)(2,1)S(1)}, u32[]{:S(2)}, u32[]{:S(2)}) collective-permute-start(bf16[1024,512]{1,0:T(8,128)(2,1)S(1)} %bitcast.2), channel_id=1, source_target_pairs={{0,1},{1,0},{2,3},{3,2},{4,5},{5,4},{6,7},{7,6},{8,9},{9,8},{10,11... | collective-permute-start | bytes 3145736 | tf_op jit(solution)/shard_map/ppermute | solution.py:682
  116.8 0.0 copy-done
  116.8 0.0 copy-done.1
  116.8 0.0 copy-done.2
  116.8 0.0 copy-done.3
  116.8 0.0 copy-done.5
  116.8 1.5 %finish_mine.1 = (f32[256,768]{1,0:T(8,128)}, f32[256,256]{1,0:T(8,128)}, f32[256,768]{1,0:T(8,128)}, f32[256,256]{1,0:T(8,128)}, f32[256,1024]{1,0:T(8,128)}, /...) custom-call(s32[1]{0:T(128)} %bitcast.core_ref, bf16[1024,512]{1,0:T(8,128)(2,1)S(1)} %bitcast.3, ...), custom_call_target="tpu_custom_call" | custom-call | tf_op jit(solution)/shard_map/finish_mine/pallas_call | solution.py:529
  118.3 0.8 collective-permute-done.2.half_ref
  119.1 2.1 %finish_other.1 = (f32[256,768]{1,0:T(8,128)}, f32[256,256]{1,0:T(8,128)}, f32[256,768]{1,0:T(8,128)}, f32[256,256]{1,0:T(8,128)}, f32[256,1024]{1,0:T(8,128)}, /*index=5*/f32[1024,256]{1,0:T(8,128)}, f32[6]{0:T(128)}) custom-call(s32[1]{0:T(128)} %bitcast.core_ref, ...), custom_call_target="tpu_custom_call", output_to_operand_aliasing={{0}: (9, {}), {1}: (10, {}), {2}: (11, {}), {3}: (12, {}), ... | custom-call | tf_op jit(solution)/shard_map/finish_other/pallas_call | solution.py:529
Async XLA Ops:
  0.6 30.4 %copy-start.14 = (s32[9,1024]{1,0:T(8,128)S(1)}, s32[9,1024]{1,0:T(8,128)}, u32[]{:S(2)}) copy-start(s32[9,1024]{1,0:T(8,128)} %pi_ref.1) | copy-start | bytes 110596
  0.6 30.4 %copy-start.15 = (s32[9,768]{1,0:T(8,128)S(1)}, s32[9,768]{1,0:T(8,128)}, u32[]{:S(2)}) copy-start(s32[9,768]{1,0:T(8,128)} %pq_ref.1) | copy-start | bytes 82948
  0.7 30.4 %copy-start.16 = (s32[35,256]{1,0:T(8,128)S(1)}, s32[35,256]{1,0:T(8,128)}, u32[]{:S(2)}) copy-start(s32[35,256]{1,0:T(8,128)} %pf_ref.1) | copy-start | bytes 107524
  0.7 30.4 %copy-start.17 = (s32[9,256]{1,0:T(8,128)S(1)}, s32[9,256]{1,0:T(8,128)}, u32[]{:S(2)}) copy-start(s32[9,256]{1,0:T(8,128)} %po_ref.1) | copy-start | bytes 27652
  5.0 26.0 %copy-start.6 = (bf16[256,1024]{1,0:T(8,128)(2,1)S(1)}, bf16[256,1024]{1,0:T(8,128)(2,1)}, u32[]{:S(2)}) copy-start(bf16[256,1024]{1,0:T(8,128)(2,1)} %wi_ref.1) | copy-start | bytes 1572868
  5.1 26.0 %copy-start.7 = (bf16[1024,256]{1,0:T(8,128)(2,1)S(1)}, bf16[1024,256]{1,0:T(8,128)(2,1)}, u32[]{:S(2)}) copy-start(bf16[1024,256]{1,0:T(8,128)(2,1)} %wf_ref.1) | copy-start | bytes 1572868
  5.1 26.0 %copy-start.9 = (bf16[256,768]{1,0:T(8,128)(2,1)S(1)}, bf16[256,768]{1,0:T(8,128)(2,1)}, u32[]{:S(2)}) copy-start(bf16[256,768]{1,0:T(8,128)(2,1)} %wq_ref.1) | copy-start | bytes 1179652
  5.1 26.0 %copy-start.13 = (bf16[256,256]{1,0:T(8,128)(2,1)S(1)}, bf16[256,256]{1,0:T(8,128)(2,1)}, u32[]{:S(2)}) copy-start(bf16[256,256]{1,0:T(8,128)(2,1)} %wo_ref.2) | copy-start | bytes 393220
  43.8 26.0 %collective-permute-start = (bf16[1536,256]{1,0:T(8,128)(2,1)S(1)}, bf16[1536,256]{1,0:T(8,128)(2,1)S(1)}, u32[]{:S(2)}, u32[]{:S(2)}) collective-permute-start(bf16[1536,256]{1,0:T(8,128)(2,1)S(1)} %get-tuple-element.35), channel_id=1, source_target_pairs={{0,1},{1,0},{2,3},{3,2},{4,5},{5,4},{6,7},{7,6},{8,9},{9,8},{10,11... | collective-permute-start | bytes 2359304 | tf_op jit(solution)/shard_map/ppermute | solution.py:657
  46.8 16.6 %copy-start.4 = (bf16[256,256]{1,0:T(8,128)(2,1)S(1)}, bf16[256,256]{1,0:T(8,128)(2,1)}, u32[]{:S(2)}) copy-start(bf16[256,256]{1,0:T(8,128)(2,1)} %get-tuple-element.41.so_ref.refs_1_) | copy-start | bytes 393220
  46.8 16.6 %copy-start.8 = (bf16[256,256]{1,0:T(8,128)(2,1)S(1)}, bf16[256,256]{1,0:T(8,128)(2,1)}, u32[]{:S(2)}) copy-start(bf16[256,256]{1,0:T(8,128)(2,1)} %wo_ref.3) | copy-start | bytes 393220
  46.8 16.6 %copy-start.10 = (bf16[512,256]{1,0:T(8,128)(2,1)S(1)}, bf16[512,256]{1,0:T(8,128)(2,1)}, u32[]{:S(2)}) copy-start(bf16[512,256]{1,0:T(8,128)(2,1)} %get-tuple-element.44.h_ref) | copy-start | bytes 786436
  46.8 16.6 %copy-start.11 = (bf16[512,256]{1,0:T(8,128)(2,1)S(1)}, bf16[512,256]{1,0:T(8,128)(2,1)}, u32[]{:S(2)}) copy-start(bf16[512,256]{1,0:T(8,128)(2,1)} %get-tuple-element.42.o_ref) | copy-start | bytes 786436
  46.8 16.6 %copy-start.12 = (bf16[512,256]{1,0:T(8,128)(2,1)S(1)}, bf16[512,256]{1,0:T(8,128)(2,1)}, u32[]{:S(2)}) copy-start(bf16[512,256]{1,0:T(8,128)(2,1)} %get-tuple-element.43.od_ref) | copy-start | bytes 786436
  66.6 3.1 %collective-permute-start.1 = (bf16[512,256]{1,0:T(8,128)(2,1)S(1)}, bf16[512,256]{1,0:T(8,128)(2,1)S(1)}, u32[]{:S(2)}, u32[]{:S(2)}) collective-permute-start(bf16[512,256]{1,0:T(8,128)(2,1)S(1)} %get-tuple-element.46), channel_id=1, source_target_pairs={{0,1},{1,0},{2,3},{3,2},{4,5},{5,4},{6,7},{7,6},{8,9},{9,8},{10,11... | collective-permute-start | bytes 786440 | tf_op jit(solution)/shard_map/ppermute | solution.py:659
  91.7 25.1 %copy-start = (bf16[256,1024]{1,0:T(8,128)(2,1)S(1)}, bf16[256,1024]{1,0:T(8,128)(2,1)}, u32[]{:S(2)}) copy-start(bf16[256,1024]{1,0:T(8,128)(2,1)} %get-tuple-element.50.refs_4_) | copy-start | bytes 1572868
  91.7 25.1 %copy-start.1 = (bf16[1024,256]{1,0:T(8,128)(2,1)S(1)}, bf16[1024,256]{1,0:T(8,128)(2,1)}, u32[]{:S(2)}) copy-start(bf16[1024,256]{1,0:T(8,128)(2,1)} %get-tuple-element.51.refs_5_) | copy-start | bytes 1572868
  91.7 25.1 %copy-start.2 = (bf16[256,768]{1,0:T(8,128)(2,1)S(1)}, bf16[256,768]{1,0:T(8,128)(2,1)}, u32[]{:S(2)}) copy-start(bf16[256,768]{1,0:T(8,128)(2,1)} %get-tuple-element.47.refs_0_) | copy-start | bytes 1179652
  91.7 25.1 %copy-start.3 = (bf16[256,768]{1,0:T(8,128)(2,1)S(1)}, bf16[256,768]{1,0:T(8,128)(2,1)}, u32[]{:S(2)}) copy-start(bf16[256,768]{1,0:T(8,128)(2,1)} %get-tuple-element.48.refs_2_) | copy-start | bytes 1179652
  91.7 25.1 %copy-start.5 = (bf16[256,256]{1,0:T(8,128)(2,1)S(1)}, bf16[256,256]{1,0:T(8,128)(2,1)}, u32[]{:S(2)}) copy-start(bf16[256,256]{1,0:T(8,128)(2,1)} %get-tuple-element.49.refs_3_) | copy-start | bytes 393220
  113.5 5.6 %collective-permute-start.2 = (bf16[1024,512]{1,0:T(8,128)(2,1)S(1)}, bf16[1024,512]{1,0:T(8,128)(2,1)S(1)}, u32[]{:S(2)}, u32[]{:S(2)}) collective-permute-start(bf16[1024,512]{1,0:T(8,128)(2,1)S(1)} %bitcast.2), channel_id=1, source_target_pairs={{0,1},{1,0},{2,3},{3,2},{4,5},{5,4},{6,7},{7,6},{8,9},{9,8},{10,11... | collective-permute-start | bytes 3145736 | tf_op jit(solution)/shard_map/ppermute | solution.py:682

commit v7 on v6

--- a/solution.py
+++ b/solution.py
@@ -654,8 +654,9 @@
         probe_mlp_in, mlp_in, probe_mlp_out, mlp_out,
     )
     back, mid_keep, mid_send, *signs = stage_middle(core, exchange(pack), factor, sources)
+    back, mid_send = lax.optimization_barrier((exchange(back), mid_send))
     mid_got = lax.ppermute(mid_send, "core", swap)
-    keep, send = stage_back(core, exchange(back), saved, block_out)
+    keep, send = stage_back(core, back, saved, block_out)
     got = lax.ppermute(send, "core", swap)
     (parts,) = call(
         pair_sum_kernel,

time: 122 us -> 120 us (0.984)
  starting transfers between devices: 8.27 us -> 6.67 us
    ppermute x1, starting transfers between devices: 1.96 us -> 0.1 us  [body(): got = lax.ppermute(send, 'core', swap)]
where the time goes in v7:
time: 120 us
  blocking collectives  85.6 us (71%)
  Pallas kernels  24.2 us (20%)
  starting transfers between devices  6.67 us (6%)
  waiting for transfers between devices  2.31 us (2%)
    all_to_all x4, blocking collectives, exchange(): return lax.all_to_all(values, PEERS, 0, 0, tiled=True)  85.6 us
    pallas_call x7, Pallas kernels, call(): pl.pallas_call(kernel, out_shape=[pltpu.HBM(out.shape, out.dtype) if spac...  24.2 us
    ppermute x1, starting transfers between devices, body(): other = lax.ppermute(mine, 'core', swap)  3.34 us
    ppermute x1, starting transfers between devices, body(): mid_got = lax.ppermute(mid_send, 'core', swap)  3.23 us
  transfers between devices with their start and end apart: 3, of which 2 were waited for; matrix products, arithmetic and copies ran while one was open for 0% of the time, Pallas kernels for 4%

profile of v7, /device:TPU:1, one launch (start us, length us, event | category | flops | bytes accessed | tf_op | source)
XLA Modules:
  0.0 119.9 jit_solution(2822293343791778497)
XLA Ops:
  0.6 0.0 copy-start.14
  0.6 0.0 copy-start.15
  0.7 0.0 copy-start.16
  0.7 0.0 copy-start.17
  0.7 4.4 %block_forward.1 = (bf16[64,16,384]{2,1,0:T(8,128)(2,1)S(1)}, bf16[512,768]{1,0:T(8,128)(2,1)S(1)}, bf16[512,768]{1,0:T(8,128)(2,1)S(1)}, bf16[512,512]{1,0:T(8,...) custom-call(s32[1]{0:T(128)} %bitcast.core_ref, ...), custom_call_target="tpu_custom_call" | custom-call | tf_op jit(solution)/shard_map/block_forward/pallas_call | solution.py:529
  5.0 0.0 copy-start.6
  5.1 0.0 copy-start.7
  5.1 0.0 copy-start.9
  5.1 0.0 copy-start.13
  5.1 26.0 %all_to_all.20.pack_ref = bf16[64,16,384]{2,1,0:T(8,128)(2,1)S(1)} all-to-all(bf16[64,16,384]{2,1,0:T(8,128)(2,1)S(1)} %get-tuple-element.35), channel_id=1, replica_groups=mesh['y_lo'=2,'x'=4,'z'=4,'y_hi'=2,'core'=2] {'x','z','y_hi','y_lo'}, dimensions={0} | all-to-all | bytes 1572864 | tf_op jit(solution)/shard_map/all_to_all | solution.py:647
  31.1 0.0 copy-done.14
  31.1 0.0 copy-done.15
  31.1 0.0 copy-done.16
  31.1 0.0 copy-done.17
  31.1 0.0 copy-done.6
  31.1 0.0 copy-done.7
  31.1 0.0 copy-done.9
  31.1 0.0 copy-done.13
  31.1 12.6 %middle.1 = (bf16[64,16,256]{2,1,0:T(8,128)(2,1)S(1)}, bf16[1536,256]{1,0:T(8,128)(2,1)S(1)}, bf16[1536,256]{1,0:T(8,128)(2,1)S(1)}, bf16[256,768]{1,0:T(8,128)(...) custom-call(s32[1]{0:T(128)} %bitcast.core_ref, ...), custom_call_target="tpu_custom_call" | custom-call | tf_op jit(solution)/shard_map/middle/pallas_call | solution.py:529
  43.8 0.0 copy-start.4
  43.8 0.0 copy-start.8
  43.8 0.0 copy-start.10
  43.8 0.0 copy-start.11
  43.8 0.0 copy-start.12
  43.8 16.4 %all_to_all.21.back_ref = bf16[64,16,256]{2,1,0:T(8,128)(2,1)S(1)} all-to-all(bf16[64,16,256]{2,1,0:T(8,128)(2,1)S(1)} %get-tuple-element.37), channel_id=1, replica_groups=mesh['y_lo'=2,'x'=4,'z'=4,'y_hi'=2,'core'=2] {'x','z','y_hi','y_lo'}, dimensions={0} | all-to-all | bytes 1048576 | tf_op jit(solution)/shard_map/all_to_all | solution.py:647
  60.2 3.2 %collective-permute-start = (bf16[1536,256]{1,0:T(8,128)(2,1)S(1)}, bf16[1536,256]{1,0:T(8,128)(2,1)S(1)}, u32[]{:S(2)}, u32[]{:S(2)}) collective-permute-start(bf16[1536,256]{1,0:T(8,128)(2,1)S(1)} %get-tuple-element.39), channel_id=1, source_target_pairs={{0,1},{1,0},{2,3},{3,2},{4,5},{5,4},{6,7},{7,6},{8,9},{9,8},{10,11... | collective-permute-start | bytes 2359304 | tf_op jit(solution)/shard_map/ppermute | solution.py:658
  63.5 0.0 copy-done.4
  63.5 0.0 copy-done.8
  63.5 0.0 copy-done.10
  63.5 0.0 copy-done.11
  63.5 0.0 copy-done.12
  63.5 3.1 %block_back.1 = (bf16[512,256]{1,0:T(8,128)(2,1)S(1)}, bf16[512,256]{1,0:T(8,128)(2,1)S(1)}) custom-call(s32[1]{0:T(128)} %bitcast.core_ref, bf16[64,16,256]{2,1,0:T(8,128)(2,1)S(1)} %all_to_all.21.back_ref, bf16[512,768]{1,0:T(8,128)(2,1)S(1)} %get-tuple-element.41.qkv_ref, bf16[512,768]{1,0:T(8,128)(2,1)S(1)} %get-tuple-element.42.qkvd_ref, ...), custom_call_target="tpu_custom_call" | custom-call | tf_op jit(solution)/shard_map/block_back/pallas_call | solution.py:529
  66.6 0.1 collective-permute-start.1
  66.7 1.5 %collective-permute-done.1.got_ref = bf16[512,256]{1,0:T(8,128)(2,1)S(1)} collective-permute-done((bf16[512,256]{1,0:T(8,128)(2,1)S(1)}, bf16[512,256]{1,0:T(8,128)(2,1)S(1)}, u32[]{:S(2)}, u32[]{:S(2)}) %collective-permute-start.1) | collective-permute-done | bytes 262176 | tf_op jit(solution)/shard_map/ppermute | solution.py:660
  68.3 0.0 collective-permute-done.mid_got_ref
  68.3 0.2 pair_sum.1
  68.5 21.7 %all_to_all.22.parts_ref = bf16[64,16,512]{2,1,0:T(8,128)(2,1)S(1)} all-to-all(bf16[64,16,512]{2,1,0:T(8,128)(2,1)S(1)} %pair_sum.1), channel_id=1, replica_groups=mesh['y_lo'=2,'x'=4,'z'=4,'y_hi'=2,'core'=2] {'x','z','y_hi','y_lo'}, dimensions={0} | all-to-all | bytes 2097152 | tf_op jit(solution)/shard_map/all_to_all | solution.py:647
  90.2 0.2 peer_sum.1
  90.5 0.0 copy-start
  90.5 0.0 copy-start.1
  90.5 0.0 copy-start.2
  90.5 0.0 copy-start.3
  90.5 0.0 copy-start.5
  90.5 21.5 %all_to_all.23 = bf16[64,16,512]{2,1,0:T(8,128)(2,1)S(1)} all-to-all(bf16[64,16,512]{2,1,0:T(8,128)(2,1)S(1)} %peer_sum.1), channel_id=1, replica_groups=mesh['y_lo'=2,'x'=4,'z'=4,'y_hi'=2,'core'=2] {'x','z','y_hi','y_lo'}, dimensions={0} | all-to-all | bytes 2097152 | tf_op jit(solution)/shard_map/all_to_all | solution.py:647
  112.0 3.3 %collective-permute-start.2 = (bf16[1024,512]{1,0:T(8,128)(2,1)S(1)}, bf16[1024,512]{1,0:T(8,128)(2,1)S(1)}, u32[]{:S(2)}, u32[]{:S(2)}) collective-permute-start(bf16[1024,512]{1,0:T(8,128)(2,1)S(1)} %bitcast.2), channel_id=1, source_target_pairs={{0,1},{1,0},{2,3},{3,2},{4,5},{5,4},{6,7},{7,6},{8,9},{9,8},{10,11... | collective-permute-start | bytes 3145736 | tf_op jit(solution)/shard_map/ppermute | solution.py:683
  115.3 0.0 copy-done
  115.3 0.0 copy-done.1
  115.3 0.0 copy-done.2
  115.3 0.0 copy-done.3
  115.3 0.0 copy-done.5
  115.3 1.5 %finish_mine.1 = (f32[256,768]{1,0:T(8,128)}, f32[256,256]{1,0:T(8,128)}, f32[256,768]{1,0:T(8,128)}, f32[256,256]{1,0:T(8,128)}, f32[256,1024]{1,0:T(8,128)}, /...) custom-call(s32[1]{0:T(128)} %bitcast.core_ref, bf16[1024,512]{1,0:T(8,128)(2,1)S(1)} %bitcast.3, ...), custom_call_target="tpu_custom_call" | custom-call | tf_op jit(solution)/shard_map/finish_mine/pallas_call | solution.py:529
  116.8 0.8 collective-permute-done.2.half_ref
  117.6 2.1 %finish_other.1 = (f32[256,768]{1,0:T(8,128)}, f32[256,256]{1,0:T(8,128)}, f32[256,768]{1,0:T(8,128)}, f32[256,256]{1,0:T(8,128)}, f32[256,1024]{1,0:T(8,128)}, /*index=5*/f32[1024,256]{1,0:T(8,128)}, f32[6]{0:T(128)}) custom-call(s32[1]{0:T(128)} %bitcast.core_ref, ...), custom_call_target="tpu_custom_call", output_to_operand_aliasing={{0}: (9, {}), {1}: (10, {}), {2}: (11, {}), {3}: (12, {}), ... | custom-call | tf_op jit(solution)/shard_map/finish_other/pallas_call | solution.py:529
Async XLA Ops:
  0.6 30.4 %copy-start.14 = (s32[9,1024]{1,0:T(8,128)S(1)}, s32[9,1024]{1,0:T(8,128)}, u32[]{:S(2)}) copy-start(s32[9,1024]{1,0:T(8,128)} %pi_ref.1) | copy-start | bytes 110596
  0.6 30.4 %copy-start.15 = (s32[9,768]{1,0:T(8,128)S(1)}, s32[9,768]{1,0:T(8,128)}, u32[]{:S(2)}) copy-start(s32[9,768]{1,0:T(8,128)} %pq_ref.1) | copy-start | bytes 82948
  0.7 30.4 %copy-start.16 = (s32[35,256]{1,0:T(8,128)S(1)}, s32[35,256]{1,0:T(8,128)}, u32[]{:S(2)}) copy-start(s32[35,256]{1,0:T(8,128)} %pf_ref.1) | copy-start | bytes 107524
  0.7 30.4 %copy-start.17 = (s32[9,256]{1,0:T(8,128)S(1)}, s32[9,256]{1,0:T(8,128)}, u32[]{:S(2)}) copy-start(s32[9,256]{1,0:T(8,128)} %po_ref.1) | copy-start | bytes 27652
  5.0 26.0 %copy-start.6 = (bf16[256,1024]{1,0:T(8,128)(2,1)S(1)}, bf16[256,1024]{1,0:T(8,128)(2,1)}, u32[]{:S(2)}) copy-start(bf16[256,1024]{1,0:T(8,128)(2,1)} %wi_ref.1) | copy-start | bytes 1572868
  5.1 26.0 %copy-start.7 = (bf16[1024,256]{1,0:T(8,128)(2,1)S(1)}, bf16[1024,256]{1,0:T(8,128)(2,1)}, u32[]{:S(2)}) copy-start(bf16[1024,256]{1,0:T(8,128)(2,1)} %wf_ref.1) | copy-start | bytes 1572868
  5.1 26.0 %copy-start.9 = (bf16[256,768]{1,0:T(8,128)(2,1)S(1)}, bf16[256,768]{1,0:T(8,128)(2,1)}, u32[]{:S(2)}) copy-start(bf16[256,768]{1,0:T(8,128)(2,1)} %wq_ref.1) | copy-start | bytes 1179652
  5.1 26.0 %copy-start.13 = (bf16[256,256]{1,0:T(8,128)(2,1)S(1)}, bf16[256,256]{1,0:T(8,128)(2,1)}, u32[]{:S(2)}) copy-start(bf16[256,256]{1,0:T(8,128)(2,1)} %wo_ref.2) | copy-start | bytes 393220
  43.8 19.7 %copy-start.4 = (bf16[256,256]{1,0:T(8,128)(2,1)S(1)}, bf16[256,256]{1,0:T(8,128)(2,1)}, u32[]{:S(2)}) copy-start(bf16[256,256]{1,0:T(8,128)(2,1)} %get-tuple-element.45.so_ref.refs_1_) | copy-start | bytes 393220
  43.8 19.7 %copy-start.8 = (bf16[256,256]{1,0:T(8,128)(2,1)S(1)}, bf16[256,256]{1,0:T(8,128)(2,1)}, u32[]{:S(2)}) copy-start(bf16[256,256]{1,0:T(8,128)(2,1)} %wo_ref.3) | copy-start | bytes 393220
  43.8 19.7 %copy-start.10 = (bf16[512,256]{1,0:T(8,128)(2,1)S(1)}, bf16[512,256]{1,0:T(8,128)(2,1)}, u32[]{:S(2)}) copy-start(bf16[512,256]{1,0:T(8,128)(2,1)} %get-tuple-element.48.h_ref) | copy-start | bytes 786436
  43.8 19.7 %copy-start.11 = (bf16[512,256]{1,0:T(8,128)(2,1)S(1)}, bf16[512,256]{1,0:T(8,128)(2,1)}, u32[]{:S(2)}) copy-start(bf16[512,256]{1,0:T(8,128)(2,1)} %get-tuple-element.46.o_ref) | copy-start | bytes 786436
  43.8 19.7 %copy-start.12 = (bf16[512,256]{1,0:T(8,128)(2,1)S(1)}, bf16[512,256]{1,0:T(8,128)(2,1)}, u32[]{:S(2)}) copy-start(bf16[512,256]{1,0:T(8,128)(2,1)} %get-tuple-element.47.od_ref) | copy-start | bytes 786436
  60.2 8.0 %collective-permute-start = (bf16[1536,256]{1,0:T(8,128)(2,1)S(1)}, bf16[1536,256]{1,0:T(8,128)(2,1)S(1)}, u32[]{:S(2)}, u32[]{:S(2)}) collective-permute-start(bf16[1536,256]{1,0:T(8,128)(2,1)S(1)} %get-tuple-element.39), channel_id=1, source_target_pairs={{0,1},{1,0},{2,3},{3,2},{4,5},{5,4},{6,7},{7,6},{8,9},{9,8},{10,11... | collective-permute-start | bytes 2359304 | tf_op jit(solution)/shard_map/ppermute | solution.py:658
  66.6 1.6 %collective-permute-start.1 = (bf16[512,256]{1,0:T(8,128)(2,1)S(1)}, bf16[512,256]{1,0:T(8,128)(2,1)S(1)}, u32[]{:S(2)}, u32[]{:S(2)}) collective-permute-start(bf16[512,256]{1,0:T(8,128)(2,1)S(1)} %get-tuple-element.50), channel_id=1, source_target_pairs={{0,1},{1,0},{2,3},{3,2},{4,5},{5,4},{6,7},{7,6},{8,9},{9,8},{10,11... | collective-permute-start | bytes 786440 | tf_op jit(solution)/shard_map/ppermute | solution.py:660
  90.5 24.9 %copy-start = (bf16[256,1024]{1,0:T(8,128)(2,1)S(1)}, bf16[256,1024]{1,0:T(8,128)(2,1)}, u32[]{:S(2)}) copy-start(bf16[256,1024]{1,0:T(8,128)(2,1)} %get-tuple-element.54.refs_4_) | copy-start | bytes 1572868
  90.5 24.9 %copy-start.1 = (bf16[1024,256]{1,0:T(8,128)(2,1)S(1)}, bf16[1024,256]{1,0:T(8,128)(2,1)}, u32[]{:S(2)}) copy-start(bf16[1024,256]{1,0:T(8,128)(2,1)} %get-tuple-element.55.refs_5_) | copy-start | bytes 1572868
  90.5 24.8 %copy-start.2 = (bf16[256,768]{1,0:T(8,128)(2,1)S(1)}, bf16[256,768]{1,0:T(8,128)(2,1)}, u32[]{:S(2)}) copy-start(bf16[256,768]{1,0:T(8,128)(2,1)} %get-tuple-element.51.refs_0_) | copy-start | bytes 1179652
  90.5 24.8 %copy-start.3 = (bf16[256,768]{1,0:T(8,128)(2,1)S(1)}, bf16[256,768]{1,0:T(8,128)(2,1)}, u32[]{:S(2)}) copy-start(bf16[256,768]{1,0:T(8,128)(2,1)} %get-tuple-element.52.refs_2_) | copy-start | bytes 1179652
  90.5 24.8 %copy-start.5 = (bf16[256,256]{1,0:T(8,128)(2,1)S(1)}, bf16[256,256]{1,0:T(8,128)(2,1)}, u32[]{:S(2)}) copy-start(bf16[256,256]{1,0:T(8,128)(2,1)} %get-tuple-element.53.refs_3_) | copy-start | bytes 393220
  112.0 5.6 %collective-permute-start.2 = (bf16[1024,512]{1,0:T(8,128)(2,1)S(1)}, bf16[1024,512]{1,0:T(8,128)(2,1)S(1)}, u32[]{:S(2)}, u32[]{:S(2)}) collective-permute-start(bf16[1024,512]{1,0:T(8,128)(2,1)S(1)} %bitcast.2), channel_id=1, source_target_pairs={{0,1},{1,0},{2,3},{3,2},{4,5},{5,4},{6,7},{7,6},{8,9},{9,8},{10,11... | collective-permute-start | bytes 3145736 | tf_op jit(solution)/shard_map/ppermute | solution.py:683

commit v8 on v7

--- a/solution.py
+++ b/solution.py
@@ -136,6 +136,11 @@
     both = nn(rows(values, dots), lanes(weight, weight_dot))
     width = weight.shape[1]
     return both[:WINDOW, :width], both[WINDOW:, :width] + both[:WINDOW, width:]
+
+
+def head_sums(values, mask):
+    total = nt(rows(*[value.astype(BF16) for value in values]), mask)
+    return [total[WINDOW * i : WINDOW * (i + 1), :] for i in range(len(values))]
 
 
 def segment_sums(values, ones):
@@ -176,10 +181,10 @@
 
 
 def attend_back(
-    qkv_ref, qkvd_ref, a_ref, ad_ref, do_ref, dod_ref, dqkv_ref, dqkvd_ref, ones_ref, mask_ref
+    qkv_ref, qkvd_ref, a_ref, ad_ref, o_ref, od_ref, do_ref, dod_ref, dqkv_ref, dqkvd_ref,
+    mask_ref,
 ):
     def step(spots):
-        ones = ones_ref[...]
         mask = mask_ref[...]
         units = [(at, g) for at in spots for g in range(2)]
         da, dad, first, second = [], [], [], []
@@ -190,12 +195,11 @@
             both = nt(twice(do_ref[at, here], dod_ref[at, here]), lanes(vb, vdb))
             da.append(both[:WINDOW])
             dad.append(both[WINDOW:])
-        for (at, g), x, xd in zip(units, da, dad):
-            spot = pl.ds(256 * g, 256)
-            a, ad = a_ref[at, spot].astype(F32), ad_ref[at, spot].astype(F32)
-            first.append(a * x)
-            second.append(ad * x + a * xd)
-        first, second = segment_sums(first, ones), segment_sums(second, ones)
+            do, dod = do_ref[at, here].astype(F32), dod_ref[at, here].astype(F32)
+            o, od = o_ref[at, here].astype(F32), od_ref[at, here].astype(F32)
+            first.append(do * o)
+            second.append(dod * o + do * od)
+        first, second = head_sums(first, mask), head_sums(second, mask)
         for (at, g), x, xd, total, total_dot in zip(units, da, dad, first, second):
             spot = pl.ds(256 * g, 256)
             here = pl.ds(GROUP * g, GROUP)
@@ -367,7 +371,7 @@
         second(i)
     dqkv, dqkvd = dqkv_ref.at[pl.ds(0, tokens), :], dqkv_ref.at[pl.ds(tokens, tokens), :]
     attend_back(
-        qkv_ref, qkvd_ref, a_ref, ad_ref, do_ref, dod_ref, dqkv, dqkvd, ones_ref, mask_ref
+        qkv_ref, qkvd_ref, a_ref, ad_ref, o_part, od_part, do_ref, dod_ref, dqkv, dqkvd, mask_ref
     )
 
     for i in range(tokens // 256):
@@ -432,7 +436,7 @@
     dod_ref[...] = nt(lanes(dxd, dx), lanes(wo_ref[...], so_ref[...])).astype(BF16)
     hv_ref[3] = tn(rows(od_ref[...], o_ref[...]), rows(dx, dxd)).astype(BF16)
     attend_back(
-        qkv_ref, qkvd_ref, a_ref, ad_ref, do_ref, dod_ref, None, dqkvd_ref, ones_ref, mask_ref
+        qkv_ref, qkvd_ref, a_ref, ad_ref, o_ref, od_ref, do_ref, dod_ref, None, dqkvd_ref, mask_ref
     )
     h = h_ref[...]
     for c in range(3):
@@ -494,21 +498,25 @@
             )
             copies[-1].start()
         sums[n] = jnp.sum(total, axis=0, keepdims=True)
+    return copies, rows(*[sums[n] for n in range(6)], jnp.zeros((2, 256), F32))
+
+
+def finish_mine_kernel(core_ref, half_ref, *refs):
+    signs, outs, sum_ref, wides, sems = refs[:6], refs[6:12], refs[12], refs[13:19], refs[19]
+    copies, sums = write_half(core_ref[0], half_ref, signs, outs, wides, sems)
+    sum_ref[...] = sums
     for copy in copies:
         copy.wait()
-    return rows(*[sums[n] for n in range(6)], jnp.zeros((2, 256), F32))
-
-
-def finish_mine_kernel(core_ref, half_ref, *refs):
-    signs, outs, sum_ref, wides, sems = refs[:6], refs[6:12], refs[12], refs[13:19], refs[19]
-    sum_ref[...] = write_half(core_ref[0], half_ref, signs, outs, wides, sems)
 
 
 def finish_other_kernel(core_ref, half_ref, sum_ref, *refs):
     signs, outs, trace_ref, wides, sems = refs[:6], refs[12:18], refs[18], refs[19:25], refs[25]
-    sums = sum_ref[...] + write_half(1 - core_ref[0], half_ref, signs, outs, wides, sems)
+    copies, sums = write_half(1 - core_ref[0], half_ref, signs, outs, wides, sems)
+    sums = sums + sum_ref[...]
     for n, out in enumerate(outs):
         trace_ref[n] = jnp.sum(sums[n : n + 1, :]) / math.sqrt(out.shape[0] * out.shape[1])
+    for copy in copies:
+        copy.wait()
 
 
 def shaped(dtype, *shape):

time: 120 us -> 120 us (level)
  no operation moved by 1% of the time
where the time goes in v8:
time: 120 us
  blocking collectives  85.6 us (71%)
  Pallas kernels  24 us (20%)
  starting transfers between devices  6.67 us (6%)
  waiting for transfers between devices  2.32 us (2%)
    all_to_all x4, blocking collectives, exchange(): return lax.all_to_all(values, PEERS, 0, 0, tiled=True)  85.6 us
    pallas_call x7, Pallas kernels, call(): pl.pallas_call(kernel, out_shape=[pltpu.HBM(out.shape, out.dtype) if spac...  24 us
    ppermute x1, starting transfers between devices, body(): other = lax.ppermute(mine, 'core', swap)  3.34 us
    ppermute x1, starting transfers between devices, body(): mid_got = lax.ppermute(mid_send, 'core', swap)  3.23 us
  transfers between devices with their start and end apart: 3, of which 2 were waited for; matrix products, arithmetic and copies ran while one was open for 0% of the time, Pallas kernels for 4%

profile of v8, /device:TPU:1, one launch (start us, length us, event | category | flops | bytes accessed | tf_op | source)
XLA Modules:
  0.0 119.8 jit_solution(16203810038904395215)
XLA Ops:
  0.6 0.0 copy-start.14
  0.6 0.0 copy-start.15
  0.7 0.0 copy-start.16
  0.7 0.0 copy-start.17
  0.7 4.4 %block_forward.1 = (bf16[64,16,384]{2,1,0:T(8,128)(2,1)S(1)}, bf16[512,768]{1,0:T(8,128)(2,1)S(1)}, bf16[512,768]{1,0:T(8,128)(2,1)S(1)}, bf16[512,512]{1,0:T(8,...) custom-call(s32[1]{0:T(128)} %bitcast.core_ref, ...), custom_call_target="tpu_custom_call" | custom-call | tf_op jit(solution)/shard_map/block_forward/pallas_call | solution.py:537
  5.0 0.0 copy-start.6
  5.1 0.0 copy-start.7
  5.1 0.0 copy-start.9
  5.1 0.0 copy-start.13
  5.1 26.0 %all_to_all.20.pack_ref = bf16[64,16,384]{2,1,0:T(8,128)(2,1)S(1)} all-to-all(bf16[64,16,384]{2,1,0:T(8,128)(2,1)S(1)} %get-tuple-element.35), channel_id=1, replica_groups=mesh['y_lo'=2,'x'=4,'z'=4,'y_hi'=2,'core'=2] {'x','z','y_hi','y_lo'}, dimensions={0} | all-to-all | bytes 1572864 | tf_op jit(solution)/shard_map/all_to_all | solution.py:655
  31.1 0.0 copy-done.14
  31.1 0.0 copy-done.15
  31.1 0.0 copy-done.16
  31.1 0.0 copy-done.17
  31.1 0.0 copy-done.6
  31.1 0.0 copy-done.7
  31.1 0.0 copy-done.9
  31.1 0.0 copy-done.13
  31.1 12.6 %middle.1 = (bf16[64,16,256]{2,1,0:T(8,128)(2,1)S(1)}, bf16[1536,256]{1,0:T(8,128)(2,1)S(1)}, bf16[1536,256]{1,0:T(8,128)(2,1)S(1)}, bf16[256,768]{1,0:T(8,128)(...) custom-call(s32[1]{0:T(128)} %bitcast.core_ref, ...), custom_call_target="tpu_custom_call" | custom-call | tf_op jit(solution)/shard_map/middle/pallas_call | solution.py:537
  43.7 0.0 copy-start.4
  43.7 0.0 copy-start.8
  43.7 0.0 copy-start.10
  43.8 0.0 copy-start.11
  43.8 0.0 copy-start.12
  43.8 16.4 %all_to_all.21.back_ref = bf16[64,16,256]{2,1,0:T(8,128)(2,1)S(1)} all-to-all(bf16[64,16,256]{2,1,0:T(8,128)(2,1)S(1)} %get-tuple-element.37), channel_id=1, replica_groups=mesh['y_lo'=2,'x'=4,'z'=4,'y_hi'=2,'core'=2] {'x','z','y_hi','y_lo'}, dimensions={0} | all-to-all | bytes 1048576 | tf_op jit(solution)/shard_map/all_to_all | solution.py:655
  60.2 3.2 %collective-permute-start = (bf16[1536,256]{1,0:T(8,128)(2,1)S(1)}, bf16[1536,256]{1,0:T(8,128)(2,1)S(1)}, u32[]{:S(2)}, u32[]{:S(2)}) collective-permute-start(bf16[1536,256]{1,0:T(8,128)(2,1)S(1)} %get-tuple-element.39), channel_id=1, source_target_pairs={{0,1},{1,0},{2,3},{3,2},{4,5},{5,4},{6,7},{7,6},{8,9},{9,8},{10,11... | collective-permute-start | bytes 2359304 | tf_op jit(solution)/shard_map/ppermute | solution.py:666
  63.4 0.0 copy-done.4
  63.4 0.0 copy-done.8
  63.4 0.0 copy-done.10
  63.4 0.0 copy-done.11
  63.4 0.0 copy-done.12
  63.5 3.1 %block_back.1 = (bf16[512,256]{1,0:T(8,128)(2,1)S(1)}, bf16[512,256]{1,0:T(8,128)(2,1)S(1)}) custom-call(s32[1]{0:T(128)} %bitcast.core_ref, bf16[64,16,256]{2,1,0:T(8,128)(2,1)S(1)} %all_to_all.21.back_ref, bf16[512,768]{1,0:T(8,128)(2,1)S(1)} %get-tuple-element.41.qkv_ref, bf16[512,768]{1,0:T(8,128)(2,1)S(1)} %get-tuple-element.42.qkvd_ref, ...), custom_call_target="tpu_custom_call" | custom-call | tf_op jit(solution)/shard_map/block_back/pallas_call | solution.py:537
  66.6 0.1 collective-permute-start.1
  66.7 1.5 %collective-permute-done.1.got_ref = bf16[512,256]{1,0:T(8,128)(2,1)S(1)} collective-permute-done((bf16[512,256]{1,0:T(8,128)(2,1)S(1)}, bf16[512,256]{1,0:T(8,128)(2,1)S(1)}, u32[]{:S(2)}, u32[]{:S(2)}) %collective-permute-start.1) | collective-permute-done | bytes 262176 | tf_op jit(solution)/shard_map/ppermute | solution.py:668
  68.2 0.0 collective-permute-done.mid_got_ref
  68.2 0.2 pair_sum.1
  68.4 21.7 %all_to_all.22.parts_ref = bf16[64,16,512]{2,1,0:T(8,128)(2,1)S(1)} all-to-all(bf16[64,16,512]{2,1,0:T(8,128)(2,1)S(1)} %pair_sum.1), channel_id=1, replica_groups=mesh['y_lo'=2,'x'=4,'z'=4,'y_hi'=2,'core'=2] {'x','z','y_hi','y_lo'}, dimensions={0} | all-to-all | bytes 2097152 | tf_op jit(solution)/shard_map/all_to_all | solution.py:655
  90.1 0.2 peer_sum.1
  90.4 0.0 copy-start
  90.4 0.0 copy-start.1
  90.4 0.0 copy-start.2
  90.4 0.0 copy-start.3
  90.4 0.0 copy-start.5
  90.4 21.5 %all_to_all.23 = bf16[64,16,512]{2,1,0:T(8,128)(2,1)S(1)} all-to-all(bf16[64,16,512]{2,1,0:T(8,128)(2,1)S(1)} %peer_sum.1), channel_id=1, replica_groups=mesh['y_lo'=2,'x'=4,'z'=4,'y_hi'=2,'core'=2] {'x','z','y_hi','y_lo'}, dimensions={0} | all-to-all | bytes 2097152 | tf_op jit(solution)/shard_map/all_to_all | solution.py:655
  111.9 3.3 %collective-permute-start.2 = (bf16[1024,512]{1,0:T(8,128)(2,1)S(1)}, bf16[1024,512]{1,0:T(8,128)(2,1)S(1)}, u32[]{:S(2)}, u32[]{:S(2)}) collective-permute-start(bf16[1024,512]{1,0:T(8,128)(2,1)S(1)} %bitcast.2), channel_id=1, source_target_pairs={{0,1},{1,0},{2,3},{3,2},{4,5},{5,4},{6,7},{7,6},{8,9},{9,8},{10,11... | collective-permute-start | bytes 3145736 | tf_op jit(solution)/shard_map/ppermute | solution.py:691
  115.2 0.0 copy-done
  115.2 0.0 copy-done.1
  115.2 0.0 copy-done.2
  115.2 0.0 copy-done.3
  115.2 0.0 copy-done.5
  115.3 1.5 %finish_mine.1 = (f32[256,768]{1,0:T(8,128)}, f32[256,256]{1,0:T(8,128)}, f32[256,768]{1,0:T(8,128)}, f32[256,256]{1,0:T(8,128)}, f32[256,1024]{1,0:T(8,128)}, /...) custom-call(s32[1]{0:T(128)} %bitcast.core_ref, bf16[1024,512]{1,0:T(8,128)(2,1)S(1)} %bitcast.3, ...), custom_call_target="tpu_custom_call" | custom-call | tf_op jit(solution)/shard_map/finish_mine/pallas_call | solution.py:537
  116.7 0.8 collective-permute-done.2.half_ref
  117.5 2.0 %finish_other.1 = (f32[256,768]{1,0:T(8,128)}, f32[256,256]{1,0:T(8,128)}, f32[256,768]{1,0:T(8,128)}, f32[256,256]{1,0:T(8,128)}, f32[256,1024]{1,0:T(8,128)}, /*index=5*/f32[1024,256]{1,0:T(8,128)}, f32[6]{0:T(128)}) custom-call(s32[1]{0:T(128)} %bitcast.core_ref, ...), custom_call_target="tpu_custom_call", output_to_operand_aliasing={{0}: (9, {}), {1}: (10, {}), {2}: (11, {}), {3}: (12, {}), ... | custom-call | tf_op jit(solution)/shard_map/finish_other/pallas_call | solution.py:537
Async XLA Ops:
  0.6 30.4 %copy-start.14 = (s32[9,1024]{1,0:T(8,128)S(1)}, s32[9,1024]{1,0:T(8,128)}, u32[]{:S(2)}) copy-start(s32[9,1024]{1,0:T(8,128)} %pi_ref.1) | copy-start | bytes 110596
  0.6 30.4 %copy-start.15 = (s32[9,768]{1,0:T(8,128)S(1)}, s32[9,768]{1,0:T(8,128)}, u32[]{:S(2)}) copy-start(s32[9,768]{1,0:T(8,128)} %pq_ref.1) | copy-start | bytes 82948
  0.7 30.4 %copy-start.16 = (s32[35,256]{1,0:T(8,128)S(1)}, s32[35,256]{1,0:T(8,128)}, u32[]{:S(2)}) copy-start(s32[35,256]{1,0:T(8,128)} %pf_ref.1) | copy-start | bytes 107524
  0.7 30.4 %copy-start.17 = (s32[9,256]{1,0:T(8,128)S(1)}, s32[9,256]{1,0:T(8,128)}, u32[]{:S(2)}) copy-start(s32[9,256]{1,0:T(8,128)} %po_ref.1) | copy-start | bytes 27652
  5.0 26.0 %copy-start.6 = (bf16[256,1024]{1,0:T(8,128)(2,1)S(1)}, bf16[256,1024]{1,0:T(8,128)(2,1)}, u32[]{:S(2)}) copy-start(bf16[256,1024]{1,0:T(8,128)(2,1)} %wi_ref.1) | copy-start | bytes 1572868
  5.1 26.0 %copy-start.7 = (bf16[1024,256]{1,0:T(8,128)(2,1)S(1)}, bf16[1024,256]{1,0:T(8,128)(2,1)}, u32[]{:S(2)}) copy-start(bf16[1024,256]{1,0:T(8,128)(2,1)} %wf_ref.1) | copy-start | bytes 1572868
  5.1 26.0 %copy-start.9 = (bf16[256,768]{1,0:T(8,128)(2,1)S(1)}, bf16[256,768]{1,0:T(8,128)(2,1)}, u32[]{:S(2)}) copy-start(bf16[256,768]{1,0:T(8,128)(2,1)} %wq_ref.1) | copy-start | bytes 1179652
  5.1 26.0 %copy-start.13 = (bf16[256,256]{1,0:T(8,128)(2,1)S(1)}, bf16[256,256]{1,0:T(8,128)(2,1)}, u32[]{:S(2)}) copy-start(bf16[256,256]{1,0:T(8,128)(2,1)} %wo_ref.2) | copy-start | bytes 393220
  43.7 19.7 %copy-start.4 = (bf16[256,256]{1,0:T(8,128)(2,1)S(1)}, bf16[256,256]{1,0:T(8,128)(2,1)}, u32[]{:S(2)}) copy-start(bf16[256,256]{1,0:T(8,128)(2,1)} %get-tuple-element.45.so_ref.refs_1_) | copy-start | bytes 393220
  43.7 19.7 %copy-start.8 = (bf16[256,256]{1,0:T(8,128)(2,1)S(1)}, bf16[256,256]{1,0:T(8,128)(2,1)}, u32[]{:S(2)}) copy-start(bf16[256,256]{1,0:T(8,128)(2,1)} %wo_ref.3) | copy-start | bytes 393220
  43.7 19.7 %copy-start.10 = (bf16[512,256]{1,0:T(8,128)(2,1)S(1)}, bf16[512,256]{1,0:T(8,128)(2,1)}, u32[]{:S(2)}) copy-start(bf16[512,256]{1,0:T(8,128)(2,1)} %get-tuple-element.48.h_ref) | copy-start | bytes 786436
  43.8 19.7 %copy-start.11 = (bf16[512,256]{1,0:T(8,128)(2,1)S(1)}, bf16[512,256]{1,0:T(8,128)(2,1)}, u32[]{:S(2)}) copy-start(bf16[512,256]{1,0:T(8,128)(2,1)} %get-tuple-element.46.o_ref) | copy-start | bytes 786436
  43.8 19.7 %copy-start.12 = (bf16[512,256]{1,0:T(8,128)(2,1)S(1)}, bf16[512,256]{1,0:T(8,128)(2,1)}, u32[]{:S(2)}) copy-start(bf16[512,256]{1,0:T(8,128)(2,1)} %get-tuple-element.47.od_ref) | copy-start | bytes 786436
  60.2 8.0 %collective-permute-start = (bf16[1536,256]{1,0:T(8,128)(2,1)S(1)}, bf16[1536,256]{1,0:T(8,128)(2,1)S(1)}, u32[]{:S(2)}, u32[]{:S(2)}) collective-permute-start(bf16[1536,256]{1,0:T(8,128)(2,1)S(1)} %get-tuple-element.39), channel_id=1, source_target_pairs={{0,1},{1,0},{2,3},{3,2},{4,5},{5,4},{6,7},{7,6},{8,9},{9,8},{10,11... | collective-permute-start | bytes 2359304 | tf_op jit(solution)/shard_map/ppermute | solution.py:666
  66.6 1.6 %collective-permute-start.1 = (bf16[512,256]{1,0:T(8,128)(2,1)S(1)}, bf16[512,256]{1,0:T(8,128)(2,1)S(1)}, u32[]{:S(2)}, u32[]{:S(2)}) collective-permute-start(bf16[512,256]{1,0:T(8,128)(2,1)S(1)} %get-tuple-element.50), channel_id=1, source_target_pairs={{0,1},{1,0},{2,3},{3,2},{4,5},{5,4},{6,7},{7,6},{8,9},{9,8},{10,11... | collective-permute-start | bytes 786440 | tf_op jit(solution)/shard_map/ppermute | solution.py:668
  90.4 24.9 %copy-start = (bf16[256,1024]{1,0:T(8,128)(2,1)S(1)}, bf16[256,1024]{1,0:T(8,128)(2,1)}, u32[]{:S(2)}) copy-start(bf16[256,1024]{1,0:T(8,128)(2,1)} %get-tuple-element.54.refs_4_) | copy-start | bytes 1572868
  90.4 24.9 %copy-start.1 = (bf16[1024,256]{1,0:T(8,128)(2,1)S(1)}, bf16[1024,256]{1,0:T(8,128)(2,1)}, u32[]{:S(2)}) copy-start(bf16[1024,256]{1,0:T(8,128)(2,1)} %get-tuple-element.55.refs_5_) | copy-start | bytes 1572868
  90.4 24.8 %copy-start.2 = (bf16[256,768]{1,0:T(8,128)(2,1)S(1)}, bf16[256,768]{1,0:T(8,128)(2,1)}, u32[]{:S(2)}) copy-start(bf16[256,768]{1,0:T(8,128)(2,1)} %get-tuple-element.51.refs_0_) | copy-start | bytes 1179652
  90.4 24.8 %copy-start.3 = (bf16[256,768]{1,0:T(8,128)(2,1)S(1)}, bf16[256,768]{1,0:T(8,128)(2,1)}, u32[]{:S(2)}) copy-start(bf16[256,768]{1,0:T(8,128)(2,1)} %get-tuple-element.52.refs_2_) | copy-start | bytes 1179652
  90.4 24.8 %copy-start.5 = (bf16[256,256]{1,0:T(8,128)(2,1)S(1)}, bf16[256,256]{1,0:T(8,128)(2,1)}, u32[]{:S(2)}) copy-start(bf16[256,256]{1,0:T(8,128)(2,1)} %get-tuple-element.53.refs_3_) | copy-start | bytes 393220
  111.9 5.6 %collective-permute-start.2 = (bf16[1024,512]{1,0:T(8,128)(2,1)S(1)}, bf16[1024,512]{1,0:T(8,128)(2,1)S(1)}, u32[]{:S(2)}, u32[]{:S(2)}) collective-permute-start(bf16[1024,512]{1,0:T(8,128)(2,1)S(1)} %bitcast.2), channel_id=1, source_target_pairs={{0,1},{1,0},{2,3},{3,2},{4,5},{5,4},{6,7},{7,6},{8,9},{9,8},{10,11... | collective-permute-start | bytes 3145736 | tf_op jit(solution)/shard_map/ppermute | solution.py:691

commit v9 on v7

--- a/solution.py
+++ b/solution.py
@@ -17,7 +17,7 @@
 SCALE = HD ** (-0.5)
 GELU_K = math.sqrt(2.0 / math.pi)
 GELU_C = 0.044715
-PEERS = ("x", "z", "y_hi", "y_lo")
+PEERS = ("y_lo", "z", "x", "y_hi")
 
 
 def nn(a, b):

time: 120 us -> 120 us (level)
  no operation moved by 1% of the time
where the time goes in v9:
time: 120 us
  blocking collectives  84.9 us (71%)
  Pallas kernels  24.2 us (20%)
  starting transfers between devices  7.13 us (6%)
  waiting for transfers between devices  2.32 us (2%)
    all_to_all x4, blocking collectives, exchange(): return lax.all_to_all(values, PEERS, 0, 0, tiled=True)  84.9 us
    pallas_call x7, Pallas kernels, call(): pl.pallas_call(kernel, out_shape=[pltpu.HBM(out.shape, out.dtype) if spac...  24.2 us
    ppermute x1, starting transfers between devices, body(): other = lax.ppermute(mine, 'core', swap)  3.55 us
    ppermute x1, starting transfers between devices, body(): mid_got = lax.ppermute(mid_send, 'core', swap)  3.49 us
  transfers between devices with their start and end apart: 3, of which 2 were waited for; matrix products, arithmetic and copies ran while one was open for 0% of the time, Pallas kernels for 4%

profile of v9, /device:TPU:1, one launch (start us, length us, event | category | flops | bytes accessed | tf_op | source)
XLA Modules:
  0.0 119.7 jit_solution(1149749851070244127)
XLA Ops:
  0.6 0.0 copy-start.14
  0.6 0.0 copy-start.15
  0.7 0.0 copy-start.16
  0.7 0.0 copy-start.17
  0.7 4.4 %block_forward.1 = (bf16[64,16,384]{2,1,0:T(8,128)(2,1)S(1)}, bf16[512,768]{1,0:T(8,128)(2,1)S(1)}, bf16[512,768]{1,0:T(8,128)(2,1)S(1)}, bf16[512,512]{1,0:T(8,...) custom-call(s32[1]{0:T(128)} %bitcast.core_ref, ...), custom_call_target="tpu_custom_call" | custom-call | tf_op jit(solution)/shard_map/block_forward/pallas_call | solution.py:529
  5.0 0.0 copy-start.6
  5.1 0.0 copy-start.7
  5.1 0.0 copy-start.9
  5.1 0.0 copy-start.13
  5.1 26.1 %all_to_all.20.pack_ref = bf16[64,16,384]{2,1,0:T(8,128)(2,1)S(1)} all-to-all(bf16[64,16,384]{2,1,0:T(8,128)(2,1)S(1)} %get-tuple-element.35), channel_id=1, replica_groups=mesh['y_lo'=2,'x'=4,'z'=4,'y_hi'=2,'core'=2] {'y_lo','z','x','y_hi'}, dimensions={0} | all-to-all | bytes 1572864 | tf_op jit(solution)/shard_map/all_to_all | solution.py:647
  31.2 0.0 copy-done.14
  31.2 0.0 copy-done.15
  31.2 0.0 copy-done.16
  31.2 0.0 copy-done.17
  31.2 0.0 copy-done.6
  31.2 0.0 copy-done.7
  31.2 0.0 copy-done.9
  31.3 0.0 copy-done.13
  31.3 12.6 %middle.1 = (bf16[64,16,256]{2,1,0:T(8,128)(2,1)S(1)}, bf16[1536,256]{1,0:T(8,128)(2,1)S(1)}, bf16[1536,256]{1,0:T(8,128)(2,1)S(1)}, bf16[256,768]{1,0:T(8,128)(...) custom-call(s32[1]{0:T(128)} %bitcast.core_ref, ...), custom_call_target="tpu_custom_call" | custom-call | tf_op jit(solution)/shard_map/middle/pallas_call | solution.py:529
  43.9 0.0 copy-start.4
  43.9 0.0 copy-start.8
  43.9 0.0 copy-start.10
  43.9 0.0 copy-start.11
  44.0 0.0 copy-start.12
  44.0 15.8 %all_to_all.21.back_ref = bf16[64,16,256]{2,1,0:T(8,128)(2,1)S(1)} all-to-all(bf16[64,16,256]{2,1,0:T(8,128)(2,1)S(1)} %get-tuple-element.37), channel_id=1, replica_groups=mesh['y_lo'=2,'x'=4,'z'=4,'y_hi'=2,'core'=2] {'y_lo','z','x','y_hi'}, dimensions={0} | all-to-all | bytes 1048576 | tf_op jit(solution)/shard_map/all_to_all | solution.py:647
  59.8 3.5 %collective-permute-start = (bf16[1536,256]{1,0:T(8,128)(2,1)S(1)}, bf16[1536,256]{1,0:T(8,128)(2,1)S(1)}, u32[]{:S(2)}, u32[]{:S(2)}) collective-permute-start(bf16[1536,256]{1,0:T(8,128)(2,1)S(1)} %get-tuple-element.39), channel_id=1, source_target_pairs={{0,1},{1,0},{2,3},{3,2},{4,5},{5,4},{6,7},{7,6},{8,9},{9,8},{10,11... | collective-permute-start | bytes 2359304 | tf_op jit(solution)/shard_map/ppermute | solution.py:658
  63.3 0.0 copy-done.4
  63.3 0.0 copy-done.8
  63.3 0.0 copy-done.10
  63.3 0.0 copy-done.11
  63.3 0.0 copy-done.12
  63.3 3.1 %block_back.1 = (bf16[512,256]{1,0:T(8,128)(2,1)S(1)}, bf16[512,256]{1,0:T(8,128)(2,1)S(1)}) custom-call(s32[1]{0:T(128)} %bitcast.core_ref, bf16[64,16,256]{2,1,0:T(8,128)(2,1)S(1)} %all_to_all.21.back_ref, bf16[512,768]{1,0:T(8,128)(2,1)S(1)} %get-tuple-element.41.qkv_ref, bf16[512,768]{1,0:T(8,128)(2,1)S(1)} %get-tuple-element.42.qkvd_ref, ...), custom_call_target="tpu_custom_call" | custom-call | tf_op jit(solution)/shard_map/block_back/pallas_call | solution.py:529
  66.5 0.1 collective-permute-start.1
  66.6 1.5 %collective-permute-done.1.got_ref = bf16[512,256]{1,0:T(8,128)(2,1)S(1)} collective-permute-done((bf16[512,256]{1,0:T(8,128)(2,1)S(1)}, bf16[512,256]{1,0:T(8,128)(2,1)S(1)}, u32[]{:S(2)}, u32[]{:S(2)}) %collective-permute-start.1) | collective-permute-done | bytes 262176 | tf_op jit(solution)/shard_map/ppermute | solution.py:660
  68.1 0.0 collective-permute-done.mid_got_ref
  68.1 0.2 pair_sum.1
  68.3 21.7 %all_to_all.22.parts_ref = bf16[64,16,512]{2,1,0:T(8,128)(2,1)S(1)} all-to-all(bf16[64,16,512]{2,1,0:T(8,128)(2,1)S(1)} %pair_sum.1), channel_id=1, replica_groups=mesh['y_lo'=2,'x'=4,'z'=4,'y_hi'=2,'core'=2] {'y_lo','z','x','y_hi'}, dimensions={0} | all-to-all | bytes 2097152 | tf_op jit(solution)/shard_map/all_to_all | solution.py:647
  90.1 0.2 peer_sum.1
  90.3 0.0 copy-start
  90.3 0.0 copy-start.1
  90.4 0.0 copy-start.2
  90.4 0.0 copy-start.3
  90.4 0.0 copy-start.5
  90.4 21.2 %all_to_all.23 = bf16[64,16,512]{2,1,0:T(8,128)(2,1)S(1)} all-to-all(bf16[64,16,512]{2,1,0:T(8,128)(2,1)S(1)} %peer_sum.1), channel_id=1, replica_groups=mesh['y_lo'=2,'x'=4,'z'=4,'y_hi'=2,'core'=2] {'y_lo','z','x','y_hi'}, dimensions={0} | all-to-all | bytes 2097152 | tf_op jit(solution)/shard_map/all_to_all | solution.py:647
  111.6 3.5 %collective-permute-start.2 = (bf16[1024,512]{1,0:T(8,128)(2,1)S(1)}, bf16[1024,512]{1,0:T(8,128)(2,1)S(1)}, u32[]{:S(2)}, u32[]{:S(2)}) collective-permute-start(bf16[1024,512]{1,0:T(8,128)(2,1)S(1)} %bitcast.2), channel_id=1, source_target_pairs={{0,1},{1,0},{2,3},{3,2},{4,5},{5,4},{6,7},{7,6},{8,9},{9,8},{10,11... | collective-permute-start | bytes 3145736 | tf_op jit(solution)/shard_map/ppermute | solution.py:683
  115.1 0.0 copy-done
  115.1 0.0 copy-done.1
  115.1 0.0 copy-done.2
  115.1 0.0 copy-done.3
  115.2 0.0 copy-done.5
  115.2 1.5 %finish_mine.1 = (f32[256,768]{1,0:T(8,128)}, f32[256,256]{1,0:T(8,128)}, f32[256,768]{1,0:T(8,128)}, f32[256,256]{1,0:T(8,128)}, f32[256,1024]{1,0:T(8,128)}, /...) custom-call(s32[1]{0:T(128)} %bitcast.core_ref, bf16[1024,512]{1,0:T(8,128)(2,1)S(1)} %bitcast.3, ...), custom_call_target="tpu_custom_call" | custom-call | tf_op jit(solution)/shard_map/finish_mine/pallas_call | solution.py:529
  116.6 0.8 collective-permute-done.2.half_ref
  117.4 2.1 %finish_other.1 = (f32[256,768]{1,0:T(8,128)}, f32[256,256]{1,0:T(8,128)}, f32[256,768]{1,0:T(8,128)}, f32[256,256]{1,0:T(8,128)}, f32[256,1024]{1,0:T(8,128)}, /*index=5*/f32[1024,256]{1,0:T(8,128)}, f32[6]{0:T(128)}) custom-call(s32[1]{0:T(128)} %bitcast.core_ref, ...), custom_call_target="tpu_custom_call", output_to_operand_aliasing={{0}: (9, {}), {1}: (10, {}), {2}: (11, {}), {3}: (12, {}), ... | custom-call | tf_op jit(solution)/shard_map/finish_other/pallas_call | solution.py:529
Async XLA Ops:
  0.6 30.6 %copy-start.14 = (s32[9,1024]{1,0:T(8,128)S(1)}, s32[9,1024]{1,0:T(8,128)}, u32[]{:S(2)}) copy-start(s32[9,1024]{1,0:T(8,128)} %pi_ref.1) | copy-start | bytes 110596
  0.6 30.6 %copy-start.15 = (s32[9,768]{1,0:T(8,128)S(1)}, s32[9,768]{1,0:T(8,128)}, u32[]{:S(2)}) copy-start(s32[9,768]{1,0:T(8,128)} %pq_ref.1) | copy-start | bytes 82948
  0.7 30.6 %copy-start.16 = (s32[35,256]{1,0:T(8,128)S(1)}, s32[35,256]{1,0:T(8,128)}, u32[]{:S(2)}) copy-start(s32[35,256]{1,0:T(8,128)} %pf_ref.1) | copy-start | bytes 107524
  0.7 30.5 %copy-start.17 = (s32[9,256]{1,0:T(8,128)S(1)}, s32[9,256]{1,0:T(8,128)}, u32[]{:S(2)}) copy-start(s32[9,256]{1,0:T(8,128)} %po_ref.1) | copy-start | bytes 27652
  5.0 26.2 %copy-start.6 = (bf16[256,1024]{1,0:T(8,128)(2,1)S(1)}, bf16[256,1024]{1,0:T(8,128)(2,1)}, u32[]{:S(2)}) copy-start(bf16[256,1024]{1,0:T(8,128)(2,1)} %wi_ref.1) | copy-start | bytes 1572868
  5.1 26.2 %copy-start.7 = (bf16[1024,256]{1,0:T(8,128)(2,1)S(1)}, bf16[1024,256]{1,0:T(8,128)(2,1)}, u32[]{:S(2)}) copy-start(bf16[1024,256]{1,0:T(8,128)(2,1)} %wf_ref.1) | copy-start | bytes 1572868
  5.1 26.2 %copy-start.9 = (bf16[256,768]{1,0:T(8,128)(2,1)S(1)}, bf16[256,768]{1,0:T(8,128)(2,1)}, u32[]{:S(2)}) copy-start(bf16[256,768]{1,0:T(8,128)(2,1)} %wq_ref.1) | copy-start | bytes 1179652
  5.1 26.2 %copy-start.13 = (bf16[256,256]{1,0:T(8,128)(2,1)S(1)}, bf16[256,256]{1,0:T(8,128)(2,1)}, u32[]{:S(2)}) copy-start(bf16[256,256]{1,0:T(8,128)(2,1)} %wo_ref.2) | copy-start | bytes 393220
  43.9 19.4 %copy-start.4 = (bf16[256,256]{1,0:T(8,128)(2,1)S(1)}, bf16[256,256]{1,0:T(8,128)(2,1)}, u32[]{:S(2)}) copy-start(bf16[256,256]{1,0:T(8,128)(2,1)} %get-tuple-element.45.so_ref.refs_1_) | copy-start | bytes 393220
  43.9 19.4 %copy-start.8 = (bf16[256,256]{1,0:T(8,128)(2,1)S(1)}, bf16[256,256]{1,0:T(8,128)(2,1)}, u32[]{:S(2)}) copy-start(bf16[256,256]{1,0:T(8,128)(2,1)} %wo_ref.3) | copy-start | bytes 393220
  43.9 19.4 %copy-start.10 = (bf16[512,256]{1,0:T(8,128)(2,1)S(1)}, bf16[512,256]{1,0:T(8,128)(2,1)}, u32[]{:S(2)}) copy-start(bf16[512,256]{1,0:T(8,128)(2,1)} %get-tuple-element.48.h_ref) | copy-start | bytes 786436
  43.9 19.4 %copy-start.11 = (bf16[512,256]{1,0:T(8,128)(2,1)S(1)}, bf16[512,256]{1,0:T(8,128)(2,1)}, u32[]{:S(2)}) copy-start(bf16[512,256]{1,0:T(8,128)(2,1)} %get-tuple-element.46.o_ref) | copy-start | bytes 786436
  44.0 19.4 %copy-start.12 = (bf16[512,256]{1,0:T(8,128)(2,1)S(1)}, bf16[512,256]{1,0:T(8,128)(2,1)}, u32[]{:S(2)}) copy-start(bf16[512,256]{1,0:T(8,128)(2,1)} %get-tuple-element.47.od_ref) | copy-start | bytes 786436
  59.8 8.3 %collective-permute-start = (bf16[1536,256]{1,0:T(8,128)(2,1)S(1)}, bf16[1536,256]{1,0:T(8,128)(2,1)S(1)}, u32[]{:S(2)}, u32[]{:S(2)}) collective-permute-start(bf16[1536,256]{1,0:T(8,128)(2,1)S(1)} %get-tuple-element.39), channel_id=1, source_target_pairs={{0,1},{1,0},{2,3},{3,2},{4,5},{5,4},{6,7},{7,6},{8,9},{9,8},{10,11... | collective-permute-start | bytes 2359304 | tf_op jit(solution)/shard_map/ppermute | solution.py:658
  66.5 1.6 %collective-permute-start.1 = (bf16[512,256]{1,0:T(8,128)(2,1)S(1)}, bf16[512,256]{1,0:T(8,128)(2,1)S(1)}, u32[]{:S(2)}, u32[]{:S(2)}) collective-permute-start(bf16[512,256]{1,0:T(8,128)(2,1)S(1)} %get-tuple-element.50), channel_id=1, source_target_pairs={{0,1},{1,0},{2,3},{3,2},{4,5},{5,4},{6,7},{7,6},{8,9},{9,8},{10,11... | collective-permute-start | bytes 786440 | tf_op jit(solution)/shard_map/ppermute | solution.py:660
  90.3 24.8 %copy-start = (bf16[256,1024]{1,0:T(8,128)(2,1)S(1)}, bf16[256,1024]{1,0:T(8,128)(2,1)}, u32[]{:S(2)}) copy-start(bf16[256,1024]{1,0:T(8,128)(2,1)} %get-tuple-element.54.refs_4_) | copy-start | bytes 1572868
  90.3 24.8 %copy-start.1 = (bf16[1024,256]{1,0:T(8,128)(2,1)S(1)}, bf16[1024,256]{1,0:T(8,128)(2,1)}, u32[]{:S(2)}) copy-start(bf16[1024,256]{1,0:T(8,128)(2,1)} %get-tuple-element.55.refs_5_) | copy-start | bytes 1572868
  90.4 24.8 %copy-start.2 = (bf16[256,768]{1,0:T(8,128)(2,1)S(1)}, bf16[256,768]{1,0:T(8,128)(2,1)}, u32[]{:S(2)}) copy-start(bf16[256,768]{1,0:T(8,128)(2,1)} %get-tuple-element.51.refs_0_) | copy-start | bytes 1179652
  90.4 24.8 %copy-start.3 = (bf16[256,768]{1,0:T(8,128)(2,1)S(1)}, bf16[256,768]{1,0:T(8,128)(2,1)}, u32[]{:S(2)}) copy-start(bf16[256,768]{1,0:T(8,128)(2,1)} %get-tuple-element.52.refs_2_) | copy-start | bytes 1179652
  90.4 24.8 %copy-start.5 = (bf16[256,256]{1,0:T(8,128)(2,1)S(1)}, bf16[256,256]{1,0:T(8,128)(2,1)}, u32[]{:S(2)}) copy-start(bf16[256,256]{1,0:T(8,128)(2,1)} %get-tuple-element.53.refs_3_) | copy-start | bytes 393220
  111.6 5.8 %collective-permute-start.2 = (bf16[1024,512]{1,0:T(8,128)(2,1)S(1)}, bf16[1024,512]{1,0:T(8,128)(2,1)S(1)}, u32[]{:S(2)}, u32[]{:S(2)}) collective-permute-start(bf16[1024,512]{1,0:T(8,128)(2,1)S(1)} %bitcast.2), channel_id=1, source_target_pairs={{0,1},{1,0},{2,3},{3,2},{4,5},{5,4},{6,7},{7,6},{8,9},{9,8},{10,11... | collective-permute-start | bytes 3145736 | tf_op jit(solution)/shard_map/ppermute | solution.py:683
